TPU v7x, 256 devices: a whole 4x4x8 slice. The times are simulated.
256 devices in a mesh: dp: 16 (over x, y_lo, core), pipe: 2 (over y_hi), tensor: 8 (over z).
Axes of the slice: x: 4, y: 4 (y_hi: 2, y_lo: 2; y = y_hi * 2 + y_lo), z: 8, core: 2. Of those that a mesh axis runs over, the one named last changes fastest.
Arguments:
- acts: bfloat16 [2, 2, 128, 8192], P('pipe', None, 'dp', 'tensor'), may hold values from -6 to 6
- output_gradient: bfloat16 [2, 128, 8192], P(None, 'dp', 'tensor'), may hold values from -6 to 6
- gate_up_weight: bfloat16 [2, 8192, 2, 14336], P('pipe', 'tensor', None, 'dp'), may hold values from -0.0625 to 0.0625
- down: bfloat16 [2, 14336, 8192], P('pipe', 'dp', 'tensor'), may hold values from -0.046875 to 0.046875
- adapter_first_weight: bfloat16 [2, 8192, 128], P('pipe', 'tensor'), may hold values from -0.0625 to 0.0625
- adapter_second_weight: bfloat16 [2, 2, 64, 14336], P('pipe', None, None, 'dp'), may hold values from -0.29882812 to 0.29882812
Outputs:
- grad_inputs: bfloat16 [2, 2, 128, 8192], P('pipe', None, 'dp', 'tensor')
- grad_lora_down: float32 [2, 8192, 128], P('pipe', 'tensor')
- grad_lora_up: float32 [2, 2, 64, 14336], P('pipe', None, None, 'dp')
All inputs are finite; a program needn't handle non-finite values.
Results may differ from a plain program's by a relative error of at most 0.014.
Values may be sent and summed in bfloat16 or wider, within the bound.
No kernel may reach another device: no remote copies, remote signals or barrier semaphores. Data moves between devices by JAX's collectives and lax.ppermute only.
A program may use at most 64 MiB of HBM per device.

v0:
```python
import math

import jax
import jax.numpy as jnp
from jax import lax
from jax.sharding import PartitionSpec as P

adapter_scale = 2.0


def passed_along(block, axis, distance):
    devices = range(lax.axis_size(axis))
    route = [(i - distance, i) for i in devices if i - distance in devices]
    return lax.ppermute(block, axis, route)


def swiglu_back(summed_joined, hidden_grad, low_sum, adapter_second):
    count_of_rows = summed_joined.shape[0]
    hidden_size_value = hidden_grad.shape[1]
    rank_count = adapter_second.shape[1]
    low_bf = low_sum.astype(jnp.bfloat16)
    reduced_triple = low_bf.reshape(count_of_rows, 2, rank_count)
    reduced_rank = jnp.einsum(
        "bnd,ndc->bnc", reduced_triple, adapter_second, preferred_element_type=jnp.float32
    )
    preactivation = (
        summed_joined.reshape(count_of_rows, 2, hidden_size_value) + adapter_scale * reduced_rank
    )
    gate_pre = preactivation[:, 0]
    up_pre = preactivation[:, 1]
    gate_sig = jax.nn.sigmoid(gate_pre)
    gate_grad = hidden_grad * up_pre * gate_sig * (1.0 + gate_pre * (1.0 - gate_sig))
    up_grad = hidden_grad * gate_pre * gate_sig
    grad_rows = jnp.stack((gate_grad, up_grad), axis=1).astype(jnp.bfloat16)
    return (grad_rows.reshape(count_of_rows, 2 * hidden_size_value), low_bf)


def local(acts, output_gradient, gate_up_weight, down, adapter_first_weight, adapter_second_weight):
    section_index = lax.axis_index("pipe")
    section_count = lax.axis_size("pipe")
    replica_copies = lax.axis_size("dp")
    last_section = section_count - 1
    microbatch_count = acts.shape[1]
    token_row_block = acts.shape[2]
    feat_dim = acts.shape[3]
    hidden_size_value = down.shape[1]
    joined_weight = gate_up_weight[0].reshape(feat_dim, 2 * hidden_size_value)
    down_weight = down[0]
    adapter_first = adapter_first_weight[0]
    adapter_second = adapter_second_weight[0]
    factor_value = adapter_scale / math.sqrt(microbatch_count * token_row_block * replica_copies)
    received = jnp.zeros((token_row_block, feat_dim), jnp.bfloat16)
    results = jnp.zeros((microbatch_count, token_row_block, feat_dim), jnp.bfloat16)
    grad_down = jnp.zeros(adapter_first.shape, jnp.float32)
    grad_up = jnp.zeros(adapter_second.shape, jnp.float32)
    tick_count = microbatch_count + section_count - 1
    for tick_num in range(tick_count):
        batch_idx = tick_num - last_section + section_index
        batch_clip = jnp.clip(batch_idx, 0, microbatch_count - 1)
        inputs = lax.dynamic_index_in_dim(acts[0], batch_clip, 0, keepdims=False)
        if tick_num < microbatch_count:
            arriving = output_gradient[tick_num]
        else:
            arriving = jnp.zeros_like(received)
        upstream = jnp.where(section_index == last_section, arriving, received)
        all_inputs, all_upstream = (
            lax.all_gather(inputs, "dp", axis=0, tiled=True),
            lax.all_gather(upstream, "dp", axis=0, tiled=True),
        )
        part_joined = jnp.dot(all_inputs, joined_weight, preferred_element_type=jnp.float32)
        part_hidden = lax.dot_general(
            all_upstream, down_weight, (((1,), (1,)), ((), ())), preferred_element_type=jnp.float32
        )
        part_low = jnp.dot(all_inputs, adapter_first, preferred_element_type=jnp.float32)
        summed_joined, hidden_grad, low_sum = (
            lax.psum_scatter(part_joined, "tensor", scatter_dimension=0, tiled=True),
            lax.psum_scatter(part_hidden, "tensor", scatter_dimension=0, tiled=True),
            lax.psum_scatter(part_low, "tensor", scatter_dimension=0, tiled=True),
        )
        grad_rows, low_bf = swiglu_back(summed_joined, hidden_grad, low_sum, adapter_second)
        all_grads, all_low = (
            lax.all_gather(grad_rows, "tensor", axis=0, tiled=True),
            lax.all_gather(low_bf, "tensor", axis=0, tiled=True),
        )
        all_count = all_grads.shape[0]
        grads_three = all_grads.reshape(all_count, 2, hidden_size_value)
        reduced_triple = all_low.reshape(all_count, 2, -1)
        grad_up = grad_up + jnp.einsum(
            "tkr,tkf->krf", reduced_triple, grads_three, preferred_element_type=jnp.float32
        )
        part_input = lax.dot_general(
            all_grads, joined_weight, (((1,), (1,)), ((), ())), preferred_element_type=jnp.float32
        )
        part_back = jnp.einsum(
            "tkf,krf->tkr", grads_three, adapter_second, preferred_element_type=jnp.float32
        ).reshape(all_count, -1)
        summed_input, back_sum = (
            lax.psum_scatter(part_input, "dp", scatter_dimension=0, tiled=True),
            lax.psum_scatter(part_back, "dp", scatter_dimension=0, tiled=True),
        )
        backward_brain = back_sum.astype(jnp.bfloat16)
        reduced_input = lax.dot_general(
            backward_brain,
            adapter_first,
            (((1,), (1,)), ((), ())),
            preferred_element_type=jnp.float32,
        )
        gradient_input = (summed_input + adapter_scale * reduced_input).astype(jnp.bfloat16)
        first_factor_term = lax.dot_general(
            inputs, backward_brain, (((0,), (0,)), ((), ())), preferred_element_type=jnp.float32
        )
        grad_down = grad_down + lax.psum(first_factor_term, "dp")
        chosen = (jnp.arange(microbatch_count) == batch_idx)[:, None, None]
        results = jnp.where(chosen, gradient_input[None], results)
        if tick_num + 1 < tick_count:
            received = passed_along(gradient_input, "pipe", -1)
    grad_down = grad_down + 0.0
    return (results[None], (grad_down * factor_value)[None], (grad_up * factor_value)[None])


def solution(mesh):
    in_specs = (
        P("pipe", None, "dp", "tensor"),
        P(None, "dp", "tensor"),
        P("pipe", "tensor", None, "dp"),
        P("pipe", "dp", "tensor"),
        P("pipe", "tensor", None),
        P("pipe", None, None, "dp"),
    )
    out_specs = (
        P("pipe", None, "dp", "tensor"),
        P("pipe", "tensor", None),
        P("pipe", None, None, "dp"),
    )
    return jax.shard_map(local, mesh=mesh, in_specs=in_specs, out_specs=out_specs, check_vma=False)
```

profile of v0, /device:TPU:1, one launch (start us, length us, event | category | flops | bytes accessed | tf_op | source)
XLA Modules:
  0.0 835.8 jit_solution(834103591331224233)
XLA Ops:
  7.2 0.9 constant_dynamic-slice_fusion
  8.1 21.7 %all-gather.1 = bf16[1,1,128,1024]{3,2,1,0:T(8,128)(2,1)S(1)} all-gather(bf16[1,1,8,1024]{3,2,1,0:T(8,128)(2,1)S(1)} %get-tuple-element.10), channel_id=3, replica_groups=mesh['dp'=16,'pipe'=2,'tensor'=8] {'dp'}, dimensions={2}, use_global_device_ids=true | all-gather | bytes 278528 | tf_op jit(solution)/shard_map/all_gather | solution.py:67
  29.9 1.8 fusion.33
  31.7 2.7 copy.75
  34.5 1.8 copy-done.1
  36.2 1.6 fusion.36
  37.9 17.0 %all-gather = bf16[1,128,1024]{2,1,0:T(8,128)(2,1)S(1)} all-gather(bf16[1,8,1024]{2,1,0:T(8,128)(2,1)S(1)} %slice_select_fusion), channel_id=2, replica_groups=mesh['dp'=16,'pipe'=2,'tensor'=8] {'dp'}, dimensions={1}, use_global_device_ids=true | all-gather | bytes 278528 | tf_op jit(solution)/shard_map/all_gather | solution.py:68
  54.9 1.5 fusion.4
  56.5 6.3 reduce-scatter.20.cloned.1.call-done
  63.5 39.7 %reduce-scatter.18.cloned.1.call-done = f32[16,1792]{1,0:T(8,128)} async-done(((f32[128,1792]{1,0:T(8,128)}), f32[16,1792]{1,0:T(8,128)}) %reduce-scatter.18.cloned.1.call-update) | async-done | bytes 114704 | tf_op jit(solution)/shard_map/reduce_scatter | solution.py:76
  103.3 1.0 fusion.11
  104.3 37.5 %reduce-scatter.16.cloned.1.call-done = f32[16,896]{1,0:T(8,128)} async-done(((f32[128,896]{1,0:T(8,128)}), f32[16,896]{1,0:T(8,128)}) %reduce-scatter.16.cloned.1.call-update) | async-done | bytes 57360 | tf_op jit(solution)/shard_map/reduce_scatter | solution.py:77
  141.8 0.9 fusion.63
  142.7 19.1 %all_gather.38 = bf16[128,1792]{1,0:T(8,128)(2,1)S(1)} all-gather(bf16[16,1792]{1,0:T(8,128)(2,1)S(1)} %bitcast.235), channel_id=1, replica_groups=mesh['dp'=16,'pipe'=2,'tensor'=8] {'tensor'}, dimensions={0}, use_global_device_ids=true | all-gather | bytes 516096 | tf_op jit(solution)/shard_map/all_gather | solution.py:82
  161.8 4.1 fusion.79
  166.0 31.5 %all-gather.2 = bf16[1,1,128,1024]{3,2,1,0:T(8,128)(2,1)S(1)} all-gather(bf16[1,1,8,1024]{3,2,1,0:T(8,128)(2,1)S(1)} %get-tuple-element.11), channel_id=4, replica_groups=mesh['dp'=16,'pipe'=2,'tensor'=8] {'dp'}, dimensions={2}, use_global_device_ids=true | all-gather | bytes 278528 | tf_op jit(solution)/shard_map/all_gather | solution.py:67
  197.5 0.8 fusion.24
  198.4 3.6 fusion.26
  203.9 49.0 %all-reduce = bf16[128,128]{0,1:T(8,128)(2,1)S(1)} all-reduce(f32[128,128]{0,1:T(8,128)S(1)} %bitcast.232), channel_id=10, replica_groups=mesh['dp'=16,'pipe'=2,'tensor'=8] {'dp'}, use_global_device_ids=true, to_apply=%region_4.5.clone | all-reduce | flops 16384 | bytes 98304
  252.8 1.0 fusion.17
  253.8 1.3 collective-permute-start
  255.2 4.7 collective-permute-done
  259.9 22.1 %all_gather.39 = bf16[128,1024]{1,0:T(8,128)(2,1)S(1)} all-gather(bf16[8,1024]{1,0:T(8,128)(2,1)S(1)} %bitcast_select_fusion), channel_id=1, replica_groups=mesh['dp'=16,'pipe'=2,'tensor'=8] {'dp'}, dimensions={0}, use_global_device_ids=true | all-gather | bytes 278528 | tf_op jit(solution)/shard_map/all_gather | solution.py:68
  281.9 1.5 fusion.2
  283.5 0.7 convert_element_type.46
  284.3 26.7 %reduce-scatter.26.cloned.1.call-done = f32[16,1792]{1,0:T(8,128)} async-done(((f32[128,1792]{1,0:T(8,128)}), f32[16,1792]{1,0:T(8,128)}) %reduce-scatter.26.cloned.1.call-update) | async-done | bytes 114704 | tf_op jit(solution)/shard_map/reduce_scatter | solution.py:76
  311.0 1.0 fusion.12
  312.0 37.6 %reduce-scatter.24.cloned.1.call-done = f32[16,896]{1,0:T(8,128)} async-done(((f32[128,896]{1,0:T(8,128)}), f32[16,896]{1,0:T(8,128)}) %reduce-scatter.24.cloned.1.call-update) | async-done | bytes 57360 | tf_op jit(solution)/shard_map/reduce_scatter | solution.py:77
  349.6 0.9 fusion.64
  350.5 19.1 %all_gather.41 = bf16[128,1792]{1,0:T(8,128)(2,1)S(1)} all-gather(bf16[16,1792]{1,0:T(8,128)(2,1)S(1)} %bitcast.236), channel_id=1, replica_groups=mesh['dp'=16,'pipe'=2,'tensor'=8] {'tensor'}, dimensions={0}, use_global_device_ids=true | all-gather | bytes 516096 | tf_op jit(solution)/shard_map/all_gather | solution.py:82
  369.6 4.1 fusion.80
  373.8 31.5 %all-gather.3 = bf16[1,1,128,1024]{3,2,1,0:T(8,128)(2,1)S(1)} all-gather(bf16[1,1,8,1024]{3,2,1,0:T(8,128)(2,1)S(1)} %get-tuple-element.9), channel_id=5, replica_groups=mesh['dp'=16,'pipe'=2,'tensor'=8] {'dp'}, dimensions={2}, use_global_device_ids=true | all-gather | bytes 278528 | tf_op jit(solution)/shard_map/all_gather | solution.py:67
  405.3 0.8 fusion.20
  406.2 3.6 fusion.22
  409.9 1.0 copy.44
  410.9 1.2 fusion.42
  412.1 48.9 %all-reduce.1 = bf16[128,128]{0,1:T(8,128)(2,1)S(1)} all-reduce(f32[128,128]{0,1:T(8,128)S(1)} %bitcast.233), channel_id=15, replica_groups=mesh['dp'=16,'pipe'=2,'tensor'=8] {'dp'}, use_global_device_ids=true, to_apply=%region_9.10.clone | all-reduce | flops 16384 | bytes 98304
  461.1 1.0 fusion.18
  462.1 1.3 collective-permute-start.1
  463.4 4.7 collective-permute-done.1
  468.1 22.1 %all_gather.42 = bf16[128,1024]{1,0:T(8,128)(2,1)S(1)} all-gather(bf16[8,1024]{1,0:T(8,128)(2,1)S(1)} %broadcast_select_fusion), channel_id=1, replica_groups=mesh['dp'=16,'pipe'=2,'tensor'=8] {'dp'}, dimensions={0}, use_global_device_ids=true | all-gather | bytes 278528 | tf_op jit(solution)/shard_map/all_gather | solution.py:68
  490.2 1.5 fusion
  491.8 0.7 convert_element_type.50
  492.6 26.4 %reduce-scatter.34.cloned.1.call-done = f32[16,1792]{1,0:T(8,128)} async-done(((f32[128,1792]{1,0:T(8,128)}), f32[16,1792]{1,0:T(8,128)}) %reduce-scatter.34.cloned.1.call-update) | async-done | bytes 114704 | tf_op jit(solution)/shard_map/reduce_scatter | solution.py:76
  518.9 1.0 fusion.13
  520.3 1.1 convolution_add_fusion.1
  521.4 35.5 %reduce-scatter.32.cloned.1.call-done = f32[16,896]{1,0:T(8,128)} async-done(((f32[128,896]{1,0:T(8,128)}), f32[16,896]{1,0:T(8,128)}) %reduce-scatter.32.cloned.1.call-update) | async-done | bytes 57360 | tf_op jit(solution)/shard_map/reduce_scatter | solution.py:77
  557.0 0.9 fusion.65
  557.9 19.1 %all_gather.44 = bf16[128,1792]{1,0:T(8,128)(2,1)S(1)} all-gather(bf16[16,1792]{1,0:T(8,128)(2,1)S(1)} %bitcast.237), channel_id=1, replica_groups=mesh['dp'=16,'pipe'=2,'tensor'=8] {'tensor'}, dimensions={0}, use_global_device_ids=true | all-gather | bytes 516096 | tf_op jit(solution)/shard_map/all_gather | solution.py:82
  577.0 1.0 copy.49
  577.9 1.2 fusion.45
  579.2 59.9 %all-reduce.2 = bf16[128,128]{0,1:T(8,128)(2,1)S(1)} all-reduce(f32[128,128]{0,1:T(8,128)S(1)} %bitcast.234), channel_id=20, replica_groups=mesh['dp'=16,'pipe'=2,'tensor'=8] {'dp'}, use_global_device_ids=true, to_apply=%region_14.15.clone | all-reduce | flops 16384 | bytes 98304
  639.1 2.2 convolution_add_fusion
  641.3 4.1 fusion.81
  645.5 18.8 %all_gather.47 = bf16[128,128]{1,0:T(8,128)(2,1)S(1)} all-gather(bf16[16,128]{1,0:T(8,128)(2,1)S(1)} %convert_element_type.50), channel_id=1, replica_groups=mesh['dp'=16,'pipe'=2,'tensor'=8] {'tensor'}, dimensions={0}, use_global_device_ids=true | all-gather | bytes 36864 | tf_op jit(solution)/shard_map/all_gather | solution.py:83
  664.4 18.9 %all_gather.45 = bf16[128,128]{1,0:T(8,128)(2,1)S(1)} all-gather(bf16[16,128]{1,0:T(8,128)(2,1)S(1)} %copy-done.11), channel_id=1, replica_groups=mesh['dp'=16,'pipe'=2,'tensor'=8] {'tensor'}, dimensions={0}, use_global_device_ids=true | all-gather | bytes 36864 | tf_op jit(solution)/shard_map/all_gather | solution.py:83
  683.5 19.1 %all_gather.46 = bf16[128,128]{1,0:T(8,128)(2,1)S(1)} all-gather(bf16[16,128]{1,0:T(8,128)(2,1)S(1)} %copy-done.13), channel_id=1, replica_groups=mesh['dp'=16,'pipe'=2,'tensor'=8] {'tensor'}, dimensions={0}, use_global_device_ids=true | all-gather | bytes 36864 | tf_op jit(solution)/shard_map/all_gather | solution.py:83
  703.0 1.3 convolution_add_fusion.3
  704.3 2.1 fusion.7
  706.4 57.8 %all-reduce.5.cloned.1.call-done = f32[1024,128]{1,0:T(8,128)} async-done(((f32[1024,128]{1,0:T(8,128)}), f32[1024,128]{1,0:T(8,128)}) %all-reduce.5.cloned.1.call-update) | async-done | bytes 524304 | tf_op jit(solution)/shard_map/psum | solution.py:112
  764.2 1.9 multiply_bitcast_fusion
  766.1 61.5 %reduce-scatter.38.cloned.1.call-done = f32[8,1024]{1,0:T(8,128)} async-done(((f32[128,1024]{1,0:T(8,128)}), f32[8,1024]{1,0:T(8,128)}) %reduce-scatter.38.cloned.1.call-update) | async-done | bytes 32784 | tf_op jit(solution)/shard_map/reduce_scatter | solution.py:98
  827.5 1.0 fusion.19
  828.6 0.7 select_select_fusion
  (84 shorter events, 3.9 us)
Async XLA Ops:
  7.2 47.7 %copy-start = (bf16[1,896,1024]{2,1,0:T(8,128)(2,1)S(1)}, bf16[1,896,1024]{2,1,0:T(8,128)(2,1)}, u32[]{:S(2)}) copy-start(bf16[1,896,1024]{2,1,0:T(8,128)(2,1)} %param.9) | copy-start | bytes 5505028
  7.2 55.6 %reduce-scatter.20.cloned.1.call-start = ((), (), s32[]{:S(2)}) async-start(), calls=%async_computation.14 | async-start | bytes 73728 | tf_op jit(solution)/shard_map/reduce_scatter | solution.py:78
  8.1 26.3 %copy-start.6 = (bf16[1,1,8,1024]{3,2,1,0:T(8,128)(2,1)}, bf16[1,1,8,1024]{3,2,1,0:T(8,128)(2,1)S(1)}, u32[]{:S(2)}) copy-start(bf16[1,1,8,1024]{3,2,1,0:T(8,128)(2,1)S(1)} %get-tuple-element.10) | copy-start | bytes 49156
  8.1 157.9 %copy-start.4 = (bf16[1,1,8,1024]{3,2,1,0:T(8,128)(2,1)}, bf16[1,1,8,1024]{3,2,1,0:T(8,128)(2,1)S(1)}, u32[]{:S(2)}) copy-start(bf16[1,1,8,1024]{3,2,1,0:T(8,128)(2,1)S(1)} %get-tuple-element.11) | copy-start | bytes 49156
  31.7 71.6 %reduce-scatter.18.cloned.1.call-start = ((), (), s32[]{:S(2)}) async-start(), calls=%async_computation.13 | async-start | bytes 1032192 | tf_op jit(solution)/shard_map/reduce_scatter | solution.py:76
  34.4 1.8 copy-start.1
  34.5 3.5 copy-start.14
  36.2 67.0 %copy-start.3 = (bf16[1,2,64,896]{3,2,1,0:T(8,128)(2,1)S(1)}, bf16[1,2,64,896]{3,2,1,0:T(8,128)(2,1)}, u32[]{:S(2)}) copy-start(bf16[1,2,64,896]{3,2,1,0:T(8,128)(2,1)} %param.11) | copy-start | bytes 688132
  37.9 104.0 %reduce-scatter.16.cloned.1.call-start = ((), (), s32[]{:S(2)}) async-start(), calls=%async_computation.12 | async-start | bytes 516096 | tf_op jit(solution)/shard_map/reduce_scatter | solution.py:77
  56.4 141.1 %copy-start.2 = (bf16[1,1024,128]{2,1,0:T(8,128)(2,1)S(1)}, bf16[1,1024,128]{2,1,0:T(8,128)(2,1)}, u32[]{:S(2)}) copy-start(bf16[1,1024,128]{2,1,0:T(8,128)(2,1)} %param.10) | copy-start | bytes 786436
  56.4 196.4 %reduce-scatter.22.cloned.1.call-start = ((), (), s32[]{:S(2)}) async-start(), calls=%async_computation.15 | async-start | bytes 557056 | tf_op jit(solution)/shard_map/reduce_scatter | solution.py:98
  63.4 134.9 %copy-start.10 = (bf16[16,128]{1,0:T(8,128)(2,1)}, bf16[16,128]{1,0:T(8,128)(2,1)S(1)}, u32[]{:S(2)}) copy-start(bf16[16,128]{1,0:T(8,128)(2,1)S(1)} %convert_element_type.42) | copy-start | bytes 12292
  166.0 36.2 %copy-start.15 = (u32[256]{0:T(256)S(1)}, u32[256]{0:T(256)}, u32[]{:S(2)}) copy-start(u32[256]{0:T(256)} %constant.45) | copy-start | bytes 3076
  166.0 117.5 %reduce-scatter.28.cloned.1.call-start = ((), (), s32[]{:S(2)}) async-start(), calls=%async_computation.18 | async-start | bytes 73728 | tf_op jit(solution)/shard_map/reduce_scatter | solution.py:78
  198.4 112.6 %reduce-scatter.26.cloned.1.call-start = ((), (), s32[]{:S(2)}) async-start(), calls=%async_computation.17 | async-start | bytes 1032192 | tf_op jit(solution)/shard_map/reduce_scatter | solution.py:76
  202.1 147.6 %reduce-scatter.24.cloned.1.call-start = ((), (), s32[]{:S(2)}) async-start(), calls=%async_computation.16 | async-start | bytes 516096 | tf_op jit(solution)/shard_map/reduce_scatter | solution.py:77
  253.8 1.3 copy-start.8
  253.8 6.0 collective-permute-start
  283.4 177.6 %reduce-scatter.30.cloned.1.call-start = ((), (), s32[]{:S(2)}) async-start(), calls=%async_computation.19 | async-start | bytes 557056 | tf_op jit(solution)/shard_map/reduce_scatter | solution.py:98
  284.2 26.8 %copy-start.12 = (bf16[16,128]{1,0:T(8,128)(2,1)}, bf16[16,128]{1,0:T(8,128)(2,1)S(1)}, u32[]{:S(2)}) copy-start(bf16[16,128]{1,0:T(8,128)(2,1)S(1)} %convert_element_type.46) | copy-start | bytes 12292
  373.8 118.0 %reduce-scatter.36.cloned.1.call-start = ((), (), s32[]{:S(2)}) async-start(), calls=%async_computation.22 | async-start | bytes 73728 | tf_op jit(solution)/shard_map/reduce_scatter | solution.py:78
  406.1 112.8 %reduce-scatter.34.cloned.1.call-start = ((), (), s32[]{:S(2)}) async-start(), calls=%async_computation.21 | async-start | bytes 1032192 | tf_op jit(solution)/shard_map/reduce_scatter | solution.py:76
  409.8 110.2 %copy-start.7 = (bf16[1,1,8,1024]{3,2,1,0:T(8,128)(2,1)S(1)}, bf16[1,1,8,1024]{3,2,1,0:T(8,128)(2,1)}, u32[]{:S(2)}) copy-start(bf16[1,1,8,1024]{3,2,1,0:T(8,128)(2,1)} %copy-done.6) | copy-start | bytes 49156
  409.8 110.5 %copy-start.5 = (bf16[1,1,8,1024]{3,2,1,0:T(8,128)(2,1)S(1)}, bf16[1,1,8,1024]{3,2,1,0:T(8,128)(2,1)}, u32[]{:S(2)}) copy-start(bf16[1,1,8,1024]{3,2,1,0:T(8,128)(2,1)} %copy-done.4) | copy-start | bytes 49156
  409.8 147.1 %reduce-scatter.32.cloned.1.call-start = ((), (), s32[]{:S(2)}) async-start(), calls=%async_computation.20 | async-start | bytes 516096 | tf_op jit(solution)/shard_map/reduce_scatter | solution.py:77
  462.1 6.0 collective-permute-start.1
  491.7 272.5 %all-reduce.5.cloned.1.call-start = ((), (), s32[]{:S(2)}) async-start(), calls=%async_computation.24 | async-start | bytes 1048576 | tf_op jit(solution)/shard_map/psum | solution.py:112
  579.2 85.3 %copy-start.11 = (bf16[16,128]{1,0:T(8,128)(2,1)S(1)}, bf16[16,128]{1,0:T(8,128)(2,1)}, u32[]{:S(2)}) copy-start(bf16[16,128]{1,0:T(8,128)(2,1)} %copy-done.10) | copy-start | bytes 12292
  579.2 104.3 %copy-start.13 = (bf16[16,128]{1,0:T(8,128)(2,1)S(1)}, bf16[16,128]{1,0:T(8,128)(2,1)}, u32[]{:S(2)}) copy-start(bf16[16,128]{1,0:T(8,128)(2,1)} %copy-done.12) | copy-start | bytes 12292
  641.3 186.3 %reduce-scatter.38.cloned.1.call-start = ((), (), s32[]{:S(2)}) async-start(), calls=%async_computation.23 | async-start | bytes 557056 | tf_op jit(solution)/shard_map/reduce_scatter | solution.py:98
  645.5 183.1 %copy-start.9 = (bf16[8,1024]{1,0:T(8,128)(2,1)S(1)}, bf16[8,1024]{1,0:T(8,128)(2,1)}, u32[]{:S(2)}) copy-start(bf16[8,1024]{1,0:T(8,128)(2,1)} %copy-done.8) | copy-start | bytes 49156
Sparse Core Ops, SparseCore 0:
  31.8 30.9 reduce-scatter.19
  65.5 37.7 reduce-scatter.17
  106.3 35.4 reduce-scatter.15
  166.1 69.1 reduce-scatter.21
  237.7 32.8 reduce-scatter.27
  273.1 37.7 reduce-scatter.25
  314.0 35.5 reduce-scatter.23
  373.9 69.2 reduce-scatter.29
  445.7 32.8 reduce-scatter.35
  481.1 37.7 reduce-scatter.33
  521.5 35.4 reduce-scatter.31
  641.4 122.7 all-reduce.4
  766.7 60.7 reduce-scatter.37
where the time goes:
time: 839 us; the launch traced here: 836 us
  blocking collectives  418 us (50%)
  waiting for transfers between devices  339 us (40%)
  matrix products  45.3 us (5%)
  between operations  14.9 us (2%)
  local copies, waits for them, and re-layouts  8.82 us (1%)
    unnamed x3, blocking collectives  158 us
    reduce_scatter x3, waiting for transfers between devices, local(): lax.psum_scatter(part_hidden, 'tensor', scatter_dimension=0, tiled=True)  111 us
    reduce_scatter x3, waiting for transfers between devices, local(): lax.psum_scatter(part_joined, 'tensor', scatter_dimension=0, tiled=True)  92.8 us
    all_gather x3, blocking collectives, local(): lax.all_gather(inputs, 'dp', axis=0, tiled=True)  84.7 us
    reduce_scatter x3, waiting for transfers between devices, local(): lax.psum_scatter(part_input, 'dp', scatter_dimension=0, tiled=True)  61.5 us
    all_gather x3, blocking collectives, local(): lax.all_gather(upstream, 'dp', axis=0, tiled=True)  61.1 us
    psum x1, waiting for transfers between devices, local(): grad_down = grad_down + lax.psum(first_factor_term, 'dp')  57.8 us
    all_gather x3, blocking collectives, local(): lax.all_gather(grad_rows, 'tensor', axis=0, tiled=True)  57.3 us
  transfers between devices with their start and end apart: 15, of which 11 were waited for; matrix products, arithmetic and copies ran while one was open for 5% of the time, Pallas kernels for 0%

commit v1 on v0

v1 whole, which is shorter than its diff:
```python
import math

import jax
import jax.numpy as jnp
from jax import lax
from jax.sharding import Mesh, PartitionSpec as P

adapter_scale = 2.0
CHIPS = ("x", "yl")
F32 = jnp.float32
BF16 = jnp.bfloat16


def dot_nn(a, b):
    return jnp.dot(a, b, preferred_element_type=F32)


def dot_nt(a, b):
    return lax.dot_general(a, b, (((1,), (1,)), ((), ())), preferred_element_type=F32)


def dot_tn(a, b):
    return lax.dot_general(a, b, (((0,), (0,)), ((), ())), preferred_element_type=F32)


def core_swap(block):
    return lax.ppermute(block, "core", [(0, 1), (1, 0)])


def to_all_chips(block, axis):
    n = lax.axis_size(axis)
    return lax.all_to_all(jnp.broadcast_to(block[None], (n,) + block.shape), axis, 0, 0)


def gather_dp(block):
    mine = to_all_chips(block, CHIPS)
    mine = mine.reshape((-1,) + block.shape[1:])
    return jnp.concatenate([mine, core_swap(mine)], axis=0)


def scatter_z(partial):
    n = lax.axis_size("z")
    parts = partial.astype(BF16).reshape(n, -1, partial.shape[1])
    return jnp.sum(lax.all_to_all(parts, "z", 0, 0).astype(F32), axis=0)


def swiglu_back(pre, hidden):
    half = pre.shape[1] // 2
    gate, up = pre[:, :half].astype(F32), pre[:, half:].astype(F32)
    sig = 1.0 / (1.0 + jnp.exp(-gate))
    gate_grad = hidden * up * sig * (1.0 + gate * (1.0 - sig))
    up_grad = hidden * gate * sig
    return jnp.concatenate([gate_grad, up_grad], axis=1).astype(BF16)


def local(acts, output_gradient, gate_up_weight, down, adapter_first_weight, adapter_second_weight):
    upper = lax.axis_index("pipe") == 1
    micro, rows, feat = acts.shape[1:]
    hidden_units = down.shape[1]
    rank = adapter_second_weight.shape[2]
    own = micro * rows
    weight = gate_up_weight[0].reshape(feat, 2 * hidden_units)
    down_weight = down[0]
    first = adapter_first_weight[0]
    second = adapter_second_weight[0]
    tokens = own * lax.axis_size(("x", "yl", "core"))
    half = tokens // 2
    factor = adapter_scale / math.sqrt(tokens)

    def adapter_up(low):
        low = low.astype(BF16)
        return jnp.concatenate(
            [dot_nn(low[:, :rank], second[0]), dot_nn(low[:, rank:], second[1])], axis=1
        )

    def adapter_back(act):
        return jnp.concatenate(
            [dot_nt(act[:, :hidden_units], second[0]), dot_nt(act[:, hidden_units:], second[1])], axis=1
        )

    def input_partial(act):
        back = adapter_back(act)
        return dot_nt(act, weight) + adapter_scale * dot_nt(back.astype(BF16), first), back

    def core_sum(partial):
        partial = partial.astype(BF16)
        return partial[:half].astype(F32) + core_swap(partial[half:]).astype(F32)

    both = jnp.concatenate([acts[0].reshape(own, feat), output_gradient.reshape(own, feat)], axis=1)
    both = gather_dp(both)
    inputs, upstream = both[:, :feat], both[:, feat:]

    low_part = dot_nn(inputs, first)
    pre_part = dot_nn(inputs, weight) + adapter_scale * adapter_up(low_part)
    hidden_part = dot_nt(upstream, down_weight)
    summed = scatter_z(jnp.concatenate([pre_part, low_part, hidden_part], axis=1))
    width = 2 * hidden_units
    pre_own = summed[:, :width]
    act_own = swiglu_back(pre_own, summed[:, width + 2 * rank:])
    sent = jnp.concatenate(
        [jnp.where(upper, act_own, pre_own.astype(BF16)), summed[:, width:width + 2 * rank].astype(BF16)],
        axis=1,
    )
    held = lax.all_gather(sent, "z", axis=0, tiled=True)
    act_or_pre, low = held[:, :width], held[:, width:]
    part, back = input_partial(act_or_pre)
    mine = core_sum(jnp.concatenate([part, back], axis=1))
    mine = lax.all_to_all(mine.astype(BF16).reshape(-1, own, mine.shape[1]), CHIPS, 0, 0)
    mine = jnp.sum(mine.astype(F32), axis=0).astype(BF16)
    grad_one, back_one = mine[:, :feat], mine[:, feat:]

    handed = lax.ppermute(grad_one, "pipe", [(1, 0)])
    sent = jnp.where(upper, jnp.pad(back_one, ((0, 0), (0, feat - 2 * rank))), handed)
    upstream = gather_dp(sent)
    back_upper = upstream[:, :2 * rank]
    hidden_own = scatter_z(dot_nt(upstream, down_weight))
    hidden_all = to_all_chips(hidden_own.astype(BF16), "z").reshape(tokens, hidden_units)
    act_lower = swiglu_back(act_or_pre, hidden_all.astype(F32))
    part, back = input_partial(act_lower)
    mine = core_sum(part).astype(BF16).reshape(-1, own, feat)
    back = core_sum(back).astype(BF16)
    chips = mine.shape[0]
    back = jnp.broadcast_to(back.reshape(1, -1, feat), (chips, back.size // feat, feat))
    got = lax.all_to_all(jnp.concatenate([mine, back], axis=1), CHIPS, 0, 0)
    got = jnp.sum(got.astype(F32), axis=0).astype(BF16)
    grad_zero = got[:own]
    back_half = got[own:].reshape(half, 2 * rank)
    back_lower = jnp.concatenate([back_half, core_swap(back_half)], axis=0)

    act = jnp.where(upper, act_or_pre, act_lower)
    grad_up = jnp.stack(
        [
            dot_tn(low[:, :rank], act[:, :hidden_units]),
            dot_tn(low[:, rank:], act[:, hidden_units:]),
        ]
    )
    grad_down = dot_tn(inputs, jnp.where(upper, back_upper, back_lower))
    grad_inputs = jnp.where(upper, grad_one, grad_zero).reshape(1, micro, rows, feat)
    return grad_inputs, (grad_down * factor)[None], (grad_up * factor)[None]


def solution(mesh):
    sizes = dict(mesh.shape)
    fine = Mesh(
        mesh.devices.reshape(sizes["dp"] // 4, 2, 2, sizes["pipe"], sizes["tensor"]),
        ("x", "yl", "core", "pipe", "z"),
    )
    dp = ("x", "yl", "core")
    in_specs = (
        P("pipe", None, dp, "z"),
        P(None, dp, "z"),
        P("pipe", "z", None, dp),
        P("pipe", dp, "z"),
        P("pipe", "z", None),
        P("pipe", None, None, dp),
    )
    out_specs = (
        P("pipe", None, dp, "z"),
        P("pipe", "z", None),
        P("pipe", None, None, dp),
    )
    return jax.shard_map(local, mesh=fine, in_specs=in_specs, out_specs=out_specs, check_vma=False)
```

time: 839 us -> 205 us (0.24)
  blocking collectives: 418 us -> 87.6 us
  waiting for transfers between devices: 339 us -> 52.3 us
  matrix products: 45.3 us -> 13 us
  starting transfers between devices: 3.16 us -> 30.2 us
  between operations: 14.9 us -> 1.08 us
    reduce_scatter x12 -> x0, waiting for transfers between devices: 271 us -> none  [the longest x3 111 us: local(): lax.psum_scatter(part_hidden, 'tensor', scatter_dimension=0, tiled=True)]
    all_gather x12 -> x1, blocking collectives: 260 us -> 21.1 us  [local(): held = lax.all_gather(sent, 'z', axis=0, tiled=True)]
    unnamed x3 -> x0, blocking collectives: 158 us -> none
    all_to_all x0 -> x5, blocking collectives: none -> 66.5 us  [the longest x3 39.2 us: to_all_chips(): lax.all_to_all(jnp.broadcast_to(block[None], (n,) + block.shape), axis, 0...]
    psum x1 -> x0, waiting for transfers between devices: 57.8 us -> none  [local(): grad_down = grad_down + lax.psum(first_factor_term, 'dp')]
    all_to_all x0 -> x2, waiting for transfers between devices: none -> 43.7 us  [the longest x1 37.6 us: scatter_z(): return jnp.sum(lax.all_to_all(parts, 'z', 0, 0).astype(F32), axis=0)]
    dot_general x27 -> x17, matrix products: 45.3 us -> 13 us  [the longest x10 7.11 us: dot_nt(): lax.dot_general(a, b, (((1,), (1,)), ((), ())), preferred_element_type=F32)]
    ppermute x2 -> x7, starting transfers between devices: 2.62 us -> 17.8 us  [the longest x6 16.6 us: core_swap(): return lax.ppermute(block, 'core', [(0, 1), (1, 0)])]
  transfers between devices with their start and end apart: 15 -> 9, of which waited for: 11 -> 7; matrix products, arithmetic and copies ran while one was open for 5% -> 5% of each run, Pallas kernels for 0% -> 0%
where the time goes in v1:
time: 205 us
  blocking collectives  87.6 us (43%)
  waiting for transfers between devices  52.3 us (26%)
  starting transfers between devices  30.2 us (15%)
  matrix products  13 us (6%)
  other arithmetic  10.8 us (5%)
  local copies, waits for them, and re-layouts  9.5 us (5%)
    all_to_all x3, blocking collectives, to_all_chips(): lax.all_to_all(jnp.broadcast_to(block[None], (n,) + block.shape), axis, 0...  39.2 us
    all_to_all x1, waiting for transfers between devices, scatter_z(): return jnp.sum(lax.all_to_all(parts, 'z', 0, 0).astype(F32), axis=0)  37.6 us
    all_gather x1, blocking collectives, local(): held = lax.all_gather(sent, 'z', axis=0, tiled=True)  21.1 us
    all_to_all x1, blocking collectives, scatter_z(): return jnp.sum(lax.all_to_all(parts, 'z', 0, 0).astype(F32), axis=0)  17.7 us
    ppermute x6, starting transfers between devices, core_swap(): return lax.ppermute(block, 'core', [(0, 1), (1, 0)])  16.6 us
    all_to_all x1, blocking collectives, local(): lax.all_to_all(mine.astype(BF16).reshape(-1, own, mine.shape[1]), CHIPS,...  9.69 us
    all_to_all x1, starting transfers between devices, scatter_z(): return jnp.sum(lax.all_to_all(parts, 'z', 0, 0).astype(F32), axis=0)  8.19 us
    dot_general x10, matrix products, dot_nt(): lax.dot_general(a, b, (((1,), (1,)), ((), ())), preferred_element_type=F32)  7.11 us
  transfers between devices with their start and end apart: 9, of which 7 were waited for; matrix products, arithmetic and copies ran while one was open for 5% of the time, Pallas kernels for 0%

profile of v1, /device:TPU:1, one launch (start us, length us, event | category | flops | bytes accessed | tf_op | source)
XLA Modules:
  0.0 204.6 jit_solution(8438043491399437418)
XLA Ops:
  0.6 0.0 copy-start
  0.6 0.9 pad_maximum_fusion.8
  1.6 14.3 %all_to_all.35 = bf16[8,16,2048]{2,1,0:T(8,128)(2,1)S(1)} all-to-all(bf16[8,16,2048]{2,1,0:T(8,128)(2,1)S(1)} %broadcast_in_dim.12), channel_id=1, replica_groups=mesh['x'=4,'yl'=2,'core'=2,'pipe'=2,'z'=8] {'x','yl'}, dimensions={0} | all-to-all | bytes 1048576 | tf_op jit(solution)/shard_map/all_to_all | solution.py:32
  15.9 2.1 %collective-permute-start = (bf16[128,2048]{1,0:T(8,128)(2,1)S(1)}, bf16[128,2048]{1,0:T(8,128)(2,1)S(1)}, u32[]{:S(2)}, u32[]{:S(2)}) collective-permute-start(bf16[128,2048]{1,0:T(8,128)(2,1)S(1)} %bitcast.69), channel_id=1, source_target_pairs={{0,16},{16,0},{1,17},{17,1},{2,18},{18,2},{3,19},{19,3},{4,20},{20... | collective-permute-start | bytes 1572872 | tf_op jit(solution)/shard_map/ppermute | solution.py:27
  18.0 4.5 %copy.18 = bf16[128,8,2,896]{3,1,2,0:T(8,128)(2,1)} copy(bf16[128,8,2,896]{3,2,1,0:T(2,128)(2,1)} %bitcast.65) | data formatting | bytes 7340032
  22.4 0.9 fusion.28
  23.3 0.1 copy-done.7
  23.4 0.3 convolution_convert_fusion.2
  23.7 0.7 copy.12
  24.4 0.3 fusion.44
  24.8 0.3 fusion.48
  25.1 0.7 fusion.12
  25.8 0.9 copy-done.4
  26.8 1.2 fusion
  28.0 1.2 pad_maximum_fusion
  29.2 8.2 %all-to-all-start.1 = ((bf16[8,32,2816]{2,1,0:T(8,128)(2,1)}), bf16[8,32,2816]{2,1,0:T(8,128)(2,1)S(1)}, u32[]{:S(2)}, u32[]{:S(2)}) async-start(bf16[8,32,2816]{2,1,0:T(8,128)(2,1)} %pad_maximum_fusion), calls=%async_computation.1 | async-start | bytes 2883584 | tf_op jit(solution)/shard_map/all_to_all | solution.py:44
  37.4 37.6 %all-to-all-done.1 = bf16[8,32,2816]{2,1,0:T(8,128)(2,1)S(1)} async-done(((bf16[8,32,2816]{2,1,0:T(8,128)(2,1)}), bf16[8,32,2816]{2,1,0:T(8,128)(2,1)S(1)}, u32[]{:S(2)}, u32[]{:S(2)}) %all-to-all-start.1) | async-done | bytes 1441824 | tf_op jit(solution)/shard_map/all_to_all | solution.py:44
  75.0 0.2 convert_reduce_fusion
  75.2 0.1 fusion.41
  75.4 21.1 %all_gather.3 = bf16[256,1920]{1,0:T(8,128)(2,1)S(1)} all-gather(bf16[32,1920]{1,0:T(8,128)(2,1)S(1)} %pad_maximum_fusion.5), channel_id=1, replica_groups=mesh['x'=4,'yl'=2,'core'=2,'pipe'=2,'z'=8] {'z'}, dimensions={0}, use_global_device_ids=true | all-gather | bytes 1105920 | tf_op jit(solution)/shard_map/all_gather | solution.py:104
  96.5 0.3 convolution_convert_fusion
  96.8 0.3 convolution_convert_fusion.1
  97.1 0.0 copy-start.15
  97.1 1.1 fusion.25
  98.3 1.1 fusion.7
  99.4 1.2 concatenate.67
  100.7 6.2 %collective-permute-start.1 = (bf16[128,1152]{1,0:T(8,128)(2,1)S(1)}, bf16[128,1152]{1,0:T(8,128)(2,1)S(1)}, u32[]{:S(2)}, u32[]{:S(2)}) collective-permute-start(bf16[128,1152]{1,0:T(8,128)(2,1)S(1)} %slice.154), channel_id=1, source_target_pairs={{0,16},{16,0},{1,17},{17,1},{2,18},{18,2},{3,19},{19,3},{4,20},{20... | collective-permute-start | bytes 884744 | tf_op jit(solution)/shard_map/ppermute | solution.py:27
  106.9 1.2 collective-permute-done.1
  108.1 0.1 add_convert_fusion
  108.2 9.7 %all_to_all.36 = bf16[8,16,1152]{2,1,0:T(8,128)(2,1)S(1)} all-to-all(bf16[8,16,1152]{2,1,0:T(8,128)(2,1)S(1)} %bitcast.71), channel_id=1, replica_groups=mesh['x'=4,'yl'=2,'core'=2,'pipe'=2,'z'=8] {'x','yl'}, dimensions={0} | all-to-all | bytes 589824 | tf_op jit(solution)/shard_map/all_to_all | solution.py:108
  117.9 1.3 collective-permute-start.2
  119.2 4.9 %collective-permute-done.2 = bf16[16,1024]{1,0:T(8,128)(2,1)S(1)} collective-permute-done((bf16[16,1024]{1,0:T(8,128)(2,1)S(1)}, bf16[16,1024]{1,0:T(8,128)(2,1)S(1)}, u32[]{:S(2)}, u32[]{:S(2)}) %collective-permute-start.2) | collective-permute-done | bytes 32800 | tf_op jit(solution)/shard_map/ppermute | solution.py:112
  124.1 8.3 %all_to_all.37 = bf16[8,16,1024]{2,1,0:T(8,128)(2,1)S(1)} all-to-all(bf16[8,16,1024]{2,1,0:T(8,128)(2,1)S(1)} %broadcast_in_dim.13), channel_id=1, replica_groups=mesh['x'=4,'yl'=2,'core'=2,'pipe'=2,'z'=8] {'x','yl'}, dimensions={0} | all-to-all | bytes 524288 | tf_op jit(solution)/shard_map/all_to_all | solution.py:32
  132.4 3.9 %collective-permute-start.3 = (bf16[128,1024]{1,0:T(8,128)(2,1)S(1)}, bf16[128,1024]{1,0:T(8,128)(2,1)S(1)}, u32[]{:S(2)}, u32[]{:S(2)}) collective-permute-start(bf16[128,1024]{1,0:T(8,128)(2,1)S(1)} %bitcast.73), channel_id=1, source_target_pairs={{0,16},{16,0},{1,17},{17,1},{2,18},{18,2},{3,19},{19,3},{4,20},{20... | collective-permute-start | bytes 786440 | tf_op jit(solution)/shard_map/ppermute | solution.py:27
  136.3 1.2 collective-permute-done.3
  137.4 0.7 fusion.9
  138.2 17.7 %all_to_all.38 = bf16[8,32,896]{2,1,0:T(8,128)(2,1)S(1)} all-to-all(bf16[8,32,896]{2,1,0:T(8,128)(2,1)S(1)} %bitcast.78), channel_id=1, replica_groups=mesh['x'=4,'yl'=2,'core'=2,'pipe'=2,'z'=8] {'z'}, dimensions={0} | all-to-all | bytes 917504 | tf_op jit(solution)/shard_map/all_to_all | solution.py:44
  155.9 0.1 reduce_sum.47
  156.0 0.0 copy-start.12
  156.0 16.6 %all_to_all.39 = bf16[8,32,896]{2,1,0:T(8,128)(2,1)S(1)} all-to-all(bf16[8,32,896]{2,1,0:T(8,128)(2,1)S(1)} %broadcast_in_dim.14), channel_id=1, replica_groups=mesh['x'=4,'yl'=2,'core'=2,'pipe'=2,'z'=8] {'z'}, dimensions={0} | all-to-all | bytes 917504 | tf_op jit(solution)/shard_map/all_to_all | solution.py:32
  172.7 0.5 fusion.24
  173.2 0.0 copy-start.3
  173.2 0.3 convolution_convert_fusion.3
  173.5 0.0 copy-start.8
  173.5 1.1 fusion.27
  174.7 0.3 convolution_convert_fusion.4
  175.0 1.1 fusion.8
  176.1 1.7 slice.158
  177.8 3.1 %collective-permute-start.4 = (bf16[128,1024]{1,0:T(8,128)(2,1)}, bf16[128,1024]{1,0:T(8,128)(2,1)}, u32[]{:S(2)}, u32[]{:S(2)}) collective-permute-start(bf16[128,1024]{1,0:T(8,128)(2,1)} %slice.158), channel_id=1, source_target_pairs={{0,16},{16,0},{1,17},{17,1},{2,18},{18,2},{3,19},{19,3},{4,20},{20... | collective-permute-start | bytes 786440 | tf_op jit(solution)/shard_map/ppermute | solution.py:27
  180.9 1.2 collective-permute-done.5
  182.1 0.1 copy.15
  182.2 0.2 collective-permute-done.4
  182.4 1.1 add_convert_fusion.1
  183.5 0.8 pad_maximum_fusion.4
  184.3 4.1 %all-to-all-start.6 = ((bf16[8,32,1024]{2,1,0:T(8,128)(2,1)}), bf16[8,32,1024]{2,1,0:T(8,128)(2,1)}, u32[]{:S(2)}, u32[]{:S(2)}) async-start(bf16[8,32,1024]{2,1,0:T(8,128)(2,1)} %pad_maximum_fusion.4), calls=%async_computation.6 | async-start | bytes 1048576 | tf_op jit(solution)/shard_map/all_to_all | solution.py:124
  188.5 1.2 broadcast_select_fusion
  189.8 1.0 convolution_bitcast_fusion
  190.8 0.9 convolution_bitcast_fusion.1
  191.7 6.1 %all-to-all-done.6 = bf16[8,32,1024]{2,1,0:T(8,128)(2,1)} async-done(((bf16[8,32,1024]{2,1,0:T(8,128)(2,1)}), bf16[8,32,1024]{2,1,0:T(8,128)(2,1)}, u32[]{:S(2)}, u32[]{:S(2)}) %all-to-all-start.6) | async-done | bytes 524320 | tf_op jit(solution)/shard_map/all_to_all | solution.py:124
  197.7 1.1 reduce_sum.48
  198.9 0.6 fusion.77
  199.5 1.3 collective-permute-start.6
  200.8 1.8 maximum_multiply_fusion.1
  202.6 1.9 fusion.15
  (49 shorter events, 0.4 us)
Async XLA Ops:
  0.6 24.4 %copy-start = (bf16[1,896,1024]{2,1,0:T(8,128)(2,1)S(1)}, bf16[1,896,1024]{2,1,0:T(8,128)(2,1)}, u32[]{:S(2)}) copy-start(bf16[1,896,1024]{2,1,0:T(8,128)(2,1)} %param.9) | copy-start | bytes 5505028
  15.9 6.6 %collective-permute-start = (bf16[128,2048]{1,0:T(8,128)(2,1)S(1)}, bf16[128,2048]{1,0:T(8,128)(2,1)S(1)}, u32[]{:S(2)}, u32[]{:S(2)}) collective-permute-start(bf16[128,2048]{1,0:T(8,128)(2,1)S(1)} %bitcast.69), channel_id=1, source_target_pairs={{0,16},{16,0},{1,17},{17,1},{2,18},{18,2},{3,19},{19,3},{4,20},{20... | collective-permute-start | bytes 1572872 | tf_op jit(solution)/shard_map/ppermute | solution.py:27
  22.4 0.9 copy-start.7
  22.4 2.0 copy-start.10
  23.3 2.5 %copy-start.1 = (bf16[256,1024]{1,0:T(8,128)(2,1)}, bf16[256,1024]{1,0:T(8,128)(2,1)S(1)}, u32[]{:S(2)}) copy-start(bf16[256,1024]{1,0:T(8,128)(2,1)S(1)} %get-tuple-element.5) | copy-start | bytes 1572868
  23.3 1.8 copy-start.13
  24.7 2.0 copy-start.4
  26.8 1.2 copy-start.16
  29.2 45.8 %all-to-all-start.1 = ((bf16[8,32,2816]{2,1,0:T(8,128)(2,1)}), bf16[8,32,2816]{2,1,0:T(8,128)(2,1)S(1)}, u32[]{:S(2)}, u32[]{:S(2)}) async-start(bf16[8,32,2816]{2,1,0:T(8,128)(2,1)} %pad_maximum_fusion), calls=%async_computation.1 | async-start | bytes 2883584 | tf_op jit(solution)/shard_map/all_to_all | solution.py:44
  75.0 21.5 %copy-start.11 = (bf16[1,2,64,896]{3,2,1,0:T(8,128)(2,1)S(1)}, bf16[1,2,64,896]{3,2,1,0:T(8,128)(2,1)}, u32[]{:S(2)}) copy-start(bf16[1,2,64,896]{3,2,1,0:T(8,128)(2,1)} %param.11) | copy-start | bytes 688132
  75.3 21.8 %copy-start.5 = (bf16[128,8,2,896]{3,1,2,0:T(8,128)(2,1)S(1)}, bf16[128,8,2,896]{3,1,2,0:T(8,128)(2,1)}, u32[]{:S(2)}) copy-start(bf16[128,8,2,896]{3,1,2,0:T(8,128)(2,1)} %copy.18) | copy-start | bytes 11010052
  96.8 1.5 copy-start.14
  97.1 1.2 copy-start.15
  100.7 7.4 %collective-permute-start.1 = (bf16[128,1152]{1,0:T(8,128)(2,1)S(1)}, bf16[128,1152]{1,0:T(8,128)(2,1)S(1)}, u32[]{:S(2)}, u32[]{:S(2)}) collective-permute-start(bf16[128,1152]{1,0:T(8,128)(2,1)S(1)} %slice.154), channel_id=1, source_target_pairs={{0,16},{16,0},{1,17},{17,1},{2,18},{18,2},{3,19},{19,3},{4,20},{20... | collective-permute-start | bytes 884744 | tf_op jit(solution)/shard_map/ppermute | solution.py:27
  117.9 6.2 %collective-permute-start.2 = (bf16[16,1024]{1,0:T(8,128)(2,1)S(1)}, bf16[16,1024]{1,0:T(8,128)(2,1)S(1)}, u32[]{:S(2)}, u32[]{:S(2)}) collective-permute-start(bf16[16,1024]{1,0:T(8,128)(2,1)S(1)} %slice.155), channel_id=1, source_target_pairs={{8,0},{9,1},{10,2},{11,3},{12,4},{13,5},{14,6},{15,7},{24,16},{25,... | collective-permute-start | bytes 98312 | tf_op jit(solution)/shard_map/ppermute | solution.py:112
  132.4 5.8 %copy-start.9 = (bf16[8,16,1024]{2,1,0:T(8,128)(2,1)}, bf16[8,16,1024]{2,1,0:T(8,128)(2,1)S(1)}, u32[]{:S(2)}) copy-start(bf16[8,16,1024]{2,1,0:T(8,128)(2,1)S(1)} %all_to_all.37) | copy-start | bytes 786436
  132.4 5.1 %collective-permute-start.3 = (bf16[128,1024]{1,0:T(8,128)(2,1)S(1)}, bf16[128,1024]{1,0:T(8,128)(2,1)S(1)}, u32[]{:S(2)}, u32[]{:S(2)}) collective-permute-start(bf16[128,1024]{1,0:T(8,128)(2,1)S(1)} %bitcast.73), channel_id=1, source_target_pairs={{0,16},{16,0},{1,17},{17,1},{2,18},{18,2},{3,19},{19,3},{4,20},{20... | collective-permute-start | bytes 786440 | tf_op jit(solution)/shard_map/ppermute | solution.py:27
  137.4 0.8 copy-start.17
  156.0 17.2 %copy-start.12 = (bf16[1,2,64,896]{3,2,1,0:T(8,128)(2,1)S(1)}, bf16[1,2,64,896]{3,2,1,0:T(8,128)(2,1)}, u32[]{:S(2)}) copy-start(bf16[1,2,64,896]{3,2,1,0:T(8,128)(2,1)} %param.11) | copy-start | bytes 688132
  156.0 17.5 %copy-start.6 = (bf16[128,8,2,896]{3,1,2,0:T(8,128)(2,1)S(1)}, bf16[128,8,2,896]{3,1,2,0:T(8,128)(2,1)}, u32[]{:S(2)}) copy-start(bf16[128,8,2,896]{3,1,2,0:T(8,128)(2,1)} %copy.18) | copy-start | bytes 11010052
  173.2 1.5 copy-start.3
  173.5 1.5 copy-start.8
  177.8 4.6 %collective-permute-start.4 = (bf16[128,1024]{1,0:T(8,128)(2,1)}, bf16[128,1024]{1,0:T(8,128)(2,1)}, u32[]{:S(2)}, u32[]{:S(2)}) collective-permute-start(bf16[128,1024]{1,0:T(8,128)(2,1)} %slice.158), channel_id=1, source_target_pairs={{0,16},{16,0},{1,17},{17,1},{2,18},{18,2},{3,19},{19,3},{4,20},{20... | collective-permute-start | bytes 786440 | tf_op jit(solution)/shard_map/ppermute | solution.py:27
  180.8 1.2 collective-permute-start.5
  184.3 13.4 %all-to-all-start.6 = ((bf16[8,32,1024]{2,1,0:T(8,128)(2,1)}), bf16[8,32,1024]{2,1,0:T(8,128)(2,1)}, u32[]{:S(2)}, u32[]{:S(2)}) async-start(bf16[8,32,1024]{2,1,0:T(8,128)(2,1)} %pad_maximum_fusion.4), calls=%async_computation.6 | async-start | bytes 1048576 | tf_op jit(solution)/shard_map/all_to_all | solution.py:124
  189.7 12.9 %copy-start.2 = (bf16[256,1024]{1,0:T(8,128)(2,1)S(1)}, bf16[256,1024]{1,0:T(8,128)(2,1)}, u32[]{:S(2)}) copy-start(bf16[256,1024]{1,0:T(8,128)(2,1)} %copy-done.1) | copy-start | bytes 1572868
  199.5 3.1 %collective-permute-start.6 = (bf16[128,128]{1,0:T(8,128)(2,1)S(1)}, bf16[128,128]{1,0:T(8,128)(2,1)S(1)}, u32[]{:S(2)}, u32[]{:S(2)}) collective-permute-start(bf16[128,128]{1,0:T(8,128)(2,1)S(1)} %reshape.87), channel_id=1, source_target_pairs={{0,16},{16,0},{1,17},{17,1},{2,18},{18,2},{3,19},{19,3},{4,20},{20... | collective-permute-start | bytes 98312 | tf_op jit(solution)/shard_map/ppermute | solution.py:27

commit v2 on v1

--- a/solution.py
+++ b/solution.py
@@ -42,6 +42,55 @@
     n = lax.axis_size("z")
     parts = partial.astype(BF16).reshape(n, -1, partial.shape[1])
     return jnp.sum(lax.all_to_all(parts, "z", 0, 0).astype(F32), axis=0)
+
+
+def ring(step):
+    n = lax.axis_size("z")
+    return [(i, (i + step) % n) for i in range(n)]
+
+
+def ring_scatter_z(partial):
+    n = lax.axis_size("z")
+    me = lax.axis_index("z")
+    parts = partial.reshape(n, -1, partial.shape[1])
+
+    def part(step):
+        return lax.dynamic_index_in_dim(parts, lax.rem(me + step + n, n), 0, keepdims=False)
+
+    def plus(total, step):
+        return total.astype(F32) + part(step).astype(F32)
+
+    ahead, behind = n // 2, n - 1 - n // 2
+    up, back = part(ahead), part(-behind)
+    for step in range(ahead - 1, -1, -1):
+        up = lax.ppermute(up, "z", ring(1))
+        if step < behind:
+            back = lax.ppermute(back, "z", ring(-1))
+        if step:
+            up = plus(up, step).astype(BF16)
+            if step < behind:
+                back = plus(back, -step).astype(BF16)
+    return plus(up, 0) + back.astype(F32)
+
+
+def ring_gather_z(block):
+    n = lax.axis_size("z")
+    me = lax.axis_index("z")
+    rows = block.shape[0]
+    out = jnp.zeros((n * rows, block.shape[1]), block.dtype)
+
+    def put(out, piece, step):
+        return lax.dynamic_update_slice(out, piece, (lax.rem(me + step + n, n) * rows, 0))
+
+    out = put(out, block, 0)
+    up = back = block
+    for step in range(1, n // 2 + 1):
+        back = lax.ppermute(back, "z", ring(-1))
+        if step < n // 2:
+            up = lax.ppermute(up, "z", ring(1))
+            out = put(out, up, -step)
+        out = put(out, back, step)
+    return out
 
 
 def swiglu_back(pre, hidden):
@@ -93,7 +142,7 @@
     low_part = dot_nn(inputs, first)
     pre_part = dot_nn(inputs, weight) + adapter_scale * adapter_up(low_part)
     hidden_part = dot_nt(upstream, down_weight)
-    summed = scatter_z(jnp.concatenate([pre_part, low_part, hidden_part], axis=1))
+    summed = ring_scatter_z(jnp.concatenate([pre_part, low_part, hidden_part], axis=1).astype(BF16))
     width = 2 * hidden_units
     pre_own = summed[:, :width]
     act_own = swiglu_back(pre_own, summed[:, width + 2 * rank:])
@@ -101,25 +150,26 @@
         [jnp.where(upper, act_own, pre_own.astype(BF16)), summed[:, width:width + 2 * rank].astype(BF16)],
         axis=1,
     )
-    held = lax.all_gather(sent, "z", axis=0, tiled=True)
+    held = ring_gather_z(sent)
     act_or_pre, low = held[:, :width], held[:, width:]
     part, back = input_partial(act_or_pre)
     mine = core_sum(jnp.concatenate([part, back], axis=1))
-    mine = lax.all_to_all(mine.astype(BF16).reshape(-1, own, mine.shape[1]), CHIPS, 0, 0)
-    mine = jnp.sum(mine.astype(F32), axis=0).astype(BF16)
+    mine = mine.astype(BF16).reshape(-1, 1, own, mine.shape[1])
+    chips, wide = mine.shape[0], mine.shape[3]
+    mine = jnp.broadcast_to(mine, (chips, 2, own, wide)).reshape(2 * chips, own, wide)
+    mine = lax.all_to_all(mine, CHIPS + ("pipe",), 0, 0).reshape(chips, 2, own, wide)
+    mine = jnp.sum(mine[:, 1].astype(F32), axis=0).astype(BF16)
     grad_one, back_one = mine[:, :feat], mine[:, feat:]
 
-    handed = lax.ppermute(grad_one, "pipe", [(1, 0)])
-    sent = jnp.where(upper, jnp.pad(back_one, ((0, 0), (0, feat - 2 * rank))), handed)
+    sent = jnp.where(upper, jnp.pad(back_one, ((0, 0), (0, feat - 2 * rank))), grad_one)
     upstream = gather_dp(sent)
     back_upper = upstream[:, :2 * rank]
     hidden_own = scatter_z(dot_nt(upstream, down_weight))
-    hidden_all = to_all_chips(hidden_own.astype(BF16), "z").reshape(tokens, hidden_units)
+    hidden_all = ring_gather_z(hidden_own.astype(BF16))
     act_lower = swiglu_back(act_or_pre, hidden_all.astype(F32))
     part, back = input_partial(act_lower)
     mine = core_sum(part).astype(BF16).reshape(-1, own, feat)
     back = core_sum(back).astype(BF16)
-    chips = mine.shape[0]
     back = jnp.broadcast_to(back.reshape(1, -1, feat), (chips, back.size // feat, feat))
     got = lax.all_to_all(jnp.concatenate([mine, back], axis=1), CHIPS, 0, 0)
     got = jnp.sum(got.astype(F32), axis=0).astype(BF16)

time: 205 us -> 211 us (1.029)
  starting transfers between devices: 30.2 us -> 58.6 us
  blocking collectives: 87.6 us -> 60.4 us
  waiting for transfers between devices: 52.3 us -> 42.7 us
  other arithmetic: 10.8 us -> 17.6 us
  matrix products: 13 us -> 18.1 us
  local copies, waits for them, and re-layouts: 9.5 us -> 11.7 us
    all_to_all x1 -> x0, waiting for transfers between devices: 37.6 us -> none  [scatter_z(): return jnp.sum(lax.all_to_all(parts, 'z', 0, 0).astype(F32), axis=0)]
    ppermute x1 -> x21, starting transfers between devices: 1.29 us -> 33.9 us  [the longest x8 19.8 us: ring_gather_z(): back = lax.ppermute(back, 'z', ring(-1))]
    ppermute x1 -> x21, waiting for transfers between devices: 4.85 us -> 32.8 us  [the longest x4 18.7 us: ring_scatter_z(): up = lax.ppermute(up, 'z', ring(1))]
    all_gather x1 -> x0, blocking collectives: 21.1 us -> none  [local(): held = lax.all_gather(sent, 'z', axis=0, tiled=True)]
    all_to_all x3 -> x2, blocking collectives: 39.2 us -> 22.8 us  [to_all_chips(): lax.all_to_all(jnp.broadcast_to(block[None], (n,) + block.shape), axis, 0...]
    all_to_all x1 -> x0, starting transfers between devices: 8.19 us -> none  [scatter_z(): return jnp.sum(lax.all_to_all(parts, 'z', 0, 0).astype(F32), axis=0)]
    all_to_all x1, blocking collectives: 9.69 us -> 16.5 us  [local(): lax.all_to_all(mine, CHIPS + ('pipe',), 0, 0).reshape(chips, 2, own, wide)]
    convert_element_type x1 -> x4, other arithmetic: 0.09 us -> 5.37 us  [the longest x3 5.28 us: ring_scatter_z(): up = plus(up, step).astype(BF16)]
  transfers between devices with their start and end apart: 9 -> 28, of which waited for: 7 -> 18; matrix products, arithmetic and copies ran while one was open for 5% -> 6% of each run, Pallas kernels for 0% -> 0%
where the time goes in v2:
time: 211 us; the launch traced here: 210 us
  blocking collectives  60.4 us (29%)
  starting transfers between devices  58.6 us (28%)
  waiting for transfers between devices  42.7 us (20%)
  matrix products  18.1 us (9%)
  other arithmetic  17.6 us (8%)
  local copies, waits for them, and re-layouts  11.7 us (6%)
    all_to_all x2, blocking collectives, to_all_chips(): lax.all_to_all(jnp.broadcast_to(block[None], (n,) + block.shape), axis, 0...  22.8 us
    all_to_all x1, blocking collectives, scatter_z(): return jnp.sum(lax.all_to_all(parts, 'z', 0, 0).astype(F32), axis=0)  21.1 us
    ppermute x6, starting transfers between devices, core_swap(): return lax.ppermute(block, 'core', [(0, 1), (1, 0)])  20.6 us
    ppermute x8, starting transfers between devices, ring_gather_z(): back = lax.ppermute(back, 'z', ring(-1))  19.8 us
    ppermute x4, waiting for transfers between devices, ring_scatter_z(): up = lax.ppermute(up, 'z', ring(1))  18.7 us
    all_to_all x1, blocking collectives, local(): lax.all_to_all(mine, CHIPS + ('pipe',), 0, 0).reshape(chips, 2, own, wide)  16.5 us
    ppermute x3, starting transfers between devices, ring_scatter_z(): back = lax.ppermute(back, 'z', ring(-1))  9.29 us
    dot_general x10, matrix products, dot_nt(): lax.dot_general(a, b, (((1,), (1,)), ((), ())), preferred_element_type=F32)  8.25 us
  transfers between devices with their start and end apart: 28, of which 18 were waited for; matrix products, arithmetic and copies ran while one was open for 6% of the time, Pallas kernels for 0%

profile of v2, /device:TPU:1, one launch (start us, length us, event | category | flops | bytes accessed | tf_op | source)
XLA Modules:
  0.0 210.2 jit_solution(16456347672017365830)
XLA Ops:
  0.6 0.9 pad_maximum_fusion.8
  1.6 14.3 %all_to_all.25 = bf16[8,16,2048]{2,1,0:T(8,128)(2,1)S(1)} all-to-all(bf16[8,16,2048]{2,1,0:T(8,128)(2,1)S(1)} %broadcast_in_dim.37), channel_id=1, replica_groups=mesh['x'=4,'yl'=2,'core'=2,'pipe'=2,'z'=8] {'x','yl'}, dimensions={0} | all-to-all | bytes 1048576 | tf_op jit(solution)/shard_map/all_to_all | solution.py:32
  15.9 2.1 collective-permute-start
  18.0 4.5 %copy.22 = bf16[128,8,2,896]{3,1,2,0:T(8,128)(2,1)} copy(bf16[128,8,2,896]{3,2,1,0:T(2,128)(2,1)} %bitcast.86) | data formatting | bytes 7340032
  22.5 2.0 fusion.26
  24.8 1.2 fusion.48
  26.0 1.3 fusion.52
  27.3 1.6 copy.16
  29.0 1.9 fusion.11
  30.9 3.2 %fusion = bf16[256,1792]{1,0:T(8,128)(2,1)S(1)} fusion(bf16[256,1024]{1,0:T(8,128)(2,1)S(1)} %get-tuple-element.13, bf16[1024,1792]{1,0:T(8,128)(2,1)} %bitcast.87, f32[256,896]{1,0:T(8,128)S(1)} %copy-done.12, f32[256,896]{1,0:T(8,128)S(1)} %copy-done.13), kind=kOutput, calls=%fused_computation.1 | convolution fusion | flops 941359104 | bytes 6946816 | tf_op jit(solution)/shard_map/dot_general | solution.py:15
  35.0 1.6 collective-permute-start.1
  36.6 3.9 %collective-permute-start.5 = (bf16[32,2816]{1,0:T(8,128)(2,1)}, bf16[32,2816]{1,0:T(8,128)(2,1)}, u32[]{:S(2)}, u32[]{:S(2)}) collective-permute-start(bf16[32,2816]{1,0:T(8,128)(2,1)} %get-tuple-element.12), channel_id=1, source_target_pairs={{0,7},{1,0},{2,1},{3,2},{4,3},{5,4},{6,5},{7,6},{8,15},{9,8},{10,9... | collective-permute-start | bytes 540680 | tf_op jit(solution)/shard_map/ppermute | solution.py:68
  40.6 5.2 %collective-permute-done.1 = bf16[32,2816]{1,0:T(8,128)(2,1)} collective-permute-done((bf16[32,2816]{1,0:T(8,128)(2,1)}, bf16[32,2816]{1,0:T(8,128)(2,1)}, u32[]{:S(2)}, u32[]{:S(2)}) %collective-permute-start.1) | collective-permute-done | bytes 180256 | tf_op jit(solution)/shard_map/ppermute | solution.py:66
  45.8 1.6 fusion.38
  47.4 7.1 %collective-permute-done.2 = bf16[32,2816]{1,0:T(8,128)(2,1)} collective-permute-done((bf16[32,2816]{1,0:T(8,128)(2,1)}, bf16[32,2816]{1,0:T(8,128)(2,1)}, u32[]{:S(2)}, u32[]{:S(2)}) %collective-permute-start.2) | collective-permute-done | bytes 180256 | tf_op jit(solution)/shard_map/ppermute | solution.py:66
  54.5 1.8 fusion.37
  56.3 2.7 %collective-permute-start.6 = (bf16[32,2816]{1,0:T(8,128)(2,1)}, bf16[32,2816]{1,0:T(8,128)(2,1)}, u32[]{:S(2)}, u32[]{:S(2)}) collective-permute-start(bf16[32,2816]{1,0:T(8,128)(2,1)} %get-tuple-element.10), channel_id=1, source_target_pairs={{0,7},{1,0},{2,1},{3,2},{4,3},{5,4},{6,5},{7,6},{8,15},{9,8},{10,9... | collective-permute-start | bytes 540680 | tf_op jit(solution)/shard_map/ppermute | solution.py:68
  59.0 3.2 %collective-permute-done.3 = bf16[32,2816]{1,0:T(8,128)(2,1)} collective-permute-done((bf16[32,2816]{1,0:T(8,128)(2,1)}, bf16[32,2816]{1,0:T(8,128)(2,1)}, u32[]{:S(2)}, u32[]{:S(2)}) %collective-permute-start.3) | collective-permute-done | bytes 180256 | tf_op jit(solution)/shard_map/ppermute | solution.py:66
  62.2 1.8 fusion.36
  64.0 2.7 %collective-permute-start.7 = (bf16[32,2816]{1,0:T(8,128)(2,1)}, bf16[32,2816]{1,0:T(8,128)(2,1)}, u32[]{:S(2)}, u32[]{:S(2)}) collective-permute-start(bf16[32,2816]{1,0:T(8,128)(2,1)} %get-tuple-element.8), channel_id=1, source_target_pairs={{0,7},{1,0},{2,1},{3,2},{4,3},{5,4},{6,5},{7,6},{8,15},{9,8},{10,9... | collective-permute-start | bytes 540680 | tf_op jit(solution)/shard_map/ppermute | solution.py:68
  66.7 3.2 %collective-permute-done.4 = bf16[32,2816]{1,0:T(8,128)(2,1)} collective-permute-done((bf16[32,2816]{1,0:T(8,128)(2,1)}, bf16[32,2816]{1,0:T(8,128)(2,1)}, u32[]{:S(2)}, u32[]{:S(2)}) %collective-permute-start.4) | collective-permute-done | bytes 180256 | tf_op jit(solution)/shard_map/ppermute | solution.py:66
  69.9 1.1 fusion.81
  71.9 1.9 collective-permute-start.8
  74.5 2.6 %collective-permute-done.8 = bf16[32,1920]{1,0:T(8,128)(2,1)} collective-permute-done((bf16[32,1920]{1,0:T(8,128)(2,1)}, bf16[32,1920]{1,0:T(8,128)(2,1)}, u32[]{:S(2)}, u32[]{:S(2)}) %collective-permute-start.8) | collective-permute-done | bytes 122912 | tf_op jit(solution)/shard_map/ppermute | solution.py:90
  77.8 2.0 collective-permute-start.11
  79.8 0.9 constant_dynamic-update-slice_fusion.14
  80.7 1.8 collective-permute-done.10
  83.0 2.5 %collective-permute-start.13 = (bf16[32,1920]{1,0:T(8,128)(2,1)S(1)}, bf16[32,1920]{1,0:T(8,128)(2,1)S(1)}, u32[]{:S(2)}, u32[]{:S(2)}) collective-permute-start(bf16[32,1920]{1,0:T(8,128)(2,1)S(1)} %collective-permute-done.11), channel_id=1, source_target_pairs={{0,7},{1,0},{2,1},{3,2},{4,3},{5,4},{6,5},{7,6},{8,15},{9,8},{10,9... | collective-permute-start | bytes 368648 | tf_op jit(solution)/shard_map/ppermute | solution.py:88
  85.6 2.5 %collective-permute-done.13 = bf16[32,1920]{1,0:T(8,128)(2,1)S(1)} collective-permute-done((bf16[32,1920]{1,0:T(8,128)(2,1)S(1)}, bf16[32,1920]{1,0:T(8,128)(2,1)S(1)}, u32[]{:S(2)}, u32[]{:S(2)}) %collective-permute-start.13) | collective-permute-done | bytes 122912 | tf_op jit(solution)/shard_map/ppermute | solution.py:88
  88.0 3.4 %collective-permute-start.14 = (bf16[32,1920]{1,0:T(8,128)(2,1)S(1)}, bf16[32,1920]{1,0:T(8,128)(2,1)S(1)}, u32[]{:S(2)}, u32[]{:S(2)}) collective-permute-start(bf16[32,1920]{1,0:T(8,128)(2,1)S(1)} %collective-permute-done.13), channel_id=1, source_target_pairs={{0,7},{1,0},{2,1},{3,2},{4,3},{5,4},{6,5},{7,6},{8,15},{9,8},{10,9... | collective-permute-start | bytes 368648 | tf_op jit(solution)/shard_map/ppermute | solution.py:88
  91.5 1.8 collective-permute-done.14
  94.5 2.0 fusion.6
  96.5 1.2 concatenate.67
  97.7 8.0 %collective-permute-start.15 = (bf16[128,1152]{1,0:T(8,128)(2,1)S(1)}, bf16[128,1152]{1,0:T(8,128)(2,1)S(1)}, u32[]{:S(2)}, u32[]{:S(2)}) collective-permute-start(bf16[128,1152]{1,0:T(8,128)(2,1)S(1)} %slice.158), channel_id=1, source_target_pairs={{0,16},{16,0},{1,17},{17,1},{2,18},{18,2},{3,19},{19,3},{4,20},{20... | collective-permute-start | bytes 884744 | tf_op jit(solution)/shard_map/ppermute | solution.py:27
  105.8 1.2 collective-permute-done.15
  107.1 16.5 %all_to_all.26 = bf16[16,16,1152]{2,1,0:T(8,128)(2,1)S(1)} all-to-all(bf16[16,16,1152]{2,1,0:T(8,128)(2,1)S(1)} %bitcast.90), channel_id=1, replica_groups=mesh['x'=4,'yl'=2,'core'=2,'pipe'=2,'z'=8] {'x','yl','pipe'}, dimensions={0} | all-to-all | bytes 1179648 | tf_op jit(solution)/shard_map/all_to_all | solution.py:160
  123.7 8.5 %all_to_all.27 = bf16[8,16,1024]{2,1,0:T(8,128)(2,1)S(1)} all-to-all(bf16[8,16,1024]{2,1,0:T(8,128)(2,1)S(1)} %broadcast_in_dim.41), channel_id=1, replica_groups=mesh['x'=4,'yl'=2,'core'=2,'pipe'=2,'z'=8] {'x','yl'}, dimensions={0} | all-to-all | bytes 524288 | tf_op jit(solution)/shard_map/all_to_all | solution.py:32
  132.2 2.8 %collective-permute-start.16 = (bf16[128,1024]{1,0:T(8,128)(2,1)S(1)}, bf16[128,1024]{1,0:T(8,128)(2,1)S(1)}, u32[]{:S(2)}, u32[]{:S(2)}) collective-permute-start(bf16[128,1024]{1,0:T(8,128)(2,1)S(1)} %bitcast.96), channel_id=1, source_target_pairs={{0,16},{16,0},{1,17},{17,1},{2,18},{18,2},{3,19},{19,3},{4,20},{20... | collective-permute-start | bytes 786440 | tf_op jit(solution)/shard_map/ppermute | solution.py:27
  135.0 1.2 collective-permute-done.16
  136.9 21.1 %all_to_all.28 = bf16[8,32,896]{2,1,0:T(8,128)(2,1)S(1)} all-to-all(bf16[8,32,896]{2,1,0:T(8,128)(2,1)S(1)} %bitcast.101), channel_id=1, replica_groups=mesh['x'=4,'yl'=2,'core'=2,'pipe'=2,'z'=8] {'z'}, dimensions={0} | all-to-all | bytes 917504 | tf_op jit(solution)/shard_map/all_to_all | solution.py:44
  158.2 2.7 %collective-permute-start.18 = (bf16[32,896]{1,0:T(8,128)(2,1)S(1)}, bf16[32,896]{1,0:T(8,128)(2,1)S(1)}, u32[]{:S(2)}, u32[]{:S(2)}) collective-permute-start(bf16[32,896]{1,0:T(8,128)(2,1)S(1)} %reduce_sum.37), channel_id=1, source_target_pairs={{0,7},{1,0},{2,1},{3,2},{4,3},{5,4},{6,5},{7,6},{8,15},{9,8},{10,9... | collective-permute-start | bytes 172040 | tf_op jit(solution)/shard_map/ppermute | solution.py:88
  160.9 1.5 collective-permute-done.17
  162.5 2.7 %collective-permute-start.20 = (bf16[32,896]{1,0:T(8,128)(2,1)S(1)}, bf16[32,896]{1,0:T(8,128)(2,1)S(1)}, u32[]{:S(2)}, u32[]{:S(2)}) collective-permute-start(bf16[32,896]{1,0:T(8,128)(2,1)S(1)} %collective-permute-done.18), channel_id=1, source_target_pairs={{0,7},{1,0},{2,1},{3,2},{4,3},{5,4},{6,5},{7,6},{8,15},{9,8},{10,9... | collective-permute-start | bytes 172040 | tf_op jit(solution)/shard_map/ppermute | solution.py:88
  165.2 1.4 collective-permute-done.19
  166.7 2.7 %collective-permute-start.22 = (bf16[32,896]{1,0:T(8,128)(2,1)S(1)}, bf16[32,896]{1,0:T(8,128)(2,1)S(1)}, u32[]{:S(2)}, u32[]{:S(2)}) collective-permute-start(bf16[32,896]{1,0:T(8,128)(2,1)S(1)} %collective-permute-done.20), channel_id=1, source_target_pairs={{0,7},{1,0},{2,1},{3,2},{4,3},{5,4},{6,5},{7,6},{8,15},{9,8},{10,9... | collective-permute-start | bytes 172040 | tf_op jit(solution)/shard_map/ppermute | solution.py:88
  169.5 1.2 collective-permute-done.22
  170.7 3.0 %collective-permute-start.23 = (bf16[32,896]{1,0:T(8,128)(2,1)S(1)}, bf16[32,896]{1,0:T(8,128)(2,1)S(1)}, u32[]{:S(2)}, u32[]{:S(2)}) collective-permute-start(bf16[32,896]{1,0:T(8,128)(2,1)S(1)} %collective-permute-done.22), channel_id=1, source_target_pairs={{0,7},{1,0},{2,1},{3,2},{4,3},{5,4},{6,5},{7,6},{8,15},{9,8},{10,9... | collective-permute-start | bytes 172040 | tf_op jit(solution)/shard_map/ppermute | solution.py:88
  173.8 1.2 collective-permute-done.23
  175.8 1.1 fusion.25
  177.3 1.1 fusion.7
  178.4 1.7 slice.163
  180.1 6.4 %collective-permute-start.24 = (bf16[128,1024]{1,0:T(8,128)(2,1)}, bf16[128,1024]{1,0:T(8,128)(2,1)}, u32[]{:S(2)}, u32[]{:S(2)}) collective-permute-start(bf16[128,1024]{1,0:T(8,128)(2,1)} %slice.163), channel_id=1, source_target_pairs={{0,16},{16,0},{1,17},{17,1},{2,18},{18,2},{3,19},{19,3},{4,20},{20... | collective-permute-start | bytes 786440 | tf_op jit(solution)/shard_map/ppermute | solution.py:27
  186.5 1.2 collective-permute-done.25
  188.1 1.1 add_convert_fusion.1
  189.2 0.8 pad_maximum_fusion.4
  190.0 4.2 %all-to-all-start.4 = ((bf16[8,32,1024]{2,1,0:T(8,128)(2,1)}), bf16[8,32,1024]{2,1,0:T(8,128)(2,1)}, u32[]{:S(2)}, u32[]{:S(2)}) async-start(bf16[8,32,1024]{2,1,0:T(8,128)(2,1)} %pad_maximum_fusion.4), calls=%async_computation.4 | async-start | bytes 1048576 | tf_op jit(solution)/shard_map/all_to_all | solution.py:174
  194.2 1.2 broadcast_select_fusion
  195.4 0.9 convolution_bitcast_fusion.1
  196.3 1.0 convolution_bitcast_fusion
  197.3 6.1 %all-to-all-done.4 = bf16[8,32,1024]{2,1,0:T(8,128)(2,1)} async-done(((bf16[8,32,1024]{2,1,0:T(8,128)(2,1)}), bf16[8,32,1024]{2,1,0:T(8,128)(2,1)}, u32[]{:S(2)}, u32[]{:S(2)}) %all-to-all-start.4) | async-done | bytes 524320 | tf_op jit(solution)/shard_map/all_to_all | solution.py:174
  203.4 1.1 reduce_sum.38
  205.2 1.3 collective-permute-start.26
  206.5 1.8 maximum_multiply_fusion.1
  208.3 1.9 fusion.14
  (106 shorter events, 8.7 us)
Async XLA Ops:
  0.6 28.3 %copy-start = (bf16[1,896,1024]{2,1,0:T(8,128)(2,1)S(1)}, bf16[1,896,1024]{2,1,0:T(8,128)(2,1)}, u32[]{:S(2)}) copy-start(bf16[1,896,1024]{2,1,0:T(8,128)(2,1)} %param.9) | copy-start | bytes 5505028
  15.9 6.6 %collective-permute-start = (bf16[128,2048]{1,0:T(8,128)(2,1)S(1)}, bf16[128,2048]{1,0:T(8,128)(2,1)}, u32[]{:S(2)}, u32[]{:S(2)}) collective-permute-start(bf16[128,2048]{1,0:T(8,128)(2,1)S(1)} %bitcast.91), channel_id=1, source_target_pairs={{0,16},{16,0},{1,17},{17,1},{2,18},{18,2},{3,19},{19,3},{4,20},{20... | collective-permute-start | bytes 1572872 | tf_op jit(solution)/shard_map/ppermute | solution.py:27
  22.5 2.0 copy-start.6
  22.5 2.3 %copy-start.9 = (bf16[1,2,64,896]{3,2,1,0:T(8,128)(2,1)S(1)}, bf16[1,2,64,896]{3,2,1,0:T(8,128)(2,1)}, u32[]{:S(2)}) copy-start(bf16[1,2,64,896]{3,2,1,0:T(8,128)(2,1)} %param.11) | copy-start | bytes 688132
  24.4 6.4 %copy-start.1 = (bf16[256,1024]{1,0:T(8,128)(2,1)}, bf16[256,1024]{1,0:T(8,128)(2,1)S(1)}, u32[]{:S(2)}) copy-start(bf16[256,1024]{1,0:T(8,128)(2,1)S(1)} %get-tuple-element.13) | copy-start | bytes 1572868
  24.8 1.2 copy-start.14
  27.3 3.5 %copy-start.12 = (f32[256,896]{1,0:T(8,128)S(1)}, f32[256,896]{1,0:T(8,128)}, u32[]{:S(2)}) copy-start(f32[256,896]{1,0:T(8,128)} %fusion.48) | copy-start | bytes 2752516
  28.9 1.9 copy-start.13
  30.9 3.2 %copy-start.17 = (bf16[256,128]{1,0:T(8,128)(2,1)S(1)}, bf16[256,128]{1,0:T(8,128)(2,1)}, u32[]{:S(2)}) copy-start(bf16[256,128]{1,0:T(8,128)(2,1)} %copy.16) | copy-start | bytes 196612
  35.0 10.8 %collective-permute-start.1 = (bf16[32,2816]{1,0:T(8,128)(2,1)}, bf16[32,2816]{1,0:T(8,128)(2,1)}, u32[]{:S(2)}, u32[]{:S(2)}) collective-permute-start(bf16[32,2816]{1,0:T(8,128)(2,1)} %get-tuple-element.11), channel_id=1, source_target_pairs={{0,1},{1,2},{2,3},{3,4},{4,5},{5,6},{6,7},{7,0},{8,9},{9,10},{10,1... | collective-permute-start | bytes 540680 | tf_op jit(solution)/shard_map/ppermute | solution.py:66
  36.6 10.8 %collective-permute-start.5 = (bf16[32,2816]{1,0:T(8,128)(2,1)}, bf16[32,2816]{1,0:T(8,128)(2,1)}, u32[]{:S(2)}, u32[]{:S(2)}) collective-permute-start(bf16[32,2816]{1,0:T(8,128)(2,1)} %get-tuple-element.12), channel_id=1, source_target_pairs={{0,7},{1,0},{2,1},{3,2},{4,3},{5,4},{6,5},{7,6},{8,15},{9,8},{10,9... | collective-permute-start | bytes 540680 | tf_op jit(solution)/shard_map/ppermute | solution.py:68
  47.4 7.1 %collective-permute-start.2 = (bf16[32,2816]{1,0:T(8,128)(2,1)}, bf16[32,2816]{1,0:T(8,128)(2,1)}, u32[]{:S(2)}, u32[]{:S(2)}) collective-permute-start(bf16[32,2816]{1,0:T(8,128)(2,1)} %fusion.38), channel_id=1, source_target_pairs={{0,1},{1,2},{2,3},{3,4},{4,5},{5,6},{6,7},{7,0},{8,9},{9,10},{10,1... | collective-permute-start | bytes 540680 | tf_op jit(solution)/shard_map/ppermute | solution.py:66
  56.3 5.9 %collective-permute-start.3 = (bf16[32,2816]{1,0:T(8,128)(2,1)}, bf16[32,2816]{1,0:T(8,128)(2,1)}, u32[]{:S(2)}, u32[]{:S(2)}) collective-permute-start(bf16[32,2816]{1,0:T(8,128)(2,1)} %get-tuple-element.9), channel_id=1, source_target_pairs={{0,1},{1,2},{2,3},{3,4},{4,5},{5,6},{6,7},{7,0},{8,9},{9,10},{10,1... | collective-permute-start | bytes 540680 | tf_op jit(solution)/shard_map/ppermute | solution.py:66
  56.3 5.9 %collective-permute-start.6 = (bf16[32,2816]{1,0:T(8,128)(2,1)}, bf16[32,2816]{1,0:T(8,128)(2,1)}, u32[]{:S(2)}, u32[]{:S(2)}) collective-permute-start(bf16[32,2816]{1,0:T(8,128)(2,1)} %get-tuple-element.10), channel_id=1, source_target_pairs={{0,7},{1,0},{2,1},{3,2},{4,3},{5,4},{6,5},{7,6},{8,15},{9,8},{10,9... | collective-permute-start | bytes 540680 | tf_op jit(solution)/shard_map/ppermute | solution.py:68
  64.0 5.9 %collective-permute-start.4 = (bf16[32,2816]{1,0:T(8,128)(2,1)}, bf16[32,2816]{1,0:T(8,128)(2,1)}, u32[]{:S(2)}, u32[]{:S(2)}) collective-permute-start(bf16[32,2816]{1,0:T(8,128)(2,1)} %get-tuple-element.7), channel_id=1, source_target_pairs={{0,1},{1,2},{2,3},{3,4},{4,5},{5,6},{6,7},{7,0},{8,9},{9,10},{10,1... | collective-permute-start | bytes 540680 | tf_op jit(solution)/shard_map/ppermute | solution.py:66
  64.0 5.9 %collective-permute-start.7 = (bf16[32,2816]{1,0:T(8,128)(2,1)}, bf16[32,2816]{1,0:T(8,128)(2,1)}, u32[]{:S(2)}, u32[]{:S(2)}) collective-permute-start(bf16[32,2816]{1,0:T(8,128)(2,1)} %get-tuple-element.8), channel_id=1, source_target_pairs={{0,7},{1,0},{2,1},{3,2},{4,3},{5,4},{6,5},{7,6},{8,15},{9,8},{10,9... | collective-permute-start | bytes 540680 | tf_op jit(solution)/shard_map/ppermute | solution.py:68
  71.0 22.3 %copy-start.10 = (bf16[1,2,64,896]{3,2,1,0:T(8,128)(2,1)S(1)}, bf16[1,2,64,896]{3,2,1,0:T(8,128)(2,1)}, u32[]{:S(2)}) copy-start(bf16[1,2,64,896]{3,2,1,0:T(8,128)(2,1)} %param.11) | copy-start | bytes 688132
  71.9 5.3 %collective-permute-start.8 = (bf16[32,1920]{1,0:T(8,128)(2,1)}, bf16[32,1920]{1,0:T(8,128)(2,1)}, u32[]{:S(2)}, u32[]{:S(2)}) collective-permute-start(bf16[32,1920]{1,0:T(8,128)(2,1)} %get-tuple-element.17), channel_id=1, source_target_pairs={{0,1},{1,2},{2,3},{3,4},{4,5},{5,6},{6,7},{7,0},{8,9},{9,10},{10,1... | collective-permute-start | bytes 368648 | tf_op jit(solution)/shard_map/ppermute | solution.py:90
  73.7 4.1 %collective-permute-start.9 = (bf16[32,1920]{1,0:T(8,128)(2,1)}, bf16[32,1920]{1,0:T(8,128)(2,1)S(1)}, u32[]{:S(2)}, u32[]{:S(2)}) collective-permute-start(bf16[32,1920]{1,0:T(8,128)(2,1)} %get-tuple-element.17), channel_id=1, source_target_pairs={{0,7},{1,0},{2,1},{3,2},{4,3},{5,4},{6,5},{7,6},{8,15},{9,8},{10,9... | collective-permute-start | bytes 368648 | tf_op jit(solution)/shard_map/ppermute | solution.py:88
  77.1 5.4 %collective-permute-start.10 = (bf16[32,1920]{1,0:T(8,128)(2,1)}, bf16[32,1920]{1,0:T(8,128)(2,1)S(1)}, u32[]{:S(2)}, u32[]{:S(2)}) collective-permute-start(bf16[32,1920]{1,0:T(8,128)(2,1)} %collective-permute-done.8), channel_id=1, source_target_pairs={{0,1},{1,2},{2,3},{3,4},{4,5},{5,6},{6,7},{7,0},{8,9},{9,10},{10,1... | collective-permute-start | bytes 368648 | tf_op jit(solution)/shard_map/ppermute | solution.py:90
  77.8 5.2 %collective-permute-start.11 = (bf16[32,1920]{1,0:T(8,128)(2,1)S(1)}, bf16[32,1920]{1,0:T(8,128)(2,1)S(1)}, u32[]{:S(2)}, u32[]{:S(2)}) collective-permute-start(bf16[32,1920]{1,0:T(8,128)(2,1)S(1)} %collective-permute-done.9), channel_id=1, source_target_pairs={{0,7},{1,0},{2,1},{3,2},{4,3},{5,4},{6,5},{7,6},{8,15},{9,8},{10,9... | collective-permute-start | bytes 368648 | tf_op jit(solution)/shard_map/ppermute | solution.py:88
  82.6 8.9 %collective-permute-start.12 = (bf16[32,1920]{1,0:T(8,128)(2,1)S(1)}, bf16[32,1920]{1,0:T(8,128)(2,1)S(1)}, u32[]{:S(2)}, u32[]{:S(2)}) collective-permute-start(bf16[32,1920]{1,0:T(8,128)(2,1)S(1)} %collective-permute-done.10), channel_id=1, source_target_pairs={{0,1},{1,2},{2,3},{3,4},{4,5},{5,6},{6,7},{7,0},{8,9},{9,10},{10,1... | collective-permute-start | bytes 368648 | tf_op jit(solution)/shard_map/ppermute | solution.py:90
  83.0 5.0 %collective-permute-start.13 = (bf16[32,1920]{1,0:T(8,128)(2,1)S(1)}, bf16[32,1920]{1,0:T(8,128)(2,1)S(1)}, u32[]{:S(2)}, u32[]{:S(2)}) collective-permute-start(bf16[32,1920]{1,0:T(8,128)(2,1)S(1)} %collective-permute-done.11), channel_id=1, source_target_pairs={{0,7},{1,0},{2,1},{3,2},{4,3},{5,4},{6,5},{7,6},{8,15},{9,8},{10,9... | collective-permute-start | bytes 368648 | tf_op jit(solution)/shard_map/ppermute | solution.py:88
  88.0 5.3 %collective-permute-start.14 = (bf16[32,1920]{1,0:T(8,128)(2,1)S(1)}, bf16[32,1920]{1,0:T(8,128)(2,1)S(1)}, u32[]{:S(2)}, u32[]{:S(2)}) collective-permute-start(bf16[32,1920]{1,0:T(8,128)(2,1)S(1)} %collective-permute-done.13), channel_id=1, source_target_pairs={{0,7},{1,0},{2,1},{3,2},{4,3},{5,4},{6,5},{7,6},{8,15},{9,8},{10,9... | collective-permute-start | bytes 368648 | tf_op jit(solution)/shard_map/ppermute | solution.py:88
  91.4 3.1 %copy-start.4 = (bf16[128,8,2,896]{3,1,2,0:T(8,128)(2,1)S(1)}, bf16[128,8,2,896]{3,1,2,0:T(8,128)(2,1)}, u32[]{:S(2)}) copy-start(bf16[128,8,2,896]{3,1,2,0:T(8,128)(2,1)} %copy.22) | copy-start | bytes 11010052
  93.6 0.6 copy-start.15
  93.9 0.6 copy-start.16
  97.7 9.3 %collective-permute-start.15 = (bf16[128,1152]{1,0:T(8,128)(2,1)S(1)}, bf16[128,1152]{1,0:T(8,128)(2,1)S(1)}, u32[]{:S(2)}, u32[]{:S(2)}) collective-permute-start(bf16[128,1152]{1,0:T(8,128)(2,1)S(1)} %slice.158), channel_id=1, source_target_pairs={{0,16},{16,0},{1,17},{17,1},{2,18},{18,2},{3,19},{19,3},{4,20},{20... | collective-permute-start | bytes 884744 | tf_op jit(solution)/shard_map/ppermute | solution.py:27
  132.2 4.7 %copy-start.8 = (bf16[8,16,1024]{2,1,0:T(8,128)(2,1)}, bf16[8,16,1024]{2,1,0:T(8,128)(2,1)S(1)}, u32[]{:S(2)}) copy-start(bf16[8,16,1024]{2,1,0:T(8,128)(2,1)S(1)} %all_to_all.27) | copy-start | bytes 786436
  132.2 3.9 %collective-permute-start.16 = (bf16[128,1024]{1,0:T(8,128)(2,1)S(1)}, bf16[128,1024]{1,0:T(8,128)(2,1)S(1)}, u32[]{:S(2)}, u32[]{:S(2)}) collective-permute-start(bf16[128,1024]{1,0:T(8,128)(2,1)S(1)} %bitcast.96), channel_id=1, source_target_pairs={{0,16},{16,0},{1,17},{17,1},{2,18},{18,2},{3,19},{19,3},{4,20},{20... | collective-permute-start | bytes 786440 | tf_op jit(solution)/shard_map/ppermute | solution.py:27
  136.2 0.8 copy-start.18
  158.1 17.4 %copy-start.11 = (bf16[1,2,64,896]{3,2,1,0:T(8,128)(2,1)S(1)}, bf16[1,2,64,896]{3,2,1,0:T(8,128)(2,1)}, u32[]{:S(2)}) copy-start(bf16[1,2,64,896]{3,2,1,0:T(8,128)(2,1)} %param.11) | copy-start | bytes 688132
  158.1 4.3 %collective-permute-start.17 = (bf16[32,896]{1,0:T(8,128)(2,1)S(1)}, bf16[32,896]{1,0:T(8,128)(2,1)S(1)}, u32[]{:S(2)}, u32[]{:S(2)}) collective-permute-start(bf16[32,896]{1,0:T(8,128)(2,1)S(1)} %reduce_sum.37), channel_id=1, source_target_pairs={{0,1},{1,2},{2,3},{3,4},{4,5},{5,6},{6,7},{7,0},{8,9},{9,10},{10,1... | collective-permute-start | bytes 172040 | tf_op jit(solution)/shard_map/ppermute | solution.py:90
  158.2 4.2 %collective-permute-start.18 = (bf16[32,896]{1,0:T(8,128)(2,1)S(1)}, bf16[32,896]{1,0:T(8,128)(2,1)S(1)}, u32[]{:S(2)}, u32[]{:S(2)}) collective-permute-start(bf16[32,896]{1,0:T(8,128)(2,1)S(1)} %reduce_sum.37), channel_id=1, source_target_pairs={{0,7},{1,0},{2,1},{3,2},{4,3},{5,4},{6,5},{7,6},{8,15},{9,8},{10,9... | collective-permute-start | bytes 172040 | tf_op jit(solution)/shard_map/ppermute | solution.py:88
  160.9 14.9 %copy-start.5 = (bf16[128,8,2,896]{3,1,2,0:T(8,128)(2,1)S(1)}, bf16[128,8,2,896]{3,1,2,0:T(8,128)(2,1)}, u32[]{:S(2)}) copy-start(bf16[128,8,2,896]{3,1,2,0:T(8,128)(2,1)} %copy.22) | copy-start | bytes 11010052
  162.4 4.2 %collective-permute-start.19 = (bf16[32,896]{1,0:T(8,128)(2,1)S(1)}, bf16[32,896]{1,0:T(8,128)(2,1)S(1)}, u32[]{:S(2)}, u32[]{:S(2)}) collective-permute-start(bf16[32,896]{1,0:T(8,128)(2,1)S(1)} %collective-permute-done.17), channel_id=1, source_target_pairs={{0,1},{1,2},{2,3},{3,4},{4,5},{5,6},{6,7},{7,0},{8,9},{9,10},{10,1... | collective-permute-start | bytes 172040 | tf_op jit(solution)/shard_map/ppermute | solution.py:90
  162.5 4.2 %collective-permute-start.20 = (bf16[32,896]{1,0:T(8,128)(2,1)S(1)}, bf16[32,896]{1,0:T(8,128)(2,1)S(1)}, u32[]{:S(2)}, u32[]{:S(2)}) collective-permute-start(bf16[32,896]{1,0:T(8,128)(2,1)S(1)} %collective-permute-done.18), channel_id=1, source_target_pairs={{0,7},{1,0},{2,1},{3,2},{4,3},{5,4},{6,5},{7,6},{8,15},{9,8},{10,9... | collective-permute-start | bytes 172040 | tf_op jit(solution)/shard_map/ppermute | solution.py:88
  166.7 7.1 %collective-permute-start.21 = (bf16[32,896]{1,0:T(8,128)(2,1)S(1)}, bf16[32,896]{1,0:T(8,128)(2,1)S(1)}, u32[]{:S(2)}, u32[]{:S(2)}) collective-permute-start(bf16[32,896]{1,0:T(8,128)(2,1)S(1)} %collective-permute-done.19), channel_id=1, source_target_pairs={{0,1},{1,2},{2,3},{3,4},{4,5},{5,6},{6,7},{7,0},{8,9},{9,10},{10,1... | collective-permute-start | bytes 172040 | tf_op jit(solution)/shard_map/ppermute | solution.py:90
  166.7 4.0 %collective-permute-start.22 = (bf16[32,896]{1,0:T(8,128)(2,1)S(1)}, bf16[32,896]{1,0:T(8,128)(2,1)S(1)}, u32[]{:S(2)}, u32[]{:S(2)}) collective-permute-start(bf16[32,896]{1,0:T(8,128)(2,1)S(1)} %collective-permute-done.20), channel_id=1, source_target_pairs={{0,7},{1,0},{2,1},{3,2},{4,3},{5,4},{6,5},{7,6},{8,15},{9,8},{10,9... | collective-permute-start | bytes 172040 | tf_op jit(solution)/shard_map/ppermute | solution.py:88
  170.7 4.3 %collective-permute-start.23 = (bf16[32,896]{1,0:T(8,128)(2,1)S(1)}, bf16[32,896]{1,0:T(8,128)(2,1)S(1)}, u32[]{:S(2)}, u32[]{:S(2)}) collective-permute-start(bf16[32,896]{1,0:T(8,128)(2,1)S(1)} %collective-permute-done.22), channel_id=1, source_target_pairs={{0,7},{1,0},{2,1},{3,2},{4,3},{5,4},{6,5},{7,6},{8,15},{9,8},{10,9... | collective-permute-start | bytes 172040 | tf_op jit(solution)/shard_map/ppermute | solution.py:88
  175.5 1.5 copy-start.3
  175.8 1.4 copy-start.7
  180.1 8.0 %collective-permute-start.24 = (bf16[128,1024]{1,0:T(8,128)(2,1)}, bf16[128,1024]{1,0:T(8,128)(2,1)}, u32[]{:S(2)}, u32[]{:S(2)}) collective-permute-start(bf16[128,1024]{1,0:T(8,128)(2,1)} %slice.163), channel_id=1, source_target_pairs={{0,16},{16,0},{1,17},{17,1},{2,18},{18,2},{3,19},{19,3},{4,20},{20... | collective-permute-start | bytes 786440 | tf_op jit(solution)/shard_map/ppermute | solution.py:27
  186.5 1.2 collective-permute-start.25
  190.0 13.4 %all-to-all-start.4 = ((bf16[8,32,1024]{2,1,0:T(8,128)(2,1)}), bf16[8,32,1024]{2,1,0:T(8,128)(2,1)}, u32[]{:S(2)}, u32[]{:S(2)}) async-start(bf16[8,32,1024]{2,1,0:T(8,128)(2,1)} %pad_maximum_fusion.4), calls=%async_computation.4 | async-start | bytes 1048576 | tf_op jit(solution)/shard_map/all_to_all | solution.py:174
  195.4 12.9 %copy-start.2 = (bf16[256,1024]{1,0:T(8,128)(2,1)S(1)}, bf16[256,1024]{1,0:T(8,128)(2,1)}, u32[]{:S(2)}) copy-start(bf16[256,1024]{1,0:T(8,128)(2,1)} %copy-done.1) | copy-start | bytes 1572868
  205.2 3.1 %collective-permute-start.26 = (bf16[128,128]{1,0:T(8,128)(2,1)S(1)}, bf16[128,128]{1,0:T(8,128)(2,1)S(1)}, u32[]{:S(2)}, u32[]{:S(2)}) collective-permute-start(bf16[128,128]{1,0:T(8,128)(2,1)S(1)} %reshape.101), channel_id=1, source_target_pairs={{0,16},{16,0},{1,17},{17,1},{2,18},{18,2},{3,19},{19,3},{4,20},{20... | collective-permute-start | bytes 98312 | tf_op jit(solution)/shard_map/ppermute | solution.py:27

commit v3 on v1

v3 whole, which is shorter than its diff:
```python
import functools
import math

import jax
import jax.numpy as jnp
from jax import lax
from jax.experimental import pallas as pl
from jax.experimental.pallas import tpu as pltpu
from jax.sharding import Mesh, PartitionSpec as P

adapter_scale = 2.0
CHIPS = ("x", "yl")
F32 = jnp.float32
BF16 = jnp.bfloat16
VMEM_LIMIT = 40 * 2**20


def dot_nn(a, b):
    return jnp.dot(a, b, preferred_element_type=F32)


def dot_nt(a, b):
    return lax.dot_general(a, b, (((1,), (1,)), ((), ())), preferred_element_type=F32)


def dot_tn(a, b):
    return lax.dot_general(a, b, (((0,), (0,)), ((), ())), preferred_element_type=F32)


def kept(shape, dtype=BF16):
    return pltpu.VMEM(shape, dtype)


def call(kernel, outs, place, *args, scratch=(), flops=0):
    size = sum(a.size * a.dtype.itemsize for a in args)
    return pl.pallas_call(
        kernel,
        out_shape=outs,
        in_specs=[pl.BlockSpec(memory_space=pltpu.SMEM)]
        + [pl.BlockSpec(memory_space=pltpu.VMEM)] * len(args),
        out_specs=jax.tree.map(lambda _: pl.BlockSpec(memory_space=pltpu.VMEM), outs),
        scratch_shapes=list(scratch),
        compiler_params=pltpu.CompilerParams(vmem_limit_bytes=VMEM_LIMIT),
        cost_estimate=pl.CostEstimate(flops=flops, bytes_accessed=size, transcendentals=0),
    )(place, *[pltpu.with_memory_space_constraint(a, pltpu.VMEM) for a in args])


def core_swap(block):
    return lax.ppermute(block, "core", [(0, 1), (1, 0)])


def ring(block, step):
    n = lax.axis_size("z")
    return lax.ppermute(block, "z", [(i, (i + step) % n) for i in range(n)])


def swiglu_back(gate, up, hidden):
    sig = 1.0 / (1.0 + jnp.exp(-gate))
    gate_grad = hidden * up * sig * (1.0 + gate * (1.0 - sig))
    up_grad = hidden * gate * sig
    return gate_grad.astype(BF16), up_grad.astype(BF16)


def tiles(width, most=512):
    return [(lo, min(most, width - lo)) for lo in range(0, width, most)]


def forward_kernel(place, mine, other, weight, down, first, second, up, back, parts):
    n, rows, width = parts.shape
    feat = first.shape[0]
    hidden, rank = second.shape[2], second.shape[1]
    x = jnp.concatenate([mine[:, :feat], other[:, :feat]], axis=0)
    low = dot_nn(x, first[...]).astype(BF16)
    parts[:, :, 2 * hidden:2 * hidden + 2 * rank] = low.reshape(n, rows, 2 * rank)
    for k in range(2):
        for lo, size in tiles(hidden):
            at = k * hidden + lo
            pre = dot_nn(x, weight[:, at:at + size])
            pre += adapter_scale * dot_nn(low[:, k * rank:(k + 1) * rank], second[k, :, lo:lo + size])
            parts[:, :, at:at + size] = pre.astype(BF16).reshape(n, rows, size)
    g = jnp.concatenate([mine[:, feat:], other[:, feat:]], axis=0)
    at = 2 * hidden + 2 * rank
    for lo, size in tiles(hidden):
        part = dot_nt(g, down[lo:lo + size, :])
        parts[:, :, at + lo:at + lo + size] = part.astype(BF16).reshape(n, rows, size)
    far = lax.rem(place[0] + n // 2, n)
    up[...] = parts[far, :, :width // 2]
    back[...] = parts[far, :, width // 2:]


def ring_add_kernel(step, place, up_in, back_in, parts, up, back):
    n, _, width = parts.shape
    half = width // 2
    ahead = lax.rem(place[0] + step, n)
    behind = lax.rem(place[0] + n - step, n)
    if up_in.shape[1] == half:
        up[:, :half] = (up_in[...].astype(F32) + parts[ahead, :, :half].astype(F32)).astype(BF16)
        up[:, half:] = parts[ahead, :, half:]
        back[:, :half] = parts[behind, :, :half]
        back[:, half:] = (back_in[...].astype(F32) + parts[behind, :, half:].astype(F32)).astype(BF16)
    else:
        up[...] = (up_in[...].astype(F32) + parts[ahead].astype(F32)).astype(BF16)
        back[...] = (back_in[...].astype(F32) + parts[behind].astype(F32)).astype(BF16)


def middle_kernel(place, up_in, back_in, parts, sent):
    total = up_in[...].astype(F32) + back_in[...].astype(F32) + parts[place[0]].astype(F32)
    width = sent.shape[1]
    hidden = total.shape[1] - width
    gate, up = total[:, :hidden], total[:, hidden:2 * hidden]
    gate_grad, up_grad = swiglu_back(gate, up, total[:, width:])
    upper = place[1] == 1
    sent[:, :hidden] = jnp.where(upper, gate_grad, gate.astype(BF16))
    sent[:, hidden:2 * hidden] = jnp.where(upper, up_grad, up.astype(BF16))
    sent[:, 2 * hidden:] = total[:, 2 * hidden:width].astype(BF16)


def collect(place, pieces, whole):
    n, rows = len(pieces), pieces[0].shape[0]
    for step, piece in enumerate(pieces):
        at = pl.multiple_of(lax.rem(place[0] + step, n) * rows, rows)
        whole[pl.ds(at, rows), :] = piece[...]


def input_partials(act, weight, first, second, mine, other):
    feat = first.shape[0]
    hidden, rank = second.shape[2], second.shape[1]
    half = mine.shape[0]
    back = jnp.concatenate(
        [dot_nt(act[:, k * hidden:(k + 1) * hidden], second[k]) for k in range(2)], axis=1
    )
    mine[:, feat:] = back[:half]
    other[:, feat:] = back[half:].astype(BF16)
    scaled = (adapter_scale * back).astype(BF16)
    for lo, size in tiles(feat, 256):
        part = dot_nt(act[:, :2 * hidden], weight[lo:lo + size, :]) + dot_nt(scaled, first[lo:lo + size, :])
        mine[:, lo:lo + size] = part[:half]
        other[:, lo:lo + size] = part[half:].astype(BF16)


def backward_kernel(count, place, *refs):
    pieces = refs[:count]
    weight, first, second, whole, mine, other = refs[count:]
    collect(place, pieces, whole)
    input_partials(whole, weight, first, second, mine, other)


def lower_kernel(count, place, *refs):
    pieces = refs[:count]
    whole, weight, first, second, act, mine, other, hidden_grad = refs[count:]
    collect(place, pieces, hidden_grad)
    hidden = hidden_grad.shape[1]
    for lo, size in tiles(hidden, 128):
        gate_grad, up_grad = swiglu_back(
            whole[:, lo:lo + size].astype(F32),
            whole[:, hidden + lo:hidden + lo + size].astype(F32),
            hidden_grad[:, lo:lo + size].astype(F32),
        )
        act[:, lo:lo + size] = gate_grad
        act[:, hidden + lo:hidden + lo + size] = up_grad
    input_partials(act, weight, first, second, mine, other)


def to_both_kernel(place, mine, other, out):
    total = (mine[...] + other[...].astype(F32)).astype(BF16)
    chips, sections, rows, width = out.shape
    for section in range(sections):
        out[:, section] = total.reshape(chips, rows, width)


def hand_kernel(place, got, grad, out):
    feat = grad.shape[1]
    total = jnp.sum(got[:, 1].astype(F32), axis=0).astype(BF16)
    grad[...] = total[:, :feat]
    back = jnp.concatenate([total[:, feat:], jnp.zeros((total.shape[0], 2 * feat - total.shape[1]), BF16)], axis=1)
    message = jnp.where(place[1] == 1, back, total[:, :feat])
    for chip in range(out.shape[0]):
        out[chip] = message


def last_message_kernel(place, mine, other, out):
    total = (mine[...] + other[...].astype(F32)).astype(BF16)
    chips, rows, _ = out.shape
    wide = total.shape[1] - (out.shape[2] - total.shape[1]) // (chips - 1)
    rank = total.shape[1] - wide
    out[:, :, :wide] = total[:, :wide].reshape(chips, rows, wide)
    for chip in range(chips):
        block = total[chip * rows:(chip + 1) * rows, wide:]
        for target in range(chips):
            out[target, :, wide + chip * rank:wide + (chip + 1) * rank] = block


def last_sum_kernel(place, got, grad_one, grad, back):
    chips, rows, _ = got.shape
    feat, rank = grad.shape[1], back.shape[1]
    total = jnp.sum(got[...].astype(F32), axis=0).astype(BF16)
    grad[...] = jnp.where(place[1] == 1, grad_one[...], total[:, :feat])
    for chip in range(chips):
        back[chip * rows:(chip + 1) * rows, :] = total[:, feat + chip * rank:feat + (chip + 1) * rank]


def grad_up_kernel(factor, place, whole, act, out):
    hidden, rank = out.shape[2], out.shape[1]
    for k in range(2):
        low = whole[:, 2 * hidden + k * rank:2 * hidden + (k + 1) * rank]
        for lo, size in tiles(hidden):
            at = k * hidden + lo
            used = jnp.where(place[1] == 1, whole[:, at:at + size], act[:, at:at + size])
            out[k, :, lo:lo + size] = dot_tn(low, used) * factor


def grad_down_kernel(factor, place, mine, other, upper_mine, upper_other, lower_mine, lower_other, out):
    feat, rank = out.shape
    upper = place[1] == 1
    back = jnp.where(upper, upper_mine[:, :rank], lower_mine[...])
    back_other = jnp.where(upper, upper_other[:, :rank], lower_other[...])
    for lo, size in tiles(feat, 256):
        part = dot_tn(mine[:, lo:lo + size], back) + dot_tn(other[:, lo:lo + size], back_other)
        out[lo:lo + size, :] = part * factor


def local(acts, output_gradient, gate_up_weight, down, adapter_first_weight, adapter_second_weight):
    micro, rows, feat = acts.shape[1:]
    hidden = down.shape[1]
    rank = adapter_second_weight.shape[2]
    own = micro * rows
    weight = gate_up_weight[0].reshape(feat, 2 * hidden)
    down_weight = down[0]
    first = adapter_first_weight[0]
    second = adapter_second_weight[0]
    chips = lax.axis_size(CHIPS)
    tokens = own * chips * lax.axis_size("core")
    half = tokens // 2
    n = lax.axis_size("z")
    block = tokens // n
    width = 2 * hidden + 2 * rank
    factor = adapter_scale / math.sqrt(tokens)
    place = jnp.stack([lax.axis_index("z"), lax.axis_index("pipe")]).astype(jnp.int32)

    def ring_gather(piece):
        up = back = piece
        ups, backs = [], []
        for step in range(1, n // 2 + 1):
            back = ring(back, -1)
            backs.append(back)
            if step < n // 2:
                up = ring(up, 1)
                ups.append(up)
        return [piece] + backs + ups[::-1]

    def to_all_chips(message):
        got = lax.all_to_all(message, CHIPS, 0, 0)
        got = got.reshape(half, message.shape[2])
        return got, core_swap(got)

    both = jnp.concatenate([acts[0].reshape(own, feat), output_gradient.reshape(own, feat)], axis=1)
    mine, other = to_all_chips(jnp.broadcast_to(both[None], (chips, own, 2 * feat)))

    full = width + hidden
    up, back, parts = call(
        forward_kernel,
        (kept((block, full // 2)), kept((block, full // 2)), kept((n, block, full))),
        place, mine, other, weight, down_weight, first, second,
        flops=2 * tokens * feat * full,
    )
    for step in range(n // 2 - 1, -1, -1):
        up, back = ring(up, 1), ring(back, -1)
        if step:
            up, back = call(
                functools.partial(ring_add_kernel, step),
                (kept((block, full)), kept((block, full))), place, up, back, parts,
            )
    sent = call(middle_kernel, kept((block, width)), place, up, back, parts)
    whole, half_mine, half_other = call(
        functools.partial(backward_kernel, n),
        (kept((tokens, width)), kept((half, feat + 2 * rank), F32), kept((half, feat + 2 * rank))),
        place, *ring_gather(sent), weight, first, second,
        flops=2 * tokens * feat * width,
    )
    message = call(
        to_both_kernel, kept((chips, 2, own, feat + 2 * rank)), place, half_mine, core_swap(half_other)
    )
    got = lax.all_to_all(message.reshape(chips * 2, own, -1), CHIPS + ("pipe",), 0, 0)
    grad_one, message = call(
        hand_kernel, (kept((own, feat)), kept((chips, own, feat))), place, got.reshape(message.shape)
    )

    next_mine, next_other = to_all_chips(message)
    upstream = jnp.concatenate([next_mine, next_other], axis=0)
    hidden_part = dot_nt(upstream, down_weight).astype(BF16).reshape(n, block, hidden)
    hidden_own = lax.all_to_all(hidden_part, "z", 0, 0)
    hidden_own = jnp.sum(hidden_own.astype(F32), axis=0).astype(BF16)
    act, half_mine, half_other = call(
        functools.partial(lower_kernel, n),
        (kept((tokens, 2 * hidden)), kept((half, feat + 2 * rank), F32), kept((half, feat + 2 * rank))),
        place, *ring_gather(hidden_own), whole, weight, first, second,
        scratch=[pltpu.VMEM((tokens, hidden), BF16)],
        flops=2 * tokens * feat * width,
    )
    message = call(
        last_message_kernel, kept((chips, own, feat + chips * 2 * rank)), place, half_mine, core_swap(half_other)
    )
    got = lax.all_to_all(message, CHIPS, 0, 0)
    grad_up = call(
        functools.partial(grad_up_kernel, factor),
        jax.ShapeDtypeStruct((2, rank, hidden), F32), place, whole, act,
        flops=4 * tokens * rank * hidden,
    )
    grad_inputs, lower_mine = call(
        last_sum_kernel,
        (jax.ShapeDtypeStruct((own, feat), BF16), kept((half, 2 * rank))), place, got, grad_one,
    )
    grad_down = call(
        functools.partial(grad_down_kernel, factor),
        jax.ShapeDtypeStruct((feat, 2 * rank), F32),
        place, mine, other, next_mine, next_other, lower_mine, core_swap(lower_mine),
        flops=4 * tokens * feat * rank,
    )
    return grad_inputs.reshape(1, micro, rows, feat), grad_down[None], grad_up[None]


def solution(mesh):
    sizes = dict(mesh.shape)
    fine = Mesh(
        mesh.devices.reshape(sizes["dp"] // 4, 2, 2, sizes["pipe"], sizes["tensor"]),
        ("x", "yl", "core", "pipe", "z"),
    )
    dp = ("x", "yl", "core")
    in_specs = (
        P("pipe", None, dp, "z"),
        P(None, dp, "z"),
        P("pipe", "z", None, dp),
        P("pipe", dp, "z"),
        P("pipe", "z", None),
        P("pipe", None, None, dp),
    )
    out_specs = (
        P("pipe", None, dp, "z"),
        P("pipe", "z", None),
        P("pipe", None, None, dp),
    )
    return jax.shard_map(local, mesh=fine, in_specs=in_specs, out_specs=out_specs, check_vma=False)
```

time: 205 us -> 184 us (0.90)
  starting transfers between devices: 30.2 us -> 55.1 us
  waiting for transfers between devices: 52.3 us -> 32.6 us
  Pallas kernels: 0 us -> 16.6 us
  blocking collectives: 87.6 us -> 71.2 us
  matrix products: 13 us -> 0.74 us
  other arithmetic: 10.8 us -> 1.95 us
  local copies, waits for them, and re-layouts: 9.5 us -> 4.95 us
    all_to_all x2 -> x0, waiting for transfers between devices: 43.7 us -> none  [the longest x1 37.6 us: scatter_z(): return jnp.sum(lax.all_to_all(parts, 'z', 0, 0).astype(F32), axis=0)]
    ppermute x1 -> x22, starting transfers between devices: 1.29 us -> 33.7 us  [ring(): return lax.ppermute(block, 'z', [(i, (i + step) % n) for i in range(n)])]
    ppermute x1 -> x22, waiting for transfers between devices: 4.85 us -> 29.1 us  [ring(): return lax.ppermute(block, 'z', [(i, (i + step) % n) for i in range(n)])]
    all_gather x1 -> x0, blocking collectives: 21.1 us -> none  [local(): held = lax.all_gather(sent, 'z', axis=0, tiled=True)]
    pallas_call x0 -> x13, Pallas kernels: none -> 16.6 us  [call(): pl.pallas_call(kernel, out_shape=outs, in_specs=[pl.BlockSpec(memory_spac...]
    all_to_all x2 -> x0, starting transfers between devices: 12.3 us -> none  [the longest x1 8.19 us: scatter_z(): return jnp.sum(lax.all_to_all(parts, 'z', 0, 0).astype(F32), axis=0)]
    dot_general x10 -> x1, matrix products: 7.11 us -> 0.74 us  [dot_nt(): lax.dot_general(a, b, (((1,), (1,)), ((), ())), preferred_element_type=F32)]
    dot_general x7 -> x0, matrix products: 5.94 us -> none  [the longest x3 3.85 us: dot_tn(): lax.dot_general(a, b, (((0,), (0,)), ((), ())), preferred_element_type=F32)]
  transfers between devices with their start and end apart: 9 -> 27, of which waited for: 7 -> 19; matrix products, arithmetic and copies ran while one was open for 5% -> 2% of each run, Pallas kernels for 0% -> 1%
where the time goes in v3:
time: 184 us
  blocking collectives  71.2 us (39%)
  starting transfers between devices  55.1 us (30%)
  waiting for transfers between devices  32.6 us (18%)
  Pallas kernels  16.6 us (9%)
  local copies, waits for them, and re-layouts  4.95 us (3%)
  other arithmetic  1.95 us (1%)
    ppermute x22, starting transfers between devices, ring(): return lax.ppermute(block, 'z', [(i, (i + step) % n) for i in range(n)])  33.7 us
    ppermute x22, waiting for transfers between devices, ring(): return lax.ppermute(block, 'z', [(i, (i + step) % n) for i in range(n)])  29.1 us
    all_to_all x2, blocking collectives, to_all_chips(): got = lax.all_to_all(message, CHIPS, 0, 0)  22.8 us
    ppermute x5, starting transfers between devices, core_swap(): return lax.ppermute(block, 'core', [(0, 1), (1, 0)])  21.4 us
    all_to_all x1, blocking collectives, local(): hidden_own = lax.all_to_all(hidden_part, 'z', 0, 0)  20.7 us
    pallas_call x13, Pallas kernels, call(): pl.pallas_call(kernel, out_shape=outs, in_specs=[pl.BlockSpec(memory_spac...  16.6 us
    all_to_all x1, blocking collectives, local(): lax.all_to_all(message.reshape(chips * 2, own, -1), CHIPS + ('pipe',), 0, 0)  16.5 us
    all_to_all x1, blocking collectives, local(): got = lax.all_to_all(message, CHIPS, 0, 0)  11.2 us
  transfers between devices with their start and end apart: 27, of which 19 were waited for; matrix products, arithmetic and copies ran while one was open for 2% of the time, Pallas kernels for 1%

profile of v3, /device:TPU:1, one launch (start us, length us, event | category | flops | bytes accessed | tf_op | source)
XLA Modules:
  0.0 184.0 jit_solution(6445009408252428855)
XLA Ops:
  0.6 0.8 pad_maximum_fusion
  1.5 14.3 %all_to_all.25 = bf16[8,16,2048]{2,1,0:T(8,128)(2,1)S(1)} all-to-all(bf16[8,16,2048]{2,1,0:T(8,128)(2,1)S(1)} %broadcast_in_dim.12), channel_id=1, replica_groups=mesh['x'=4,'yl'=2,'core'=2,'pipe'=2,'z'=8] {'x','yl'}, dimensions={0} | all-to-all | bytes 1048576 | tf_op jit(solution)/shard_map/all_to_all | solution.py:252
  15.7 2.1 %collective-permute-start = (bf16[128,2048]{1,0:T(8,128)(2,1)S(1)}, bf16[128,2048]{1,0:T(8,128)(2,1)S(1)}, u32[]{:S(2)}, u32[]{:S(2)}) collective-permute-start(bf16[128,2048]{1,0:T(8,128)(2,1)S(1)} %bitcast.23), channel_id=1, source_target_pairs={{0,16},{16,0},{1,17},{17,1},{2,18},{18,2},{3,19},{19,3},{4,20},{20... | collective-permute-start | bytes 1572872 | tf_op jit(solution)/shard_map/ppermute | solution.py:49
  17.8 2.9 %copy.9 = bf16[128,8,2,896]{3,1,2,0:T(8,128)(2,1)S(1)} copy(bf16[128,8,2,896]{3,2,1,0:T(2,128)(2,1)} %bitcast.38) | data formatting | bytes 7340032
  20.8 2.8 %shard_map.85 = (bf16[32,1408]{1,0:T(8,128)(2,1)S(1)}, bf16[32,1408]{1,0:T(8,128)(2,1)S(1)}, bf16[8,32,2816]{2,1,0:T(8,128)(2,1)S(1)}) custom-call(s32[2]{0:T(128)S(1)} %pad_add_fusion.place, bf16[128,2048]{1,0:T(8,128)(2,1)S(1)} %bitcast.24, bf16[128,2048]{1,0:T(8,128)(2,1)S(1)} %collective-permute-done.other, bf16[1024,1792]{1,0:T(8,128)(2,1)S(1)} %bitcast.20, ...), custom_call_target="tpu_custom_call" | custom-call | flops 1476395008 | bytes 7045120 | tf_op jit(solution)/shard_map/pallas_call | solution.py:36
  23.6 1.7 collective-permute-start.1
  25.3 4.0 %collective-permute-start.2 = (bf16[32,1408]{1,0:T(8,128)(2,1)S(1)}, bf16[32,1408]{1,0:T(8,128)(2,1)S(1)}, u32[]{:S(2)}, u32[]{:S(2)}) collective-permute-start(bf16[32,1408]{1,0:T(8,128)(2,1)S(1)} %get-tuple-element.23), channel_id=1, source_target_pairs={{0,7},{1,0},{2,1},{3,2},{4,3},{5,4},{6,5},{7,6},{8,15},{9,8},{10,9... | collective-permute-start | bytes 270344 | tf_op jit(solution)/shard_map/ppermute | solution.py:54
  29.4 2.9 %collective-permute-done.1.up_in = bf16[32,1408]{1,0:T(8,128)(2,1)S(1)} collective-permute-done((bf16[32,1408]{1,0:T(8,128)(2,1)S(1)}, bf16[32,1408]{1,0:T(8,128)(2,1)S(1)}, u32[]{:S(2)}, u32[]{:S(2)}) %collective-permute-start.1) | collective-permute-done | bytes 90144 | tf_op jit(solution)/shard_map/ppermute | solution.py:54
  32.3 0.6 shard_map.86
  32.9 0.1 collective-permute-start.3
  32.9 2.7 %collective-permute-start.4 = (bf16[32,2816]{1,0:T(8,128)(2,1)S(1)}, bf16[32,2816]{1,0:T(8,128)(2,1)S(1)}, u32[]{:S(2)}, u32[]{:S(2)}) collective-permute-start(bf16[32,2816]{1,0:T(8,128)(2,1)S(1)} %get-tuple-element.26), channel_id=1, source_target_pairs={{0,7},{1,0},{2,1},{3,2},{4,3},{5,4},{6,5},{7,6},{8,15},{9,8},{10,9... | collective-permute-start | bytes 540680 | tf_op jit(solution)/shard_map/ppermute | solution.py:54
  35.6 4.1 %collective-permute-done.3.up_in = bf16[32,2816]{1,0:T(8,128)(2,1)S(1)} collective-permute-done((bf16[32,2816]{1,0:T(8,128)(2,1)S(1)}, bf16[32,2816]{1,0:T(8,128)(2,1)S(1)}, u32[]{:S(2)}, u32[]{:S(2)}) %collective-permute-start.3) | collective-permute-done | bytes 180256 | tf_op jit(solution)/shard_map/ppermute | solution.py:54
  39.7 0.6 shard_map.87
  40.3 1.1 collective-permute-start.5
  41.5 1.6 collective-permute-start.6
  43.1 2.9 %collective-permute-done.5.up_in = bf16[32,2816]{1,0:T(8,128)(2,1)S(1)} collective-permute-done((bf16[32,2816]{1,0:T(8,128)(2,1)S(1)}, bf16[32,2816]{1,0:T(8,128)(2,1)S(1)}, u32[]{:S(2)}, u32[]{:S(2)}) %collective-permute-start.5) | collective-permute-done | bytes 180256 | tf_op jit(solution)/shard_map/ppermute | solution.py:54
  45.9 0.6 shard_map.88
  46.6 1.8 collective-permute-start.7
  48.4 1.0 collective-permute-start.8
  49.4 2.8 %collective-permute-done.7.up_in = bf16[32,2816]{1,0:T(8,128)(2,1)S(1)} collective-permute-done((bf16[32,2816]{1,0:T(8,128)(2,1)S(1)}, bf16[32,2816]{1,0:T(8,128)(2,1)S(1)}, u32[]{:S(2)}, u32[]{:S(2)}) %collective-permute-start.7) | collective-permute-done | bytes 180256 | tf_op jit(solution)/shard_map/ppermute | solution.py:54
  52.2 0.5 collective-permute-done.8.back_in
  52.7 0.7 shard_map.89.refs_0_
  53.4 2.3 %collective-permute-start.9 = (bf16[32,1920]{1,0:T(8,128)(2,1)S(1)}, bf16[32,1920]{1,0:T(8,128)(2,1)S(1)}, u32[]{:S(2)}, u32[]{:S(2)}) collective-permute-start(bf16[32,1920]{1,0:T(8,128)(2,1)S(1)} %shard_map.89.refs_0_), channel_id=1, source_target_pairs={{0,7},{1,0},{2,1},{3,2},{4,3},{5,4},{6,5},{7,6},{8,15},{9,8},{10,9... | collective-permute-start | bytes 368648 | tf_op jit(solution)/shard_map/ppermute | solution.py:54
  55.7 2.1 %collective-permute-done.9.refs_1_ = bf16[32,1920]{1,0:T(8,128)(2,1)S(1)} collective-permute-done((bf16[32,1920]{1,0:T(8,128)(2,1)S(1)}, bf16[32,1920]{1,0:T(8,128)(2,1)S(1)}, u32[]{:S(2)}, u32[]{:S(2)}) %collective-permute-start.9) | collective-permute-done | bytes 122912 | tf_op jit(solution)/shard_map/ppermute | solution.py:54
  57.8 2.8 %collective-permute-start.10 = (bf16[32,1920]{1,0:T(8,128)(2,1)S(1)}, bf16[32,1920]{1,0:T(8,128)(2,1)S(1)}, u32[]{:S(2)}, u32[]{:S(2)}) collective-permute-start(bf16[32,1920]{1,0:T(8,128)(2,1)S(1)} %collective-permute-done.9.refs_1_), channel_id=1, source_target_pairs={{0,7},{1,0},{2,1},{3,2},{4,3},{5,4},{6,5},{7,6},{8,15},{9,8},{10,9... | collective-permute-start | bytes 368648 | tf_op jit(solution)/shard_map/ppermute | solution.py:54
  60.7 3.0 %collective-permute-done.10.refs_2_ = bf16[32,1920]{1,0:T(8,128)(2,1)S(1)} collective-permute-done((bf16[32,1920]{1,0:T(8,128)(2,1)S(1)}, bf16[32,1920]{1,0:T(8,128)(2,1)S(1)}, u32[]{:S(2)}, u32[]{:S(2)}) %collective-permute-start.10) | collective-permute-done | bytes 122912 | tf_op jit(solution)/shard_map/ppermute | solution.py:54
  63.6 3.4 %collective-permute-start.11 = (bf16[32,1920]{1,0:T(8,128)(2,1)S(1)}, bf16[32,1920]{1,0:T(8,128)(2,1)S(1)}, u32[]{:S(2)}, u32[]{:S(2)}) collective-permute-start(bf16[32,1920]{1,0:T(8,128)(2,1)S(1)} %collective-permute-done.10.refs_2_), channel_id=1, source_target_pairs={{0,7},{1,0},{2,1},{3,2},{4,3},{5,4},{6,5},{7,6},{8,15},{9,8},{10,9... | collective-permute-start | bytes 368648 | tf_op jit(solution)/shard_map/ppermute | solution.py:54
  67.1 2.1 %collective-permute-done.11.refs_3_ = bf16[32,1920]{1,0:T(8,128)(2,1)S(1)} collective-permute-done((bf16[32,1920]{1,0:T(8,128)(2,1)S(1)}, bf16[32,1920]{1,0:T(8,128)(2,1)S(1)}, u32[]{:S(2)}, u32[]{:S(2)}) %collective-permute-start.11) | collective-permute-done | bytes 122912 | tf_op jit(solution)/shard_map/ppermute | solution.py:54
  69.2 3.4 %collective-permute-start.12 = (bf16[32,1920]{1,0:T(8,128)(2,1)S(1)}, bf16[32,1920]{1,0:T(8,128)(2,1)S(1)}, u32[]{:S(2)}, u32[]{:S(2)}) collective-permute-start(bf16[32,1920]{1,0:T(8,128)(2,1)S(1)} %collective-permute-done.11.refs_3_), channel_id=1, source_target_pairs={{0,7},{1,0},{2,1},{3,2},{4,3},{5,4},{6,5},{7,6},{8,15},{9,8},{10,9... | collective-permute-start | bytes 368648 | tf_op jit(solution)/shard_map/ppermute | solution.py:54
  72.6 1.9 %collective-permute-done.12.refs_4_ = bf16[32,1920]{1,0:T(8,128)(2,1)S(1)} collective-permute-done((bf16[32,1920]{1,0:T(8,128)(2,1)S(1)}, bf16[32,1920]{1,0:T(8,128)(2,1)S(1)}, u32[]{:S(2)}, u32[]{:S(2)}) %collective-permute-start.12) | collective-permute-done | bytes 122912 | tf_op jit(solution)/shard_map/ppermute | solution.py:54
  74.4 2.2 %shard_map.90 = (bf16[256,1920]{1,0:T(8,128)(2,1)S(1)}, f32[128,1152]{1,0:T(8,128)S(1)}, bf16[128,1152]{1,0:T(8,128)(2,1)S(1)}) custom-call(s32[2]{0:T(128)S(1)} %pad_add_fusion.place, bf16[32,1920]{1,0:T(8,128)(2,1)S(1)} %shard_map.89.refs_0_, bf16[32,1920]{1,0:T(8,128)(2,1)S(1)} %collective-permute-done.9.refs_1_, ...), custom_call_target="tpu_custom_call" | custom-call | flops 1006632960 | bytes 5144576 | tf_op jit(solution)/shard_map/pallas_call | solution.py:36
  76.7 8.5 %collective-permute-start.16 = (bf16[128,1152]{1,0:T(8,128)(2,1)S(1)}, bf16[128,1152]{1,0:T(8,128)(2,1)S(1)}, u32[]{:S(2)}, u32[]{:S(2)}) collective-permute-start(bf16[128,1152]{1,0:T(8,128)(2,1)S(1)} %get-tuple-element.32), channel_id=1, source_target_pairs={{0,16},{16,0},{1,17},{17,1},{2,18},{18,2},{3,19},{19,3},{4,20},{20... | collective-permute-start | bytes 884744 | tf_op jit(solution)/shard_map/ppermute | solution.py:49
  85.2 1.2 collective-permute-done.16.other
  86.4 0.6 shard_map.91
  87.0 16.5 %all_to_all.26 = bf16[16,16,1152]{2,1,0:T(8,128)(2,1)S(1)} all-to-all(bf16[16,16,1152]{2,1,0:T(8,128)(2,1)S(1)} %bitcast.30), channel_id=1, replica_groups=mesh['x'=4,'yl'=2,'core'=2,'pipe'=2,'z'=8] {'x','yl','pipe'}, dimensions={0} | all-to-all | bytes 1179648 | tf_op jit(solution)/shard_map/all_to_all | solution.py:283
  103.5 0.6 shard_map.92
  104.1 8.5 %all_to_all.27 = bf16[8,16,1024]{2,1,0:T(8,128)(2,1)S(1)} all-to-all(bf16[8,16,1024]{2,1,0:T(8,128)(2,1)S(1)} %get-tuple-element.33), channel_id=1, replica_groups=mesh['x'=4,'yl'=2,'core'=2,'pipe'=2,'z'=8] {'x','yl'}, dimensions={0} | all-to-all | bytes 524288 | tf_op jit(solution)/shard_map/all_to_all | solution.py:252
  112.5 2.8 %collective-permute-start.17 = (bf16[128,1024]{1,0:T(8,128)(2,1)S(1)}, bf16[128,1024]{1,0:T(8,128)(2,1)S(1)}, u32[]{:S(2)}, u32[]{:S(2)}) collective-permute-start(bf16[128,1024]{1,0:T(8,128)(2,1)S(1)} %bitcast.35), channel_id=1, source_target_pairs={{0,16},{16,0},{1,17},{17,1},{2,18},{18,2},{3,19},{19,3},{4,20},{20... | collective-permute-start | bytes 786440 | tf_op jit(solution)/shard_map/ppermute | solution.py:49
  115.3 1.2 collective-permute-done.17.upper_other
  116.5 0.7 convolution_convert_fusion
  117.2 20.7 %all_to_all.28 = bf16[8,32,896]{2,1,0:T(8,128)(2,1)} all-to-all(bf16[8,32,896]{2,1,0:T(8,128)(2,1)S(1)} %bitcast.41), channel_id=1, replica_groups=mesh['x'=4,'yl'=2,'core'=2,'pipe'=2,'z'=8] {'z'}, dimensions={0} | all-to-all | bytes 917504 | tf_op jit(solution)/shard_map/all_to_all | solution.py:291
  137.9 1.1 reduce_sum.12.refs_0_
  139.1 1.5 collective-permute-start.22
  140.6 1.6 collective-permute-done.18.refs_1_
  142.1 1.2 collective-permute-start.19
  143.4 0.1 collective-permute-done.22.refs_7_
  143.4 0.2 collective-permute-start.23
  143.6 1.9 %collective-permute-done.19.refs_2_ = bf16[32,896]{1,0:T(8,128)(2,1)S(1)} collective-permute-done((bf16[32,896]{1,0:T(8,128)(2,1)S(1)}, bf16[32,896]{1,0:T(8,128)(2,1)S(1)}, u32[]{:S(2)}, u32[]{:S(2)}) %collective-permute-start.19) | collective-permute-done | bytes 57376 | tf_op jit(solution)/shard_map/ppermute | solution.py:54
  145.5 2.1 %collective-permute-start.20 = (bf16[32,896]{1,0:T(8,128)(2,1)S(1)}, bf16[32,896]{1,0:T(8,128)(2,1)S(1)}, u32[]{:S(2)}, u32[]{:S(2)}) collective-permute-start(bf16[32,896]{1,0:T(8,128)(2,1)S(1)} %collective-permute-done.19.refs_2_), channel_id=1, source_target_pairs={{0,7},{1,0},{2,1},{3,2},{4,3},{5,4},{6,5},{7,6},{8,15},{9,8},{10,9... | collective-permute-start | bytes 172040 | tf_op jit(solution)/shard_map/ppermute | solution.py:54
  147.6 0.1 collective-permute-done.23.refs_6_
  147.7 1.6 collective-permute-done.20.refs_3_
  149.3 2.5 %collective-permute-start.21 = (bf16[32,896]{1,0:T(8,128)(2,1)S(1)}, bf16[32,896]{1,0:T(8,128)(2,1)S(1)}, u32[]{:S(2)}, u32[]{:S(2)}) collective-permute-start(bf16[32,896]{1,0:T(8,128)(2,1)S(1)} %collective-permute-done.20.refs_3_), channel_id=1, source_target_pairs={{0,7},{1,0},{2,1},{3,2},{4,3},{5,4},{6,5},{7,6},{8,15},{9,8},{10,9... | collective-permute-start | bytes 172040 | tf_op jit(solution)/shard_map/ppermute | solution.py:54
  151.8 0.1 collective-permute-done.24.refs_5_
  151.9 1.6 collective-permute-done.21.refs_4_
  153.5 2.0 %copy-done.1 = bf16[128,8,2,896]{3,1,2,0:T(8,128)(2,1)S(1)} copy-done((bf16[128,8,2,896]{3,1,2,0:T(8,128)(2,1)S(1)}, bf16[128,8,2,896]{3,1,2,0:T(8,128)(2,1)}, u32[]{:S(2)}) %copy-start.1) | copy-done | bytes 3670040
  155.6 2.7 %shard_map.93 = (bf16[256,1792]{1,0:T(8,128)(2,1)S(1)}, f32[128,1152]{1,0:T(8,128)S(1)}, bf16[128,1152]{1,0:T(8,128)(2,1)S(1)}) custom-call(s32[2]{0:T(128)S(1)} %pad_add_fusion.place, bf16[32,896]{1,0:T(8,128)(2,1)S(1)} %reduce_sum.12.refs_0_, bf16[32,896]{1,0:T(8,128)(2,1)S(1)} %collective-permute-done.18.refs_1_, ...), custom_call_target="tpu_custom_call" | custom-call | flops 1006632960 | bytes 5603328 | tf_op jit(solution)/shard_map/pallas_call | solution.py:36
  158.3 6.1 %collective-permute-start.25 = (bf16[128,1152]{1,0:T(8,128)(2,1)S(1)}, bf16[128,1152]{1,0:T(8,128)(2,1)S(1)}, u32[]{:S(2)}, u32[]{:S(2)}) collective-permute-start(bf16[128,1152]{1,0:T(8,128)(2,1)S(1)} %get-tuple-element.36), channel_id=1, source_target_pairs={{0,16},{16,0},{1,17},{17,1},{2,18},{18,2},{3,19},{19,3},{4,20},{20... | collective-permute-start | bytes 884744 | tf_op jit(solution)/shard_map/ppermute | solution.py:49
  164.3 1.2 collective-permute-done.25.other
  165.5 0.6 shard_map.94
  166.2 11.2 %all_to_all.29.got = bf16[8,16,2048]{2,1,0:T(8,128)(2,1)S(1)} all-to-all(bf16[8,16,2048]{2,1,0:T(8,128)(2,1)S(1)} %shard_map.94), channel_id=1, replica_groups=mesh['x'=4,'yl'=2,'core'=2,'pipe'=2,'z'=8] {'x','yl'}, dimensions={0} | all-to-all | bytes 1048576 | tf_op jit(solution)/shard_map/all_to_all | solution.py:303
  177.4 1.2 shard_map.95
  178.6 2.1 %collective-permute-start.26 = (bf16[128,128]{1,0:T(8,128)(2,1)S(1)}, bf16[128,128]{1,0:T(8,128)(2,1)S(1)}, u32[]{:S(2)}, u32[]{:S(2)}) collective-permute-start(bf16[128,128]{1,0:T(8,128)(2,1)S(1)} %get-tuple-element.39.lower_mine), channel_id=1, source_target_pairs={{0,16},{16,0},{1,17},{17,1},{2,18},{18,2},{3,19},{19,3},{4,20},{20... | collective-permute-start | bytes 98312 | tf_op jit(solution)/shard_map/ppermute | solution.py:49
  180.7 1.7 shard_map.97
  182.3 1.7 shard_map.96
  (24 shorter events, 0.3 us)
Async XLA Ops:
  15.7 5.0 %collective-permute-start = (bf16[128,2048]{1,0:T(8,128)(2,1)S(1)}, bf16[128,2048]{1,0:T(8,128)(2,1)S(1)}, u32[]{:S(2)}, u32[]{:S(2)}) collective-permute-start(bf16[128,2048]{1,0:T(8,128)(2,1)S(1)} %bitcast.23), channel_id=1, source_target_pairs={{0,16},{16,0},{1,17},{17,1},{2,18},{18,2},{3,19},{19,3},{4,20},{20... | collective-permute-start | bytes 1572872 | tf_op jit(solution)/shard_map/ppermute | solution.py:49
  17.8 3.0 %copy-start.2 = (bf16[1,1024,128]{2,1,0:T(8,128)(2,1)S(1)}, bf16[1,1024,128]{2,1,0:T(8,128)(2,1)}, u32[]{:S(2)}) copy-start(bf16[1,1024,128]{2,1,0:T(8,128)(2,1)} %param.10) | copy-start | bytes 786436
  17.8 3.0 %copy-start.3 = (bf16[1,2,64,896]{3,2,1,0:T(8,128)(2,1)S(1)}, bf16[1,2,64,896]{3,2,1,0:T(8,128)(2,1)}, u32[]{:S(2)}) copy-start(bf16[1,2,64,896]{3,2,1,0:T(8,128)(2,1)} %param.11) | copy-start | bytes 688132
  17.8 3.0 %copy-start.4 = (bf16[1,896,1024]{2,1,0:T(8,128)(2,1)S(1)}, bf16[1,896,1024]{2,1,0:T(8,128)(2,1)}, u32[]{:S(2)}) copy-start(bf16[1,896,1024]{2,1,0:T(8,128)(2,1)} %param.9) | copy-start | bytes 5505028
  20.7 53.8 %copy-start = (bf16[128,8,2,896]{3,1,2,0:T(8,128)(2,1)}, bf16[128,8,2,896]{3,1,2,0:T(8,128)(2,1)S(1)}, u32[]{:S(2)}) copy-start(bf16[128,8,2,896]{3,1,2,0:T(8,128)(2,1)S(1)} %copy.9) | copy-start | bytes 11010052
  23.6 8.6 %collective-permute-start.1 = (bf16[32,1408]{1,0:T(8,128)(2,1)S(1)}, bf16[32,1408]{1,0:T(8,128)(2,1)S(1)}, u32[]{:S(2)}, u32[]{:S(2)}) collective-permute-start(bf16[32,1408]{1,0:T(8,128)(2,1)S(1)} %get-tuple-element.22), channel_id=1, source_target_pairs={{0,1},{1,2},{2,3},{3,4},{4,5},{5,6},{6,7},{7,0},{8,9},{9,10},{10,1... | collective-permute-start | bytes 270344 | tf_op jit(solution)/shard_map/ppermute | solution.py:54
  25.3 6.9 %collective-permute-start.2 = (bf16[32,1408]{1,0:T(8,128)(2,1)S(1)}, bf16[32,1408]{1,0:T(8,128)(2,1)S(1)}, u32[]{:S(2)}, u32[]{:S(2)}) collective-permute-start(bf16[32,1408]{1,0:T(8,128)(2,1)S(1)} %get-tuple-element.23), channel_id=1, source_target_pairs={{0,7},{1,0},{2,1},{3,2},{4,3},{5,4},{6,5},{7,6},{8,15},{9,8},{10,9... | collective-permute-start | bytes 270344 | tf_op jit(solution)/shard_map/ppermute | solution.py:54
  32.9 6.8 %collective-permute-start.3 = (bf16[32,2816]{1,0:T(8,128)(2,1)S(1)}, bf16[32,2816]{1,0:T(8,128)(2,1)S(1)}, u32[]{:S(2)}, u32[]{:S(2)}) collective-permute-start(bf16[32,2816]{1,0:T(8,128)(2,1)S(1)} %get-tuple-element.25), channel_id=1, source_target_pairs={{0,1},{1,2},{2,3},{3,4},{4,5},{5,6},{6,7},{7,0},{8,9},{9,10},{10,1... | collective-permute-start | bytes 540680 | tf_op jit(solution)/shard_map/ppermute | solution.py:54
  32.9 6.7 %collective-permute-start.4 = (bf16[32,2816]{1,0:T(8,128)(2,1)S(1)}, bf16[32,2816]{1,0:T(8,128)(2,1)S(1)}, u32[]{:S(2)}, u32[]{:S(2)}) collective-permute-start(bf16[32,2816]{1,0:T(8,128)(2,1)S(1)} %get-tuple-element.26), channel_id=1, source_target_pairs={{0,7},{1,0},{2,1},{3,2},{4,3},{5,4},{6,5},{7,6},{8,15},{9,8},{10,9... | collective-permute-start | bytes 540680 | tf_op jit(solution)/shard_map/ppermute | solution.py:54
  40.3 5.6 %collective-permute-start.5 = (bf16[32,2816]{1,0:T(8,128)(2,1)S(1)}, bf16[32,2816]{1,0:T(8,128)(2,1)S(1)}, u32[]{:S(2)}, u32[]{:S(2)}) collective-permute-start(bf16[32,2816]{1,0:T(8,128)(2,1)S(1)} %get-tuple-element.27), channel_id=1, source_target_pairs={{0,1},{1,2},{2,3},{3,4},{4,5},{5,6},{6,7},{7,0},{8,9},{9,10},{10,1... | collective-permute-start | bytes 540680 | tf_op jit(solution)/shard_map/ppermute | solution.py:54
  41.5 4.5 %collective-permute-start.6 = (bf16[32,2816]{1,0:T(8,128)(2,1)S(1)}, bf16[32,2816]{1,0:T(8,128)(2,1)S(1)}, u32[]{:S(2)}, u32[]{:S(2)}) collective-permute-start(bf16[32,2816]{1,0:T(8,128)(2,1)S(1)} %get-tuple-element.28), channel_id=1, source_target_pairs={{0,7},{1,0},{2,1},{3,2},{4,3},{5,4},{6,5},{7,6},{8,15},{9,8},{10,9... | collective-permute-start | bytes 540680 | tf_op jit(solution)/shard_map/ppermute | solution.py:54
  46.6 5.6 %collective-permute-start.7 = (bf16[32,2816]{1,0:T(8,128)(2,1)S(1)}, bf16[32,2816]{1,0:T(8,128)(2,1)S(1)}, u32[]{:S(2)}, u32[]{:S(2)}) collective-permute-start(bf16[32,2816]{1,0:T(8,128)(2,1)S(1)} %get-tuple-element.29), channel_id=1, source_target_pairs={{0,1},{1,2},{2,3},{3,4},{4,5},{5,6},{6,7},{7,0},{8,9},{9,10},{10,1... | collective-permute-start | bytes 540680 | tf_op jit(solution)/shard_map/ppermute | solution.py:54
  48.4 4.3 %collective-permute-start.8 = (bf16[32,2816]{1,0:T(8,128)(2,1)S(1)}, bf16[32,2816]{1,0:T(8,128)(2,1)S(1)}, u32[]{:S(2)}, u32[]{:S(2)}) collective-permute-start(bf16[32,2816]{1,0:T(8,128)(2,1)S(1)} %get-tuple-element.30), channel_id=1, source_target_pairs={{0,7},{1,0},{2,1},{3,2},{4,3},{5,4},{6,5},{7,6},{8,15},{9,8},{10,9... | collective-permute-start | bytes 540680 | tf_op jit(solution)/shard_map/ppermute | solution.py:54
  53.4 4.4 %collective-permute-start.9 = (bf16[32,1920]{1,0:T(8,128)(2,1)S(1)}, bf16[32,1920]{1,0:T(8,128)(2,1)S(1)}, u32[]{:S(2)}, u32[]{:S(2)}) collective-permute-start(bf16[32,1920]{1,0:T(8,128)(2,1)S(1)} %shard_map.89.refs_0_), channel_id=1, source_target_pairs={{0,7},{1,0},{2,1},{3,2},{4,3},{5,4},{6,5},{7,6},{8,15},{9,8},{10,9... | collective-permute-start | bytes 368648 | tf_op jit(solution)/shard_map/ppermute | solution.py:54
  55.7 4.9 %collective-permute-start.13 = (bf16[32,1920]{1,0:T(8,128)(2,1)S(1)}, bf16[32,1920]{1,0:T(8,128)(2,1)S(1)}, u32[]{:S(2)}, u32[]{:S(2)}) collective-permute-start(bf16[32,1920]{1,0:T(8,128)(2,1)S(1)} %shard_map.89.refs_0_), channel_id=1, source_target_pairs={{0,1},{1,2},{2,3},{3,4},{4,5},{5,6},{6,7},{7,0},{8,9},{9,10},{10,1... | collective-permute-start | bytes 368648 | tf_op jit(solution)/shard_map/ppermute | solution.py:54
  57.8 5.8 %collective-permute-start.10 = (bf16[32,1920]{1,0:T(8,128)(2,1)S(1)}, bf16[32,1920]{1,0:T(8,128)(2,1)S(1)}, u32[]{:S(2)}, u32[]{:S(2)}) collective-permute-start(bf16[32,1920]{1,0:T(8,128)(2,1)S(1)} %collective-permute-done.9.refs_1_), channel_id=1, source_target_pairs={{0,7},{1,0},{2,1},{3,2},{4,3},{5,4},{6,5},{7,6},{8,15},{9,8},{10,9... | collective-permute-start | bytes 368648 | tf_op jit(solution)/shard_map/ppermute | solution.py:54
  60.7 6.4 %collective-permute-start.14 = (bf16[32,1920]{1,0:T(8,128)(2,1)S(1)}, bf16[32,1920]{1,0:T(8,128)(2,1)S(1)}, u32[]{:S(2)}, u32[]{:S(2)}) collective-permute-start(bf16[32,1920]{1,0:T(8,128)(2,1)S(1)} %collective-permute-done.13.refs_7_), channel_id=1, source_target_pairs={{0,1},{1,2},{2,3},{3,4},{4,5},{5,6},{6,7},{7,0},{8,9},{9,10},{10,1... | collective-permute-start | bytes 368648 | tf_op jit(solution)/shard_map/ppermute | solution.py:54
  63.6 5.5 %collective-permute-start.11 = (bf16[32,1920]{1,0:T(8,128)(2,1)S(1)}, bf16[32,1920]{1,0:T(8,128)(2,1)S(1)}, u32[]{:S(2)}, u32[]{:S(2)}) collective-permute-start(bf16[32,1920]{1,0:T(8,128)(2,1)S(1)} %collective-permute-done.10.refs_2_), channel_id=1, source_target_pairs={{0,7},{1,0},{2,1},{3,2},{4,3},{5,4},{6,5},{7,6},{8,15},{9,8},{10,9... | collective-permute-start | bytes 368648 | tf_op jit(solution)/shard_map/ppermute | solution.py:54
  67.1 5.5 %collective-permute-start.15 = (bf16[32,1920]{1,0:T(8,128)(2,1)S(1)}, bf16[32,1920]{1,0:T(8,128)(2,1)S(1)}, u32[]{:S(2)}, u32[]{:S(2)}) collective-permute-start(bf16[32,1920]{1,0:T(8,128)(2,1)S(1)} %collective-permute-done.14.refs_6_), channel_id=1, source_target_pairs={{0,1},{1,2},{2,3},{3,4},{4,5},{5,6},{6,7},{7,0},{8,9},{9,10},{10,1... | collective-permute-start | bytes 368648 | tf_op jit(solution)/shard_map/ppermute | solution.py:54
  69.2 5.3 %collective-permute-start.12 = (bf16[32,1920]{1,0:T(8,128)(2,1)S(1)}, bf16[32,1920]{1,0:T(8,128)(2,1)S(1)}, u32[]{:S(2)}, u32[]{:S(2)}) collective-permute-start(bf16[32,1920]{1,0:T(8,128)(2,1)S(1)} %collective-permute-done.11.refs_3_), channel_id=1, source_target_pairs={{0,7},{1,0},{2,1},{3,2},{4,3},{5,4},{6,5},{7,6},{8,15},{9,8},{10,9... | collective-permute-start | bytes 368648 | tf_op jit(solution)/shard_map/ppermute | solution.py:54
  76.7 9.7 %collective-permute-start.16 = (bf16[128,1152]{1,0:T(8,128)(2,1)S(1)}, bf16[128,1152]{1,0:T(8,128)(2,1)S(1)}, u32[]{:S(2)}, u32[]{:S(2)}) collective-permute-start(bf16[128,1152]{1,0:T(8,128)(2,1)S(1)} %get-tuple-element.32), channel_id=1, source_target_pairs={{0,16},{16,0},{1,17},{17,1},{2,18},{18,2},{3,19},{19,3},{4,20},{20... | collective-permute-start | bytes 884744 | tf_op jit(solution)/shard_map/ppermute | solution.py:49
  112.5 3.9 %collective-permute-start.17 = (bf16[128,1024]{1,0:T(8,128)(2,1)S(1)}, bf16[128,1024]{1,0:T(8,128)(2,1)S(1)}, u32[]{:S(2)}, u32[]{:S(2)}) collective-permute-start(bf16[128,1024]{1,0:T(8,128)(2,1)S(1)} %bitcast.35), channel_id=1, source_target_pairs={{0,16},{16,0},{1,17},{17,1},{2,18},{18,2},{3,19},{19,3},{4,20},{20... | collective-permute-start | bytes 786440 | tf_op jit(solution)/shard_map/ppermute | solution.py:49
  139.0 3.1 %collective-permute-start.18 = (bf16[32,896]{1,0:T(8,128)(2,1)S(1)}, bf16[32,896]{1,0:T(8,128)(2,1)S(1)}, u32[]{:S(2)}, u32[]{:S(2)}) collective-permute-start(bf16[32,896]{1,0:T(8,128)(2,1)S(1)} %reduce_sum.12.refs_0_), channel_id=1, source_target_pairs={{0,7},{1,0},{2,1},{3,2},{4,3},{5,4},{6,5},{7,6},{8,15},{9,8},{10,9... | collective-permute-start | bytes 172040 | tf_op jit(solution)/shard_map/ppermute | solution.py:54
  139.1 4.3 %collective-permute-start.22 = (bf16[32,896]{1,0:T(8,128)(2,1)S(1)}, bf16[32,896]{1,0:T(8,128)(2,1)S(1)}, u32[]{:S(2)}, u32[]{:S(2)}) collective-permute-start(bf16[32,896]{1,0:T(8,128)(2,1)S(1)} %reduce_sum.12.refs_0_), channel_id=1, source_target_pairs={{0,1},{1,2},{2,3},{3,4},{4,5},{5,6},{6,7},{7,0},{8,9},{9,10},{10,1... | collective-permute-start | bytes 172040 | tf_op jit(solution)/shard_map/ppermute | solution.py:54
  142.1 3.3 %collective-permute-start.19 = (bf16[32,896]{1,0:T(8,128)(2,1)S(1)}, bf16[32,896]{1,0:T(8,128)(2,1)S(1)}, u32[]{:S(2)}, u32[]{:S(2)}) collective-permute-start(bf16[32,896]{1,0:T(8,128)(2,1)S(1)} %collective-permute-done.18.refs_1_), channel_id=1, source_target_pairs={{0,7},{1,0},{2,1},{3,2},{4,3},{5,4},{6,5},{7,6},{8,15},{9,8},{10,9... | collective-permute-start | bytes 172040 | tf_op jit(solution)/shard_map/ppermute | solution.py:54
  143.4 4.2 %collective-permute-start.23 = (bf16[32,896]{1,0:T(8,128)(2,1)S(1)}, bf16[32,896]{1,0:T(8,128)(2,1)S(1)}, u32[]{:S(2)}, u32[]{:S(2)}) collective-permute-start(bf16[32,896]{1,0:T(8,128)(2,1)S(1)} %collective-permute-done.22.refs_7_), channel_id=1, source_target_pairs={{0,1},{1,2},{2,3},{3,4},{4,5},{5,6},{6,7},{7,0},{8,9},{9,10},{10,1... | collective-permute-start | bytes 172040 | tf_op jit(solution)/shard_map/ppermute | solution.py:54
  145.5 3.8 %collective-permute-start.20 = (bf16[32,896]{1,0:T(8,128)(2,1)S(1)}, bf16[32,896]{1,0:T(8,128)(2,1)S(1)}, u32[]{:S(2)}, u32[]{:S(2)}) collective-permute-start(bf16[32,896]{1,0:T(8,128)(2,1)S(1)} %collective-permute-done.19.refs_2_), channel_id=1, source_target_pairs={{0,7},{1,0},{2,1},{3,2},{4,3},{5,4},{6,5},{7,6},{8,15},{9,8},{10,9... | collective-permute-start | bytes 172040 | tf_op jit(solution)/shard_map/ppermute | solution.py:54
  147.7 4.2 %collective-permute-start.24 = (bf16[32,896]{1,0:T(8,128)(2,1)S(1)}, bf16[32,896]{1,0:T(8,128)(2,1)S(1)}, u32[]{:S(2)}, u32[]{:S(2)}) collective-permute-start(bf16[32,896]{1,0:T(8,128)(2,1)S(1)} %collective-permute-done.23.refs_6_), channel_id=1, source_target_pairs={{0,1},{1,2},{2,3},{3,4},{4,5},{5,6},{6,7},{7,0},{8,9},{9,10},{10,1... | collective-permute-start | bytes 172040 | tf_op jit(solution)/shard_map/ppermute | solution.py:54
  149.3 4.2 %collective-permute-start.21 = (bf16[32,896]{1,0:T(8,128)(2,1)S(1)}, bf16[32,896]{1,0:T(8,128)(2,1)S(1)}, u32[]{:S(2)}, u32[]{:S(2)}) collective-permute-start(bf16[32,896]{1,0:T(8,128)(2,1)S(1)} %collective-permute-done.20.refs_3_), channel_id=1, source_target_pairs={{0,7},{1,0},{2,1},{3,2},{4,3},{5,4},{6,5},{7,6},{8,15},{9,8},{10,9... | collective-permute-start | bytes 172040 | tf_op jit(solution)/shard_map/ppermute | solution.py:54
  153.5 2.0 %copy-start.1 = (bf16[128,8,2,896]{3,1,2,0:T(8,128)(2,1)S(1)}, bf16[128,8,2,896]{3,1,2,0:T(8,128)(2,1)}, u32[]{:S(2)}) copy-start(bf16[128,8,2,896]{3,1,2,0:T(8,128)(2,1)} %copy-done) | copy-start | bytes 11010052
  158.3 7.3 %collective-permute-start.25 = (bf16[128,1152]{1,0:T(8,128)(2,1)S(1)}, bf16[128,1152]{1,0:T(8,128)(2,1)S(1)}, u32[]{:S(2)}, u32[]{:S(2)}) collective-permute-start(bf16[128,1152]{1,0:T(8,128)(2,1)S(1)} %get-tuple-element.36), channel_id=1, source_target_pairs={{0,16},{16,0},{1,17},{17,1},{2,18},{18,2},{3,19},{19,3},{4,20},{20... | collective-permute-start | bytes 884744 | tf_op jit(solution)/shard_map/ppermute | solution.py:49
  178.6 3.7 %collective-permute-start.26 = (bf16[128,128]{1,0:T(8,128)(2,1)S(1)}, bf16[128,128]{1,0:T(8,128)(2,1)S(1)}, u32[]{:S(2)}, u32[]{:S(2)}) collective-permute-start(bf16[128,128]{1,0:T(8,128)(2,1)S(1)} %get-tuple-element.39.lower_mine), channel_id=1, source_target_pairs={{0,16},{16,0},{1,17},{17,1},{2,18},{18,2},{3,19},{19,3},{4,20},{20... | collective-permute-start | bytes 98312 | tf_op jit(solution)/shard_map/ppermute | solution.py:49

commit v4 on v3

v4 whole, which is shorter than its diff:
```python
import functools
import math

import jax
import jax.numpy as jnp
from jax import lax
from jax.experimental import pallas as pl
from jax.experimental.pallas import tpu as pltpu
from jax.sharding import Mesh, PartitionSpec as P

adapter_scale = 2.0
CHIPS = ("x", "yl")
F32 = jnp.float32
BF16 = jnp.bfloat16
VMEM_LIMIT = 16 * 2**20


def dot_nn(a, b):
    return jnp.dot(a, b, preferred_element_type=F32)


def dot_nt(a, b):
    return lax.dot_general(a, b, (((1,), (1,)), ((), ())), preferred_element_type=F32)


def dot_tn(a, b):
    return lax.dot_general(a, b, (((0,), (0,)), ((), ())), preferred_element_type=F32)


def kept(shape, dtype=BF16):
    return pltpu.VMEM(shape, dtype)


def call(kernel, outs, *args, scratch=(), flops=0, pin=True):
    size = sum(a.size * a.dtype.itemsize for a in args)
    return pl.pallas_call(
        kernel,
        out_shape=outs,
        in_specs=[pl.BlockSpec(memory_space=pltpu.VMEM)] * len(args),
        out_specs=jax.tree.map(lambda _: pl.BlockSpec(memory_space=pltpu.VMEM), outs),
        scratch_shapes=list(scratch),
        compiler_params=pltpu.CompilerParams(vmem_limit_bytes=VMEM_LIMIT),
        cost_estimate=pl.CostEstimate(flops=flops, bytes_accessed=size, transcendentals=0),
    )(*[pltpu.with_memory_space_constraint(a, pltpu.VMEM) if pin else a for a in args])


def core_swap(block):
    return lax.ppermute(block, "core", [(0, 1), (1, 0)])


def ring(block, step):
    n = lax.axis_size("z")
    return lax.ppermute(block, "z", [(i, (i + step) % n) for i in range(n)])


def swiglu_back(gate, up, hidden):
    sig = 1.0 / (1.0 + jnp.exp(-gate))
    gate_grad = hidden * up * sig * (1.0 + gate * (1.0 - sig))
    up_grad = hidden * gate * sig
    return gate_grad.astype(BF16), up_grad.astype(BF16)


def tiles(width, most=512):
    return [(lo, min(most, width - lo)) for lo in range(0, width, most)]


def forward_columns(x, g, weight, down, first, second, put):
    hidden, rank = second.shape[2], second.shape[1]
    low = dot_nn(x, first[...]).astype(BF16)
    put(2 * hidden, low)
    for k in range(2):
        for lo, size in tiles(hidden):
            at = k * hidden + lo
            pre = dot_nn(x, weight[:, at:at + size])
            pre += adapter_scale * dot_nn(low[:, k * rank:(k + 1) * rank], second[k, :, lo:lo + size])
            put(at, pre.astype(BF16))
    for lo, size in tiles(hidden):
        put(2 * hidden + 2 * rank + lo, dot_nt(g, down[lo:lo + size, :]).astype(BF16))


def first_kernel(mine, other, weight, down, first, second, up, back):
    rows, width = up.shape
    feat = first.shape[0]
    blocks = mine.shape[0] // rows
    far = lax.rem(lax.axis_index("z") + blocks, 2 * blocks)
    at = pl.multiple_of(lax.rem(far, blocks) * rows, rows)
    both = jnp.where(far < blocks, mine[pl.ds(at, rows), :], other[pl.ds(at, rows), :])

    def put(lo, value):
        size = value.shape[1]
        cut = min(max(width - lo, 0), size)
        if cut > 0:
            up[:, lo:lo + cut] = value[:, :cut]
        if cut < size:
            back[:, lo + cut - width:lo + size - width] = value[:, cut:]

    forward_columns(both[:, :feat], both[:, feat:], weight, down, first, second, put)


def forward_kernel(mine, other, weight, down, first, second, parts):
    n, rows, _ = parts.shape
    feat = first.shape[0]

    def put(lo, value):
        parts[:, :, lo:lo + value.shape[1]] = value.reshape(n, rows, value.shape[1])

    x = jnp.concatenate([mine[:, :feat], other[:, :feat]], axis=0)
    g = jnp.concatenate([mine[:, feat:], other[:, feat:]], axis=0)
    forward_columns(x, g, weight, down, first, second, put)


def ring_add_kernel(step, moving, parts, out):
    n, _, width = parts.shape
    size = moving.shape[1]
    part = lax.rem(lax.axis_index("z") + n + step, n)
    lo = 0 if step > 0 else width - size
    out[:, lo:lo + size] = (moving[...].astype(F32) + parts[part, :, lo:lo + size].astype(F32)).astype(BF16)
    if size < width:
        rest = width - size - lo
        out[:, rest:rest + width - size] = parts[part, :, rest:rest + width - size]


def middle_kernel(up_in, back_in, parts, sent):
    total = up_in[...].astype(F32) + back_in[...].astype(F32) + parts[lax.axis_index("z")].astype(F32)
    width = sent.shape[1]
    hidden = total.shape[1] - width
    gate, up = total[:, :hidden], total[:, hidden:2 * hidden]
    gate_grad, up_grad = swiglu_back(gate, up, total[:, width:])
    upper = lax.axis_index("pipe") == 1
    sent[:, :hidden] = jnp.where(upper, gate_grad, gate.astype(BF16))
    sent[:, hidden:2 * hidden] = jnp.where(upper, up_grad, up.astype(BF16))
    sent[:, 2 * hidden:] = total[:, 2 * hidden:width].astype(BF16)


def collect(pieces, whole):
    rows = pieces[0].shape[0]
    n = len(pieces) - 1
    far = n // 2
    for step, piece in enumerate(pieces):
        lo = pieces[far].shape[1] if step == far + 1 else 0
        distance = step if step <= far else step - 1
        at = pl.multiple_of(lax.rem(lax.axis_index("z") + distance, n) * rows, rows)
        whole[pl.ds(at, rows), lo:lo + piece.shape[1]] = piece[...]


def input_partials(act, weight, first, second, mine, other):
    feat = first.shape[0]
    hidden, rank = second.shape[2], second.shape[1]
    half = mine.shape[0]
    back = jnp.concatenate(
        [dot_nt(act[:, k * hidden:(k + 1) * hidden], second[k]) for k in range(2)], axis=1
    )
    mine[:, feat:] = back[:half]
    other[:, feat:] = back[half:].astype(BF16)
    scaled = (adapter_scale * back).astype(BF16)
    for lo, size in tiles(feat, 256):
        part = dot_nt(act[:, :2 * hidden], weight[lo:lo + size, :]) + dot_nt(scaled, first[lo:lo + size, :])
        mine[:, lo:lo + size] = part[:half]
        other[:, lo:lo + size] = part[half:].astype(BF16)


def backward_kernel(count, *refs):
    pieces = refs[:count]
    weight, first, second, whole, mine, other = refs[count:]
    collect(pieces, whole)
    input_partials(whole, weight, first, second, mine, other)


def lower_kernel(count, *refs):
    pieces = refs[:count]
    whole, weight, first, second, act, mine, other, hidden_grad = refs[count:]
    collect(pieces, hidden_grad)
    hidden = hidden_grad.shape[1]
    for lo, size in tiles(hidden, 128):
        gate_grad, up_grad = swiglu_back(
            whole[:, lo:lo + size].astype(F32),
            whole[:, hidden + lo:hidden + lo + size].astype(F32),
            hidden_grad[:, lo:lo + size].astype(F32),
        )
        act[:, lo:lo + size] = gate_grad
        act[:, hidden + lo:hidden + lo + size] = up_grad
    input_partials(act, weight, first, second, mine, other)


def spread_kernel(acts, grads, out):
    feat = acts.shape[1]
    for chip in range(out.shape[0]):
        out[chip, :, :feat] = acts[...]
        out[chip, :, feat:] = grads[...]


def add_cores_kernel(mine, other, out):
    out[...] = (mine[...] + other[...].astype(F32)).astype(BF16).reshape(out.shape)


def hand_kernel(got, out):
    total = jnp.sum(got[...].astype(F32), axis=0).astype(BF16)
    for section in range(out.shape[0]):
        for chip in range(out.shape[1]):
            out[section, chip] = total


def hidden_kernel(mine, other, down, *outs):
    *blocks, far_one, far_two, held = outs
    chips, own, feat = other.shape
    n, rows, _ = held.shape
    g = jnp.concatenate([mine[1, :, :, :feat], other[...]], axis=0).reshape(2 * chips * own, feat)
    held[...] = dot_nt(g, down[...]).astype(BF16).reshape(held.shape)
    for distance in range(n):
        block = held[lax.rem(lax.axis_index("z") + distance, n)]
        if distance == n // 2:
            cut = far_one.shape[1]
            far_one[...] = block[:, :cut]
            far_two[...] = block[:, cut:]
        else:
            blocks[distance if distance < n // 2 else distance - 1][...] = block


def pass_on_kernel(ahead, behind, three_up, three_back, far_up, far_back, up, back):
    cut = far_up.shape[1]
    total = ahead[...].astype(F32) + three_up[...].astype(F32)
    up[:, :cut] = (total[:, :cut] + far_up[...].astype(F32)).astype(BF16)
    up[:, cut:] = total[:, cut:].astype(BF16)
    total = behind[...].astype(F32) + three_back[...].astype(F32)
    back[:, :cut] = total[:, :cut].astype(BF16)
    back[:, cut:] = (total[:, cut:] + far_back[...].astype(F32)).astype(BF16)


def sum_z_kernel(*refs):
    *terms, out = refs
    total = terms[0][...].astype(F32)
    for term in terms[1:]:
        total += term[...].astype(F32)
    out[...] = total.astype(BF16)


def last_message_kernel(mine, other, out):
    total = (mine[...] + other[...].astype(F32)).astype(BF16)
    chips, rows, _ = out.shape
    wide = total.shape[1] - (out.shape[2] - total.shape[1]) // (chips - 1)
    rank = total.shape[1] - wide
    out[:, :, :wide] = total[:, :wide].reshape(chips, rows, wide)
    for chip in range(chips):
        block = total[chip * rows:(chip + 1) * rows, wide:]
        for target in range(chips):
            out[target, :, wide + chip * rank:wide + (chip + 1) * rank] = block


def last_sum_kernel(got, handed, grad, back):
    chips, rows, _ = got.shape
    feat, rank = grad.shape[1], back.shape[1]
    total = jnp.sum(got[...].astype(F32), axis=0).astype(BF16)
    upper = lax.axis_index("pipe") == 1
    grad[...] = jnp.where(upper, handed[1, lax.axis_index(CHIPS), :, :feat], total[:, :feat])
    for chip in range(chips):
        held = jnp.where(upper, handed[1, chip, :, feat:], total[:, feat + chip * rank:feat + (chip + 1) * rank])
        back[chip * rows:(chip + 1) * rows, :] = held


def grad_up_kernel(factor, whole, act, out):
    hidden, rank = out.shape[2], out.shape[1]
    for k in range(2):
        low = whole[:, 2 * hidden + k * rank:2 * hidden + (k + 1) * rank]
        for lo, size in tiles(hidden):
            at = k * hidden + lo
            used = jnp.where(lax.axis_index("pipe") == 1, whole[:, at:at + size], act[:, at:at + size])
            out[k, :, lo:lo + size] = dot_tn(low, used) * factor


def grad_down_kernel(inputs, back, out):
    for lo, size in tiles(out.shape[0], 256):
        out[lo:lo + size, :] = dot_tn(inputs[:, lo:lo + size], back[...])


def grad_down_end_kernel(factor, inputs, back, half, out):
    for lo, size in tiles(out.shape[0], 256):
        part = half[lo:lo + size, :] + dot_tn(inputs[:, lo:lo + size], back[...])
        out[lo:lo + size, :] = part * factor


def local(acts, output_gradient, gate_up_weight, down, adapter_first_weight, adapter_second_weight):
    micro, rows, feat = acts.shape[1:]
    hidden = down.shape[1]
    rank = adapter_second_weight.shape[2]
    own = micro * rows
    weight = gate_up_weight[0].reshape(feat, 2 * hidden)
    down_weight = down[0]
    first = adapter_first_weight[0]
    second = adapter_second_weight[0]
    chips = lax.axis_size(CHIPS)
    tokens = own * chips * lax.axis_size("core")
    half = tokens // 2
    n = lax.axis_size("z")
    block = tokens // n
    width = 2 * hidden + 2 * rank
    factor = adapter_scale / math.sqrt(tokens)

    def gather_z(piece):
        cut = piece.shape[1] // 256 * 128
        ahead_two, behind_two = ring(piece, -2), ring(piece, 2)
        ahead, behind = ring(piece, -1), ring(piece, 1)
        ahead_three, behind_three = ring(ahead_two, -1), ring(behind_two, 1)
        far = [ring(ahead_two[:, :cut], -2), ring(behind_two[:, cut:], 2)]
        return [piece, ahead, ahead_two, ahead_three] + far + [behind_three, behind_two, behind]

    message = call(
        spread_kernel, kept((chips, own, 2 * feat)),
        acts[0].reshape(own, feat), output_gradient.reshape(own, feat),
        pin=False,
    )
    mine = lax.all_to_all(message, CHIPS, 0, 0).reshape(half, 2 * feat)
    other = core_swap(mine)

    full = width + hidden
    up, back = call(
        first_kernel, (kept((block, full // 2)), kept((block, full // 2))),
        mine, other, weight, down_weight, first, second,
        flops=2 * block * feat * full,
    )
    parts = call(
        forward_kernel, kept((n, block, full)),
        mine, other, weight, down_weight, first, second,
        flops=2 * tokens * feat * full,
    )
    for step in range(n // 2 - 1, -1, -1):
        up, back = ring(up, 1), ring(back, -1)
        if step:
            up = call(functools.partial(ring_add_kernel, step), kept((block, full)), up, parts)
            back = call(functools.partial(ring_add_kernel, -step), kept((block, full)), back, parts)
    sent = call(middle_kernel, kept((block, width)), up, back, parts)
    whole, half_mine, half_other = call(
        functools.partial(backward_kernel, n + 1),
        (kept((tokens, width)), kept((half, feat + 2 * rank), F32), kept((half, feat + 2 * rank))),
        *gather_z(sent), weight, first, second,
        flops=2 * tokens * feat * width,
    )
    shape = (chips, own, feat + 2 * rank)
    message = call(add_cores_kernel, kept(shape), half_mine, core_swap(half_other))
    message = call(hand_kernel, kept((2,) + shape), lax.all_to_all(message, CHIPS, 0, 0))

    handed = lax.all_to_all(message.reshape((2 * chips,) + shape[1:]), ("pipe",) + CHIPS, 0, 0)
    handed = handed.reshape((2,) + shape)
    cut = hidden // 256 * 128
    zero, one, two, three, minus_three, minus_two, minus_one, far_one, far_two = call(
        hidden_kernel,
        (kept((block, hidden)),) * (n - 1) + (kept((block, cut)), kept((block, hidden - cut))),
        handed, core_swap(handed[1, :, :, :feat]), down_weight,
        scratch=[pltpu.VMEM((n, block, hidden), BF16)],
        flops=2 * tokens * feat * hidden,
    )
    up, back = call(
        pass_on_kernel, (kept((block, hidden)),) * 2,
        two, minus_two, ring(three, 1), ring(minus_three, -1), ring(far_one, 2), ring(far_two, -2),
    )
    message = call(
        sum_z_kernel, kept((block, hidden)),
        zero, ring(one, 1), ring(minus_one, -1), ring(up, 2), ring(back, -2),
    )
    act, half_mine, half_other = call(
        functools.partial(lower_kernel, n + 1),
        (kept((tokens, 2 * hidden)), kept((half, feat + 2 * rank), F32), kept((half, feat + 2 * rank))),
        *gather_z(message), whole, weight, first, second,
        scratch=[pltpu.VMEM((tokens, hidden), BF16)],
        flops=2 * tokens * feat * width,
    )
    grad_up = call(
        functools.partial(grad_up_kernel, factor),
        jax.ShapeDtypeStruct((2, rank, hidden), F32), whole, act,
        flops=4 * tokens * rank * hidden,
    )
    half_mine, grad_up = lax.optimization_barrier((half_mine, grad_up))
    message = call(
        last_message_kernel, kept((chips, own, feat + chips * 2 * rank)), half_mine, core_swap(half_other)
    )
    got = lax.all_to_all(message, CHIPS, 0, 0)
    grad_inputs, back_mine = call(
        last_sum_kernel,
        (jax.ShapeDtypeStruct((own, feat), BF16), kept((half, 2 * rank))), got, handed,
    )
    grad_down = call(
        grad_down_kernel, kept((feat, 2 * rank), F32), mine, back_mine,
        flops=2 * tokens * feat * rank,
    )
    grad_down = call(
        functools.partial(grad_down_end_kernel, factor),
        jax.ShapeDtypeStruct((feat, 2 * rank), F32), other, core_swap(back_mine), grad_down,
        flops=2 * tokens * feat * rank,
    )
    return grad_inputs.reshape(1, micro, rows, feat), grad_down[None], grad_up[None]


def solution(mesh):
    sizes = dict(mesh.shape)
    fine = Mesh(
        mesh.devices.reshape(sizes["dp"] // 4, 2, 2, sizes["pipe"], sizes["tensor"]),
        ("x", "yl", "core", "pipe", "z"),
    )
    dp = ("x", "yl", "core")
    in_specs = (
        P("pipe", None, dp, "z"),
        P(None, dp, "z"),
        P("pipe", "z", None, dp),
        P("pipe", dp, "z"),
        P("pipe", "z", None),
        P("pipe", None, None, dp),
    )
    out_specs = (
        P("pipe", None, dp, "z"),
        P("pipe", "z", None),
        P("pipe", None, None, dp),
    )
    return jax.shard_map(local, mesh=fine, in_specs=in_specs, out_specs=out_specs, check_vma=False)
```

time: 184 us -> 163 us (0.89)
  blocking collectives: 71.2 us -> 50.5 us
  starting transfers between devices: 55.1 us -> 69.7 us
  waiting for transfers between devices: 32.6 us -> 24.7 us
  Pallas kernels: 16.6 us -> 12 us
  other arithmetic: 1.95 us -> 0 us
    all_to_all x4 -> x3, blocking collectives: 59.9 us -> 38.8 us  [the longest x1 14.8 us: local(): lax.all_to_all(message.reshape((2 * chips,) + shape[1:]), ('pipe',) + CHI...]
    ppermute x22 -> x32, starting transfers between devices: 33.7 us -> 50.4 us  [ring(): return lax.ppermute(block, 'z', [(i, (i + step) % n) for i in range(n)])]
    ppermute x22 -> x32, waiting for transfers between devices: 29.1 us -> 21.6 us  [ring(): return lax.ppermute(block, 'z', [(i, (i + step) % n) for i in range(n)])]
    pallas_call x13 -> x22, Pallas kernels: 16.6 us -> 12 us  [call(): pl.pallas_call(kernel, out_shape=outs, in_specs=[pl.BlockSpec(memory_spac...]
    ppermute x5, starting transfers between devices: 21.4 us -> 19.3 us  [core_swap(): return lax.ppermute(block, 'core', [(0, 1), (1, 0)])]
  transfers between devices with their start and end apart: 27 -> 37, of which waited for: 19 -> 14; matrix products, arithmetic and copies ran while one was open for 2% -> 2% of each run, Pallas kernels for 1% -> 2%
where the time goes in v4:
time: 163 us; the launch traced here: 162 us
  starting transfers between devices  69.7 us (43%)
  blocking collectives  50.5 us (31%)
  waiting for transfers between devices  24.7 us (15%)
  Pallas kernels  12 us (7%)
  local copies, waits for them, and re-layouts  4.41 us (3%)
    ppermute x32, starting transfers between devices, ring(): return lax.ppermute(block, 'z', [(i, (i + step) % n) for i in range(n)])  50.4 us
    ppermute x32, waiting for transfers between devices, ring(): return lax.ppermute(block, 'z', [(i, (i + step) % n) for i in range(n)])  21.6 us
    ppermute x5, starting transfers between devices, core_swap(): return lax.ppermute(block, 'core', [(0, 1), (1, 0)])  19.3 us
    all_to_all x1, blocking collectives, local(): lax.all_to_all(message.reshape((2 * chips,) + shape[1:]), ('pipe',) + CHI...  14.8 us
    all_to_all x1, blocking collectives, local(): mine = lax.all_to_all(message, CHIPS, 0, 0).reshape(half, 2 * feat)  14.3 us
    pallas_call x22, Pallas kernels, call(): pl.pallas_call(kernel, out_shape=outs, in_specs=[pl.BlockSpec(memory_spac...  12 us
    all_to_all x1, blocking collectives, local(): got = lax.all_to_all(message, CHIPS, 0, 0)  11.8 us
    all_to_all x1, blocking collectives, local(): lax.all_to_all(message, CHIPS, 0, 0)  9.69 us
  transfers between devices with their start and end apart: 37, of which 14 were waited for; matrix products, arithmetic and copies ran while one was open for 2% of the time, Pallas kernels for 2%

profile of v4, /device:TPU:1, one launch (start us, length us, event | category | flops | bytes accessed | tf_op | source)
XLA Modules:
  0.0 162.3 jit_solution(826915384510377265)
XLA Ops:
  0.6 0.7 copy-done.3
  1.4 0.8 copy-done.4
  2.2 14.3 %all_to_all.20 = bf16[8,16,2048]{2,1,0:T(8,128)(2,1)S(1)} all-to-all(bf16[8,16,2048]{2,1,0:T(8,128)(2,1)S(1)} %shard_map.85), channel_id=1, replica_groups=mesh['x'=4,'yl'=2,'core'=2,'pipe'=2,'z'=8] {'x','yl'}, dimensions={0} | all-to-all | bytes 1048576 | tf_op jit(solution)/shard_map/all_to_all | solution.py:311
  16.5 2.1 %collective-permute-start = (bf16[128,2048]{1,0:T(8,128)(2,1)S(1)}, bf16[128,2048]{1,0:T(8,128)(2,1)S(1)}, u32[]{:S(2)}, u32[]{:S(2)}) collective-permute-start(bf16[128,2048]{1,0:T(8,128)(2,1)S(1)} %bitcast.23), channel_id=1, source_target_pairs={{0,16},{16,0},{1,17},{17,1},{2,18},{18,2},{3,19},{19,3},{4,20},{20... | collective-permute-start | bytes 1572872 | tf_op jit(solution)/shard_map/ppermute | solution.py:48
  18.5 2.9 %copy.9 = bf16[128,8,2,896]{3,1,2,0:T(8,128)(2,1)S(1)} copy(bf16[128,8,2,896]{3,2,1,0:T(2,128)(2,1)} %bitcast.41) | data formatting | bytes 7340032
  21.4 1.4 shard_map.86
  22.8 1.7 %collective-permute-start.1 = (bf16[32,1408]{1,0:T(8,128)(2,1)S(1)}, bf16[32,1408]{1,0:T(8,128)(2,1)S(1)}, u32[]{:S(2)}, u32[]{:S(2)}) collective-permute-start(bf16[32,1408]{1,0:T(8,128)(2,1)S(1)} %get-tuple-element.26), channel_id=1, source_target_pairs={{0,1},{1,2},{2,3},{3,4},{4,5},{5,6},{6,7},{7,0},{8,9},{9,10},{10,1... | collective-permute-start | bytes 270344 | tf_op jit(solution)/shard_map/ppermute | solution.py:53
  24.5 4.0 %collective-permute-start.5 = (bf16[32,1408]{1,0:T(8,128)(2,1)S(1)}, bf16[32,1408]{1,0:T(8,128)(2,1)S(1)}, u32[]{:S(2)}, u32[]{:S(2)}) collective-permute-start(bf16[32,1408]{1,0:T(8,128)(2,1)S(1)} %get-tuple-element.27), channel_id=1, source_target_pairs={{0,7},{1,0},{2,1},{3,2},{4,3},{5,4},{6,5},{7,6},{8,15},{9,8},{10,9... | collective-permute-start | bytes 270344 | tf_op jit(solution)/shard_map/ppermute | solution.py:53
  28.5 2.3 %shard_map.87.parts = bf16[8,32,2816]{2,1,0:T(8,128)(2,1)S(1)} custom-call(bf16[128,2048]{1,0:T(8,128)(2,1)S(1)} %bitcast.25, bf16[128,2048]{1,0:T(8,128)(2,1)S(1)} %collective-permute-done.other.inputs, bf16[1024,1792]{1,0:T(8,128)(2,1)S(1)} %bitcast.17, bf16[896,1024]{1,0:T(8,128)(2,1)S(1)} %bitcast.21, bf16[1024,128]{1,0:T(8,128)(2,1)S(1)} %bitcast.31, ...), custom_call_target="tpu_custom_call" | custom-call | flops 1476395008 | bytes 7045120 | tf_op jit(solution)/shard_map/pallas_call | solution.py:36
  30.8 0.6 collective-permute-done.1.moving
  31.5 0.1 collective-permute-start.2
  31.6 2.7 %collective-permute-start.6 = (bf16[32,2816]{1,0:T(8,128)(2,1)S(1)}, bf16[32,2816]{1,0:T(8,128)(2,1)S(1)}, u32[]{:S(2)}, u32[]{:S(2)}) collective-permute-start(bf16[32,2816]{1,0:T(8,128)(2,1)S(1)} %shard_map.91), channel_id=1, source_target_pairs={{0,7},{1,0},{2,1},{3,2},{4,3},{5,4},{6,5},{7,6},{8,15},{9,8},{10,9... | collective-permute-start | bytes 540680 | tf_op jit(solution)/shard_map/ppermute | solution.py:53
  34.3 3.9 %collective-permute-done.2.moving = bf16[32,2816]{1,0:T(8,128)(2,1)S(1)} collective-permute-done((bf16[32,2816]{1,0:T(8,128)(2,1)S(1)}, bf16[32,2816]{1,0:T(8,128)(2,1)S(1)}, u32[]{:S(2)}, u32[]{:S(2)}) %collective-permute-start.2) | collective-permute-done | bytes 180256 | tf_op jit(solution)/shard_map/ppermute | solution.py:53
  38.5 2.7 %collective-permute-start.7 = (bf16[32,2816]{1,0:T(8,128)(2,1)S(1)}, bf16[32,2816]{1,0:T(8,128)(2,1)S(1)}, u32[]{:S(2)}, u32[]{:S(2)}) collective-permute-start(bf16[32,2816]{1,0:T(8,128)(2,1)S(1)} %shard_map.92), channel_id=1, source_target_pairs={{0,7},{1,0},{2,1},{3,2},{4,3},{5,4},{6,5},{7,6},{8,15},{9,8},{10,9... | collective-permute-start | bytes 540680 | tf_op jit(solution)/shard_map/ppermute | solution.py:53
  41.2 2.7 %collective-permute-done.3.moving = bf16[32,2816]{1,0:T(8,128)(2,1)S(1)} collective-permute-done((bf16[32,2816]{1,0:T(8,128)(2,1)S(1)}, bf16[32,2816]{1,0:T(8,128)(2,1)S(1)}, u32[]{:S(2)}, u32[]{:S(2)}) %collective-permute-start.3) | collective-permute-done | bytes 180256 | tf_op jit(solution)/shard_map/ppermute | solution.py:53
  44.2 2.7 %collective-permute-start.8 = (bf16[32,2816]{1,0:T(8,128)(2,1)S(1)}, bf16[32,2816]{1,0:T(8,128)(2,1)S(1)}, u32[]{:S(2)}, u32[]{:S(2)}) collective-permute-start(bf16[32,2816]{1,0:T(8,128)(2,1)S(1)} %shard_map.93), channel_id=1, source_target_pairs={{0,7},{1,0},{2,1},{3,2},{4,3},{5,4},{6,5},{7,6},{8,15},{9,8},{10,9... | collective-permute-start | bytes 540680 | tf_op jit(solution)/shard_map/ppermute | solution.py:53
  46.9 2.7 %collective-permute-done.4.up_in = bf16[32,2816]{1,0:T(8,128)(2,1)S(1)} collective-permute-done((bf16[32,2816]{1,0:T(8,128)(2,1)S(1)}, bf16[32,2816]{1,0:T(8,128)(2,1)S(1)}, u32[]{:S(2)}, u32[]{:S(2)}) %collective-permute-start.4) | collective-permute-done | bytes 180256 | tf_op jit(solution)/shard_map/ppermute | solution.py:53
  49.7 0.1 shard_map.94.refs_0_
  49.8 1.7 %collective-permute-start.13 = (bf16[32,1920]{1,0:T(8,128)(2,1)S(1)}, bf16[32,1920]{1,0:T(8,128)(2,1)S(1)}, u32[]{:S(2)}, u32[]{:S(2)}) collective-permute-start(bf16[32,1920]{1,0:T(8,128)(2,1)S(1)} %shard_map.94.refs_0_), channel_id=1, source_target_pairs={{0,2},{1,3},{2,4},{3,5},{4,6},{5,7},{6,0},{7,1},{8,10},{9,11},{10,... | collective-permute-start | bytes 368648 | tf_op jit(solution)/shard_map/ppermute | solution.py:53
  51.5 2.0 %collective-permute-start.10 = (bf16[32,1920]{1,0:T(8,128)(2,1)S(1)}, bf16[32,1920]{1,0:T(8,128)(2,1)S(1)}, u32[]{:S(2)}, u32[]{:S(2)}) collective-permute-start(bf16[32,1920]{1,0:T(8,128)(2,1)S(1)} %shard_map.94.refs_0_), channel_id=1, source_target_pairs={{0,6},{1,7},{2,0},{3,1},{4,2},{5,3},{6,4},{7,5},{8,14},{9,15},{10,... | collective-permute-start | bytes 368648 | tf_op jit(solution)/shard_map/ppermute | solution.py:53
  53.4 0.7 collective-permute-start.16
  54.1 2.0 %collective-permute-start.9 = (bf16[32,1920]{1,0:T(8,128)(2,1)S(1)}, bf16[32,1920]{1,0:T(8,128)(2,1)S(1)}, u32[]{:S(2)}, u32[]{:S(2)}) collective-permute-start(bf16[32,1920]{1,0:T(8,128)(2,1)S(1)} %shard_map.94.refs_0_), channel_id=1, source_target_pairs={{0,7},{1,0},{2,1},{3,2},{4,3},{5,4},{6,5},{7,6},{8,15},{9,8},{10,9... | collective-permute-start | bytes 368648 | tf_op jit(solution)/shard_map/ppermute | solution.py:53
  56.1 1.4 collective-permute-start.15
  57.6 2.3 %collective-permute-start.11 = (bf16[32,1920]{1,0:T(8,128)(2,1)S(1)}, bf16[32,1920]{1,0:T(8,128)(2,1)S(1)}, u32[]{:S(2)}, u32[]{:S(2)}) collective-permute-start(bf16[32,1920]{1,0:T(8,128)(2,1)S(1)} %collective-permute-done.10.refs_2_), channel_id=1, source_target_pairs={{0,7},{1,0},{2,1},{3,2},{4,3},{5,4},{6,5},{7,6},{8,15},{9,8},{10,9... | collective-permute-start | bytes 368648 | tf_op jit(solution)/shard_map/ppermute | solution.py:53
  59.8 1.3 collective-permute-start.14
  61.1 2.4 %collective-permute-start.12 = (bf16[32,896]{1,0:T(8,128)(2,1)S(1)}, bf16[32,896]{1,0:T(8,128)(2,1)S(1)}, u32[]{:S(2)}, u32[]{:S(2)}) collective-permute-start(bf16[32,896]{1,0:T(8,128)(2,1)S(1)} %slice.20), channel_id=1, source_target_pairs={{0,6},{1,7},{2,0},{3,1},{4,2},{5,3},{6,4},{7,5},{8,14},{9,15},{10,... | collective-permute-start | bytes 172040 | tf_op jit(solution)/shard_map/ppermute | solution.py:53
  63.5 3.3 %collective-permute-done.12.refs_4_ = bf16[32,896]{1,0:T(8,128)(2,1)S(1)} collective-permute-done((bf16[32,896]{1,0:T(8,128)(2,1)S(1)}, bf16[32,896]{1,0:T(8,128)(2,1)S(1)}, u32[]{:S(2)}, u32[]{:S(2)}) %collective-permute-start.12) | collective-permute-done | bytes 57376 | tf_op jit(solution)/shard_map/ppermute | solution.py:53
  66.8 1.7 %shard_map.95 = (bf16[256,1920]{1,0:T(8,128)(2,1)S(1)}, f32[128,1152]{1,0:T(8,128)S(1)}, bf16[128,1152]{1,0:T(8,128)(2,1)S(1)}) custom-call(bf16[32,1920]{1,0:T(8,128)(2,1)S(1)} %shard_map.94.refs_0_, bf16[32,1920]{1,0:T(8,128)(2,1)S(1)} %collective-permute-done.9.refs_1_, bf16[32,1920]{1,0:T(8,128)(2,1)S(1)} %collective-permute-done.10.refs_2_, ...), custom_call_target="tpu_custom_call" | custom-call | flops 1006632960 | bytes 5144576 | tf_op jit(solution)/shard_map/pallas_call | solution.py:36
  68.5 6.5 %collective-permute-start.17 = (bf16[128,1152]{1,0:T(8,128)(2,1)S(1)}, bf16[128,1152]{1,0:T(8,128)(2,1)S(1)}, u32[]{:S(2)}, u32[]{:S(2)}) collective-permute-start(bf16[128,1152]{1,0:T(8,128)(2,1)S(1)} %get-tuple-element.29), channel_id=1, source_target_pairs={{0,16},{16,0},{1,17},{17,1},{2,18},{18,2},{3,19},{19,3},{4,20},{20... | collective-permute-start | bytes 884744 | tf_op jit(solution)/shard_map/ppermute | solution.py:48
  75.0 1.2 collective-permute-done.17.other
  76.3 9.7 %all_to_all.21.got = bf16[8,16,1152]{2,1,0:T(8,128)(2,1)S(1)} all-to-all(bf16[8,16,1152]{2,1,0:T(8,128)(2,1)S(1)} %shard_map.96), channel_id=1, replica_groups=mesh['x'=4,'yl'=2,'core'=2,'pipe'=2,'z'=8] {'x','yl'}, dimensions={0} | all-to-all | bytes 589824 | tf_op jit(solution)/shard_map/all_to_all | solution.py:339
  86.0 14.8 %all_to_all.22 = bf16[16,16,1152]{2,1,0:T(8,128)(2,1)S(1)} all-to-all(bf16[16,16,1152]{2,1,0:T(8,128)(2,1)S(1)} %bitcast.38), channel_id=1, replica_groups=mesh['x'=4,'yl'=2,'core'=2,'pipe'=2,'z'=8] {'pipe','x','yl'}, dimensions={0} | all-to-all | bytes 1179648 | tf_op jit(solution)/shard_map/all_to_all | solution.py:341
  100.9 3.0 %collective-permute-start.18 = (bf16[8,16,1024]{2,1,0:T(8,128)(2,1)S(1)}, bf16[8,16,1024]{2,1,0:T(8,128)(2,1)S(1)}, u32[]{:S(2)}, u32[]{:S(2)}) collective-permute-start(bf16[8,16,1024]{2,1,0:T(8,128)(2,1)S(1)} %slice_bitcast_fusion), channel_id=1, source_target_pairs={{0,16},{16,0},{1,17},{17,1},{2,18},{18,2},{3,19},{19,3},{4,20},{20... | collective-permute-start | bytes 786440 | tf_op jit(solution)/shard_map/ppermute | solution.py:48
  103.8 1.2 collective-permute-done.18.other
  105.0 0.8 shard_map.98
  105.8 1.3 collective-permute-start.21
  107.0 1.6 collective-permute-start.22
  108.6 2.9 %collective-permute-start.24 = (bf16[32,512]{1,0:T(8,128)(2,1)S(1)}, bf16[32,512]{1,0:T(8,128)(2,1)S(1)}, u32[]{:S(2)}, u32[]{:S(2)}) collective-permute-start(bf16[32,512]{1,0:T(8,128)(2,1)S(1)} %get-tuple-element.38), channel_id=1, source_target_pairs={{0,6},{1,7},{2,0},{3,1},{4,2},{5,3},{6,4},{7,5},{8,14},{9,15},{10,... | collective-permute-start | bytes 98312 | tf_op jit(solution)/shard_map/ppermute | solution.py:53
  111.5 0.6 collective-permute-start.19
  112.1 4.4 %collective-permute-done.23.far_up = bf16[32,384]{1,0:T(8,128)(2,1)S(1)} collective-permute-done((bf16[32,384]{1,0:T(8,128)(2,1)S(1)}, bf16[32,384]{1,0:T(8,128)(2,1)S(1)}, u32[]{:S(2)}, u32[]{:S(2)}) %collective-permute-start.23) | collective-permute-done | bytes 24608 | tf_op jit(solution)/shard_map/ppermute | solution.py:53
  116.5 1.2 collective-permute-start.25
  117.7 2.5 %collective-permute-start.26 = (bf16[32,896]{1,0:T(8,128)(2,1)S(1)}, bf16[32,896]{1,0:T(8,128)(2,1)S(1)}, u32[]{:S(2)}, u32[]{:S(2)}) collective-permute-start(bf16[32,896]{1,0:T(8,128)(2,1)S(1)} %get-tuple-element.40), channel_id=1, source_target_pairs={{0,6},{1,7},{2,0},{3,1},{4,2},{5,3},{6,4},{7,5},{8,14},{9,15},{10,... | collective-permute-start | bytes 172040 | tf_op jit(solution)/shard_map/ppermute | solution.py:53
  120.2 1.6 collective-permute-done.25.refs_3_
  121.8 0.9 collective-permute-done.26.refs_4_
  122.7 2.1 %collective-permute-start.31 = (bf16[32,896]{1,0:T(8,128)(2,1)S(1)}, bf16[32,896]{1,0:T(8,128)(2,1)S(1)}, u32[]{:S(2)}, u32[]{:S(2)}) collective-permute-start(bf16[32,896]{1,0:T(8,128)(2,1)S(1)} %shard_map.100.refs_0_), channel_id=1, source_target_pairs={{0,2},{1,3},{2,4},{3,5},{4,6},{5,7},{6,0},{7,1},{8,10},{9,11},{10,... | collective-permute-start | bytes 172040 | tf_op jit(solution)/shard_map/ppermute | solution.py:53
  124.8 1.6 collective-permute-start.28
  126.4 0.9 collective-permute-start.34
  127.3 1.8 %collective-permute-start.27 = (bf16[32,896]{1,0:T(8,128)(2,1)S(1)}, bf16[32,896]{1,0:T(8,128)(2,1)S(1)}, u32[]{:S(2)}, u32[]{:S(2)}) collective-permute-start(bf16[32,896]{1,0:T(8,128)(2,1)S(1)} %shard_map.100.refs_0_), channel_id=1, source_target_pairs={{0,7},{1,0},{2,1},{3,2},{4,3},{5,4},{6,5},{7,6},{8,15},{9,8},{10,9... | collective-permute-start | bytes 172040 | tf_op jit(solution)/shard_map/ppermute | solution.py:53
  129.1 0.4 collective-permute-start.33
  129.5 2.3 %collective-permute-start.29 = (bf16[32,896]{1,0:T(8,128)(2,1)S(1)}, bf16[32,896]{1,0:T(8,128)(2,1)S(1)}, u32[]{:S(2)}, u32[]{:S(2)}) collective-permute-start(bf16[32,896]{1,0:T(8,128)(2,1)S(1)} %collective-permute-done.28.refs_2_), channel_id=1, source_target_pairs={{0,7},{1,0},{2,1},{3,2},{4,3},{5,4},{6,5},{7,6},{8,15},{9,8},{10,9... | collective-permute-start | bytes 172040 | tf_op jit(solution)/shard_map/ppermute | solution.py:53
  131.8 3.6 %collective-permute-start.30 = (bf16[32,384]{1,0:T(8,128)(2,1)S(1)}, bf16[32,384]{1,0:T(8,128)(2,1)S(1)}, u32[]{:S(2)}, u32[]{:S(2)}) collective-permute-start(bf16[32,384]{1,0:T(8,128)(2,1)S(1)} %slice.23), channel_id=1, source_target_pairs={{0,6},{1,7},{2,0},{3,1},{4,2},{5,3},{6,4},{7,5},{8,14},{9,15},{10,... | collective-permute-start | bytes 73736 | tf_op jit(solution)/shard_map/ppermute | solution.py:53
  135.4 0.9 collective-permute-done.30.refs_4_
  136.3 0.3 collective-permute-done.32.refs_5_
  136.7 2.2 %shard_map.101 = (bf16[256,1792]{1,0:T(8,128)(2,1)S(1)}, f32[128,1152]{1,0:T(8,128)S(1)}, bf16[128,1152]{1,0:T(8,128)(2,1)S(1)}) custom-call(bf16[32,896]{1,0:T(8,128)(2,1)S(1)} %shard_map.100.refs_0_, bf16[32,896]{1,0:T(8,128)(2,1)S(1)} %collective-permute-done.27.refs_1_, bf16[32,896]{1,0:T(8,128)(2,1)S(1)} %collective-permute-done.28.refs_2_, ...), custom_call_target="tpu_custom_call" | custom-call | flops 1006632960 | bytes 5603328 | tf_op jit(solution)/shard_map/pallas_call | solution.py:36
  138.8 6.5 %collective-permute-start.35 = (bf16[128,1152]{1,0:T(8,128)(2,1)S(1)}, bf16[128,1152]{1,0:T(8,128)(2,1)S(1)}, u32[]{:S(2)}, u32[]{:S(2)}) collective-permute-start(bf16[128,1152]{1,0:T(8,128)(2,1)S(1)} %get-tuple-element.45), channel_id=1, source_target_pairs={{0,16},{16,0},{1,17},{17,1},{2,18},{18,2},{3,19},{19,3},{4,20},{20... | collective-permute-start | bytes 884744 | tf_op jit(solution)/shard_map/ppermute | solution.py:48
  145.3 1.1 shard_map.102
  146.4 0.1 collective-permute-done.35.other
  146.5 0.1 shard_map.103
  146.6 11.8 %all_to_all.23.got = bf16[8,16,2048]{2,1,0:T(8,128)(2,1)S(1)} all-to-all(bf16[8,16,2048]{2,1,0:T(8,128)(2,1)S(1)} %shard_map.103), channel_id=1, replica_groups=mesh['x'=4,'yl'=2,'core'=2,'pipe'=2,'z'=8] {'x','yl'}, dimensions={0} | all-to-all | bytes 1048576 | tf_op jit(solution)/shard_map/all_to_all | solution.py:375
  158.4 0.7 shard_map.104
  159.0 1.3 collective-permute-start.36
  160.4 0.3 shard_map.105.half
  160.6 0.6 collective-permute-done.36.back
  161.2 1.1 shard_map.106
  (52 shorter events, 0.8 us)
Async XLA Ops:
  0.6 0.8 copy-start.3
  1.4 0.8 copy-start.4
  16.5 4.9 %collective-permute-start = (bf16[128,2048]{1,0:T(8,128)(2,1)S(1)}, bf16[128,2048]{1,0:T(8,128)(2,1)S(1)}, u32[]{:S(2)}, u32[]{:S(2)}) collective-permute-start(bf16[128,2048]{1,0:T(8,128)(2,1)S(1)} %bitcast.23), channel_id=1, source_target_pairs={{0,16},{16,0},{1,17},{17,1},{2,18},{18,2},{3,19},{19,3},{4,20},{20... | collective-permute-start | bytes 1572872 | tf_op jit(solution)/shard_map/ppermute | solution.py:48
  18.5 2.9 %copy-start = (bf16[1,896,1024]{2,1,0:T(8,128)(2,1)S(1)}, bf16[1,896,1024]{2,1,0:T(8,128)(2,1)}, u32[]{:S(2)}) copy-start(bf16[1,896,1024]{2,1,0:T(8,128)(2,1)} %param.9) | copy-start | bytes 5505028
  18.5 2.9 %copy-start.1 = (bf16[1,1024,128]{2,1,0:T(8,128)(2,1)S(1)}, bf16[1,1024,128]{2,1,0:T(8,128)(2,1)}, u32[]{:S(2)}) copy-start(bf16[1,1024,128]{2,1,0:T(8,128)(2,1)} %param.10) | copy-start | bytes 786436
  18.5 2.9 %copy-start.2 = (bf16[1,2,64,896]{3,2,1,0:T(8,128)(2,1)S(1)}, bf16[1,2,64,896]{3,2,1,0:T(8,128)(2,1)}, u32[]{:S(2)}) copy-start(bf16[1,2,64,896]{3,2,1,0:T(8,128)(2,1)} %param.11) | copy-start | bytes 688132
  22.8 8.6 %collective-permute-start.1 = (bf16[32,1408]{1,0:T(8,128)(2,1)S(1)}, bf16[32,1408]{1,0:T(8,128)(2,1)S(1)}, u32[]{:S(2)}, u32[]{:S(2)}) collective-permute-start(bf16[32,1408]{1,0:T(8,128)(2,1)S(1)} %get-tuple-element.26), channel_id=1, source_target_pairs={{0,1},{1,2},{2,3},{3,4},{4,5},{5,6},{6,7},{7,0},{8,9},{9,10},{10,1... | collective-permute-start | bytes 270344 | tf_op jit(solution)/shard_map/ppermute | solution.py:53
  24.5 7.0 %collective-permute-start.5 = (bf16[32,1408]{1,0:T(8,128)(2,1)S(1)}, bf16[32,1408]{1,0:T(8,128)(2,1)S(1)}, u32[]{:S(2)}, u32[]{:S(2)}) collective-permute-start(bf16[32,1408]{1,0:T(8,128)(2,1)S(1)} %get-tuple-element.27), channel_id=1, source_target_pairs={{0,7},{1,0},{2,1},{3,2},{4,3},{5,4},{6,5},{7,6},{8,15},{9,8},{10,9... | collective-permute-start | bytes 270344 | tf_op jit(solution)/shard_map/ppermute | solution.py:53
  31.5 6.8 %collective-permute-start.2 = (bf16[32,2816]{1,0:T(8,128)(2,1)S(1)}, bf16[32,2816]{1,0:T(8,128)(2,1)S(1)}, u32[]{:S(2)}, u32[]{:S(2)}) collective-permute-start(bf16[32,2816]{1,0:T(8,128)(2,1)S(1)} %shard_map.88), channel_id=1, source_target_pairs={{0,1},{1,2},{2,3},{3,4},{4,5},{5,6},{6,7},{7,0},{8,9},{9,10},{10,1... | collective-permute-start | bytes 540680 | tf_op jit(solution)/shard_map/ppermute | solution.py:53
  31.6 6.8 %collective-permute-start.6 = (bf16[32,2816]{1,0:T(8,128)(2,1)S(1)}, bf16[32,2816]{1,0:T(8,128)(2,1)S(1)}, u32[]{:S(2)}, u32[]{:S(2)}) collective-permute-start(bf16[32,2816]{1,0:T(8,128)(2,1)S(1)} %shard_map.91), channel_id=1, source_target_pairs={{0,7},{1,0},{2,1},{3,2},{4,3},{5,4},{6,5},{7,6},{8,15},{9,8},{10,9... | collective-permute-start | bytes 540680 | tf_op jit(solution)/shard_map/ppermute | solution.py:53
  38.3 5.6 %collective-permute-start.3 = (bf16[32,2816]{1,0:T(8,128)(2,1)S(1)}, bf16[32,2816]{1,0:T(8,128)(2,1)S(1)}, u32[]{:S(2)}, u32[]{:S(2)}) collective-permute-start(bf16[32,2816]{1,0:T(8,128)(2,1)S(1)} %shard_map.89), channel_id=1, source_target_pairs={{0,1},{1,2},{2,3},{3,4},{4,5},{5,6},{6,7},{7,0},{8,9},{9,10},{10,1... | collective-permute-start | bytes 540680 | tf_op jit(solution)/shard_map/ppermute | solution.py:53
  38.5 5.6 %collective-permute-start.7 = (bf16[32,2816]{1,0:T(8,128)(2,1)S(1)}, bf16[32,2816]{1,0:T(8,128)(2,1)S(1)}, u32[]{:S(2)}, u32[]{:S(2)}) collective-permute-start(bf16[32,2816]{1,0:T(8,128)(2,1)S(1)} %shard_map.92), channel_id=1, source_target_pairs={{0,7},{1,0},{2,1},{3,2},{4,3},{5,4},{6,5},{7,6},{8,15},{9,8},{10,9... | collective-permute-start | bytes 540680 | tf_op jit(solution)/shard_map/ppermute | solution.py:53
  44.0 5.6 %collective-permute-start.4 = (bf16[32,2816]{1,0:T(8,128)(2,1)S(1)}, bf16[32,2816]{1,0:T(8,128)(2,1)S(1)}, u32[]{:S(2)}, u32[]{:S(2)}) collective-permute-start(bf16[32,2816]{1,0:T(8,128)(2,1)S(1)} %shard_map.90), channel_id=1, source_target_pairs={{0,1},{1,2},{2,3},{3,4},{4,5},{5,6},{6,7},{7,0},{8,9},{9,10},{10,1... | collective-permute-start | bytes 540680 | tf_op jit(solution)/shard_map/ppermute | solution.py:53
  44.2 5.5 %collective-permute-start.8 = (bf16[32,2816]{1,0:T(8,128)(2,1)S(1)}, bf16[32,2816]{1,0:T(8,128)(2,1)S(1)}, u32[]{:S(2)}, u32[]{:S(2)}) collective-permute-start(bf16[32,2816]{1,0:T(8,128)(2,1)S(1)} %shard_map.93), channel_id=1, source_target_pairs={{0,7},{1,0},{2,1},{3,2},{4,3},{5,4},{6,5},{7,6},{8,15},{9,8},{10,9... | collective-permute-start | bytes 540680 | tf_op jit(solution)/shard_map/ppermute | solution.py:53
  49.8 6.3 %collective-permute-start.13 = (bf16[32,1920]{1,0:T(8,128)(2,1)S(1)}, bf16[32,1920]{1,0:T(8,128)(2,1)S(1)}, u32[]{:S(2)}, u32[]{:S(2)}) collective-permute-start(bf16[32,1920]{1,0:T(8,128)(2,1)S(1)} %shard_map.94.refs_0_), channel_id=1, source_target_pairs={{0,2},{1,3},{2,4},{3,5},{4,6},{5,7},{6,0},{7,1},{8,10},{9,11},{10,... | collective-permute-start | bytes 368648 | tf_op jit(solution)/shard_map/ppermute | solution.py:53
  51.5 6.1 %collective-permute-start.10 = (bf16[32,1920]{1,0:T(8,128)(2,1)S(1)}, bf16[32,1920]{1,0:T(8,128)(2,1)S(1)}, u32[]{:S(2)}, u32[]{:S(2)}) collective-permute-start(bf16[32,1920]{1,0:T(8,128)(2,1)S(1)} %shard_map.94.refs_0_), channel_id=1, source_target_pairs={{0,6},{1,7},{2,0},{3,1},{4,2},{5,3},{6,4},{7,5},{8,14},{9,15},{10,... | collective-permute-start | bytes 368648 | tf_op jit(solution)/shard_map/ppermute | solution.py:53
  53.4 7.6 %collective-permute-start.16 = (bf16[32,1920]{1,0:T(8,128)(2,1)S(1)}, bf16[32,1920]{1,0:T(8,128)(2,1)S(1)}, u32[]{:S(2)}, u32[]{:S(2)}) collective-permute-start(bf16[32,1920]{1,0:T(8,128)(2,1)S(1)} %shard_map.94.refs_0_), channel_id=1, source_target_pairs={{0,1},{1,2},{2,3},{3,4},{4,5},{5,6},{6,7},{7,0},{8,9},{9,10},{10,1... | collective-permute-start | bytes 368648 | tf_op jit(solution)/shard_map/ppermute | solution.py:53
  54.1 9.3 %collective-permute-start.9 = (bf16[32,1920]{1,0:T(8,128)(2,1)S(1)}, bf16[32,1920]{1,0:T(8,128)(2,1)S(1)}, u32[]{:S(2)}, u32[]{:S(2)}) collective-permute-start(bf16[32,1920]{1,0:T(8,128)(2,1)S(1)} %shard_map.94.refs_0_), channel_id=1, source_target_pairs={{0,7},{1,0},{2,1},{3,2},{4,3},{5,4},{6,5},{7,6},{8,15},{9,8},{10,9... | collective-permute-start | bytes 368648 | tf_op jit(solution)/shard_map/ppermute | solution.py:53
  56.1 10.7 %collective-permute-start.15 = (bf16[32,1920]{1,0:T(8,128)(2,1)S(1)}, bf16[32,1920]{1,0:T(8,128)(2,1)S(1)}, u32[]{:S(2)}, u32[]{:S(2)}) collective-permute-start(bf16[32,1920]{1,0:T(8,128)(2,1)S(1)} %collective-permute-done.13.refs_7_), channel_id=1, source_target_pairs={{0,1},{1,2},{2,3},{3,4},{4,5},{5,6},{6,7},{7,0},{8,9},{9,10},{10,1... | collective-permute-start | bytes 368648 | tf_op jit(solution)/shard_map/ppermute | solution.py:53
  57.6 9.3 %collective-permute-start.11 = (bf16[32,1920]{1,0:T(8,128)(2,1)S(1)}, bf16[32,1920]{1,0:T(8,128)(2,1)S(1)}, u32[]{:S(2)}, u32[]{:S(2)}) collective-permute-start(bf16[32,1920]{1,0:T(8,128)(2,1)S(1)} %collective-permute-done.10.refs_2_), channel_id=1, source_target_pairs={{0,7},{1,0},{2,1},{3,2},{4,3},{5,4},{6,5},{7,6},{8,15},{9,8},{10,9... | collective-permute-start | bytes 368648 | tf_op jit(solution)/shard_map/ppermute | solution.py:53
  59.8 7.0 %collective-permute-start.14 = (bf16[32,1024]{1,0:T(8,128)(2,1)S(1)}, bf16[32,1024]{1,0:T(8,128)(2,1)S(1)}, u32[]{:S(2)}, u32[]{:S(2)}) collective-permute-start(bf16[32,1024]{1,0:T(8,128)(2,1)S(1)} %slice.21), channel_id=1, source_target_pairs={{0,2},{1,3},{2,4},{3,5},{4,6},{5,7},{6,0},{7,1},{8,10},{9,11},{10,... | collective-permute-start | bytes 196616 | tf_op jit(solution)/shard_map/ppermute | solution.py:53
  61.1 5.7 %collective-permute-start.12 = (bf16[32,896]{1,0:T(8,128)(2,1)S(1)}, bf16[32,896]{1,0:T(8,128)(2,1)S(1)}, u32[]{:S(2)}, u32[]{:S(2)}) collective-permute-start(bf16[32,896]{1,0:T(8,128)(2,1)S(1)} %slice.20), channel_id=1, source_target_pairs={{0,6},{1,7},{2,0},{3,1},{4,2},{5,3},{6,4},{7,5},{8,14},{9,15},{10,... | collective-permute-start | bytes 172040 | tf_op jit(solution)/shard_map/ppermute | solution.py:53
  68.5 7.7 %collective-permute-start.17 = (bf16[128,1152]{1,0:T(8,128)(2,1)S(1)}, bf16[128,1152]{1,0:T(8,128)(2,1)S(1)}, u32[]{:S(2)}, u32[]{:S(2)}) collective-permute-start(bf16[128,1152]{1,0:T(8,128)(2,1)S(1)} %get-tuple-element.29), channel_id=1, source_target_pairs={{0,16},{16,0},{1,17},{17,1},{2,18},{18,2},{3,19},{19,3},{4,20},{20... | collective-permute-start | bytes 884744 | tf_op jit(solution)/shard_map/ppermute | solution.py:48
  100.9 4.1 %collective-permute-start.18 = (bf16[8,16,1024]{2,1,0:T(8,128)(2,1)S(1)}, bf16[8,16,1024]{2,1,0:T(8,128)(2,1)S(1)}, u32[]{:S(2)}, u32[]{:S(2)}) collective-permute-start(bf16[8,16,1024]{2,1,0:T(8,128)(2,1)S(1)} %slice_bitcast_fusion), channel_id=1, source_target_pairs={{0,16},{16,0},{1,17},{17,1},{2,18},{18,2},{3,19},{19,3},{4,20},{20... | collective-permute-start | bytes 786440 | tf_op jit(solution)/shard_map/ppermute | solution.py:48
  105.8 10.7 %collective-permute-start.21 = (bf16[32,896]{1,0:T(8,128)(2,1)S(1)}, bf16[32,896]{1,0:T(8,128)(2,1)S(1)}, u32[]{:S(2)}, u32[]{:S(2)}) collective-permute-start(bf16[32,896]{1,0:T(8,128)(2,1)S(1)} %get-tuple-element.35), channel_id=1, source_target_pairs={{0,1},{1,2},{2,3},{3,4},{4,5},{5,6},{6,7},{7,0},{8,9},{9,10},{10,1... | collective-permute-start | bytes 172040 | tf_op jit(solution)/shard_map/ppermute | solution.py:53
  107.0 9.4 %collective-permute-start.22 = (bf16[32,896]{1,0:T(8,128)(2,1)S(1)}, bf16[32,896]{1,0:T(8,128)(2,1)S(1)}, u32[]{:S(2)}, u32[]{:S(2)}) collective-permute-start(bf16[32,896]{1,0:T(8,128)(2,1)S(1)} %get-tuple-element.36), channel_id=1, source_target_pairs={{0,7},{1,0},{2,1},{3,2},{4,3},{5,4},{6,5},{7,6},{8,15},{9,8},{10,9... | collective-permute-start | bytes 172040 | tf_op jit(solution)/shard_map/ppermute | solution.py:53
  108.6 7.8 %collective-permute-start.24 = (bf16[32,512]{1,0:T(8,128)(2,1)S(1)}, bf16[32,512]{1,0:T(8,128)(2,1)S(1)}, u32[]{:S(2)}, u32[]{:S(2)}) collective-permute-start(bf16[32,512]{1,0:T(8,128)(2,1)S(1)} %get-tuple-element.38), channel_id=1, source_target_pairs={{0,6},{1,7},{2,0},{3,1},{4,2},{5,3},{6,4},{7,5},{8,14},{9,15},{10,... | collective-permute-start | bytes 98312 | tf_op jit(solution)/shard_map/ppermute | solution.py:53
  111.5 5.0 %collective-permute-start.23 = (bf16[32,384]{1,0:T(8,128)(2,1)S(1)}, bf16[32,384]{1,0:T(8,128)(2,1)S(1)}, u32[]{:S(2)}, u32[]{:S(2)}) collective-permute-start(bf16[32,384]{1,0:T(8,128)(2,1)S(1)} %get-tuple-element.37), channel_id=1, source_target_pairs={{0,2},{1,3},{2,4},{3,5},{4,6},{5,7},{6,0},{7,1},{8,10},{9,11},{10,... | collective-permute-start | bytes 73736 | tf_op jit(solution)/shard_map/ppermute | solution.py:53
  111.5 8.7 %collective-permute-start.19 = (bf16[32,896]{1,0:T(8,128)(2,1)S(1)}, bf16[32,896]{1,0:T(8,128)(2,1)S(1)}, u32[]{:S(2)}, u32[]{:S(2)}) collective-permute-start(bf16[32,896]{1,0:T(8,128)(2,1)S(1)} %get-tuple-element.31), channel_id=1, source_target_pairs={{0,1},{1,2},{2,3},{3,4},{4,5},{5,6},{6,7},{7,0},{8,9},{9,10},{10,1... | collective-permute-start | bytes 172040 | tf_op jit(solution)/shard_map/ppermute | solution.py:53
  116.4 3.7 %collective-permute-start.20 = (bf16[32,896]{1,0:T(8,128)(2,1)S(1)}, bf16[32,896]{1,0:T(8,128)(2,1)S(1)}, u32[]{:S(2)}, u32[]{:S(2)}) collective-permute-start(bf16[32,896]{1,0:T(8,128)(2,1)S(1)} %get-tuple-element.32), channel_id=1, source_target_pairs={{0,7},{1,0},{2,1},{3,2},{4,3},{5,4},{6,5},{7,6},{8,15},{9,8},{10,9... | collective-permute-start | bytes 172040 | tf_op jit(solution)/shard_map/ppermute | solution.py:53
  116.5 5.3 %collective-permute-start.25 = (bf16[32,896]{1,0:T(8,128)(2,1)S(1)}, bf16[32,896]{1,0:T(8,128)(2,1)S(1)}, u32[]{:S(2)}, u32[]{:S(2)}) collective-permute-start(bf16[32,896]{1,0:T(8,128)(2,1)S(1)} %get-tuple-element.39), channel_id=1, source_target_pairs={{0,2},{1,3},{2,4},{3,5},{4,6},{5,7},{6,0},{7,1},{8,10},{9,11},{10,... | collective-permute-start | bytes 172040 | tf_op jit(solution)/shard_map/ppermute | solution.py:53
  117.7 5.0 %collective-permute-start.26 = (bf16[32,896]{1,0:T(8,128)(2,1)S(1)}, bf16[32,896]{1,0:T(8,128)(2,1)S(1)}, u32[]{:S(2)}, u32[]{:S(2)}) collective-permute-start(bf16[32,896]{1,0:T(8,128)(2,1)S(1)} %get-tuple-element.40), channel_id=1, source_target_pairs={{0,6},{1,7},{2,0},{3,1},{4,2},{5,3},{6,4},{7,5},{8,14},{9,15},{10,... | collective-permute-start | bytes 172040 | tf_op jit(solution)/shard_map/ppermute | solution.py:53
  122.7 6.3 %collective-permute-start.31 = (bf16[32,896]{1,0:T(8,128)(2,1)S(1)}, bf16[32,896]{1,0:T(8,128)(2,1)S(1)}, u32[]{:S(2)}, u32[]{:S(2)}) collective-permute-start(bf16[32,896]{1,0:T(8,128)(2,1)S(1)} %shard_map.100.refs_0_), channel_id=1, source_target_pairs={{0,2},{1,3},{2,4},{3,5},{4,6},{5,7},{6,0},{7,1},{8,10},{9,11},{10,... | collective-permute-start | bytes 172040 | tf_op jit(solution)/shard_map/ppermute | solution.py:53
  124.8 4.6 %collective-permute-start.28 = (bf16[32,896]{1,0:T(8,128)(2,1)S(1)}, bf16[32,896]{1,0:T(8,128)(2,1)S(1)}, u32[]{:S(2)}, u32[]{:S(2)}) collective-permute-start(bf16[32,896]{1,0:T(8,128)(2,1)S(1)} %shard_map.100.refs_0_), channel_id=1, source_target_pairs={{0,6},{1,7},{2,0},{3,1},{4,2},{5,3},{6,4},{7,5},{8,14},{9,15},{10,... | collective-permute-start | bytes 172040 | tf_op jit(solution)/shard_map/ppermute | solution.py:53
  126.4 5.4 %collective-permute-start.34 = (bf16[32,896]{1,0:T(8,128)(2,1)S(1)}, bf16[32,896]{1,0:T(8,128)(2,1)S(1)}, u32[]{:S(2)}, u32[]{:S(2)}) collective-permute-start(bf16[32,896]{1,0:T(8,128)(2,1)S(1)} %shard_map.100.refs_0_), channel_id=1, source_target_pairs={{0,1},{1,2},{2,3},{3,4},{4,5},{5,6},{6,7},{7,0},{8,9},{9,10},{10,1... | collective-permute-start | bytes 172040 | tf_op jit(solution)/shard_map/ppermute | solution.py:53
  127.3 8.1 %collective-permute-start.27 = (bf16[32,896]{1,0:T(8,128)(2,1)S(1)}, bf16[32,896]{1,0:T(8,128)(2,1)S(1)}, u32[]{:S(2)}, u32[]{:S(2)}) collective-permute-start(bf16[32,896]{1,0:T(8,128)(2,1)S(1)} %shard_map.100.refs_0_), channel_id=1, source_target_pairs={{0,7},{1,0},{2,1},{3,2},{4,3},{5,4},{6,5},{7,6},{8,15},{9,8},{10,9... | collective-permute-start | bytes 172040 | tf_op jit(solution)/shard_map/ppermute | solution.py:53
  129.1 7.6 %collective-permute-start.33 = (bf16[32,896]{1,0:T(8,128)(2,1)S(1)}, bf16[32,896]{1,0:T(8,128)(2,1)S(1)}, u32[]{:S(2)}, u32[]{:S(2)}) collective-permute-start(bf16[32,896]{1,0:T(8,128)(2,1)S(1)} %collective-permute-done.31.refs_7_), channel_id=1, source_target_pairs={{0,1},{1,2},{2,3},{3,4},{4,5},{5,6},{6,7},{7,0},{8,9},{9,10},{10,1... | collective-permute-start | bytes 172040 | tf_op jit(solution)/shard_map/ppermute | solution.py:53
  129.5 7.2 %collective-permute-start.29 = (bf16[32,896]{1,0:T(8,128)(2,1)S(1)}, bf16[32,896]{1,0:T(8,128)(2,1)S(1)}, u32[]{:S(2)}, u32[]{:S(2)}) collective-permute-start(bf16[32,896]{1,0:T(8,128)(2,1)S(1)} %collective-permute-done.28.refs_2_), channel_id=1, source_target_pairs={{0,7},{1,0},{2,1},{3,2},{4,3},{5,4},{6,5},{7,6},{8,15},{9,8},{10,9... | collective-permute-start | bytes 172040 | tf_op jit(solution)/shard_map/ppermute | solution.py:53
  131.8 4.9 %collective-permute-start.32 = (bf16[32,512]{1,0:T(8,128)(2,1)S(1)}, bf16[32,512]{1,0:T(8,128)(2,1)S(1)}, u32[]{:S(2)}, u32[]{:S(2)}) collective-permute-start(bf16[32,512]{1,0:T(8,128)(2,1)S(1)} %slice.24), channel_id=1, source_target_pairs={{0,2},{1,3},{2,4},{3,5},{4,6},{5,7},{6,0},{7,1},{8,10},{9,11},{10,... | collective-permute-start | bytes 98312 | tf_op jit(solution)/shard_map/ppermute | solution.py:53
  131.8 4.5 %collective-permute-start.30 = (bf16[32,384]{1,0:T(8,128)(2,1)S(1)}, bf16[32,384]{1,0:T(8,128)(2,1)S(1)}, u32[]{:S(2)}, u32[]{:S(2)}) collective-permute-start(bf16[32,384]{1,0:T(8,128)(2,1)S(1)} %slice.23), channel_id=1, source_target_pairs={{0,6},{1,7},{2,0},{3,1},{4,2},{5,3},{6,4},{7,5},{8,14},{9,15},{10,... | collective-permute-start | bytes 73736 | tf_op jit(solution)/shard_map/ppermute | solution.py:53
  138.8 7.7 %collective-permute-start.35 = (bf16[128,1152]{1,0:T(8,128)(2,1)S(1)}, bf16[128,1152]{1,0:T(8,128)(2,1)S(1)}, u32[]{:S(2)}, u32[]{:S(2)}) collective-permute-start(bf16[128,1152]{1,0:T(8,128)(2,1)S(1)} %get-tuple-element.45), channel_id=1, source_target_pairs={{0,16},{16,0},{1,17},{17,1},{2,18},{18,2},{3,19},{19,3},{4,20},{20... | collective-permute-start | bytes 884744 | tf_op jit(solution)/shard_map/ppermute | solution.py:48
  159.0 2.2 %collective-permute-start.36 = (bf16[128,128]{1,0:T(8,128)(2,1)S(1)}, bf16[128,128]{1,0:T(8,128)(2,1)S(1)}, u32[]{:S(2)}, u32[]{:S(2)}) collective-permute-start(bf16[128,128]{1,0:T(8,128)(2,1)S(1)} %get-tuple-element.47.back), channel_id=1, source_target_pairs={{0,16},{16,0},{1,17},{17,1},{2,18},{18,2},{3,19},{19,3},{4,20},{20... | collective-permute-start | bytes 98312 | tf_op jit(solution)/shard_map/ppermute | solution.py:48

commit v5 on v4

--- a/solution.py
+++ b/solution.py
@@ -132,13 +132,12 @@
     sent[:, 2 * hidden:] = total[:, 2 * hidden:width].astype(BF16)
 
 
-def collect(pieces, whole):
+def collect(n, pieces, whole):
     rows = pieces[0].shape[0]
-    n = len(pieces) - 1
-    far = n // 2
+    split = len(pieces) - n
     for step, piece in enumerate(pieces):
-        lo = pieces[far].shape[1] if step == far + 1 else 0
-        distance = step if step <= far else step - 1
+        distance = step if step <= n // 2 else step - split
+        lo = pieces[n // 2].shape[1] if split and step == n // 2 + 1 else 0
         at = pl.multiple_of(lax.rem(lax.axis_index("z") + distance, n) * rows, rows)
         whole[pl.ds(at, rows), lo:lo + piece.shape[1]] = piece[...]
 
@@ -162,14 +161,14 @@
 def backward_kernel(count, *refs):
     pieces = refs[:count]
     weight, first, second, whole, mine, other = refs[count:]
-    collect(pieces, whole)
+    collect(lax.axis_size("z"), pieces, whole)
     input_partials(whole, weight, first, second, mine, other)
 
 
 def lower_kernel(count, *refs):
     pieces = refs[:count]
     whole, weight, first, second, act, mine, other, hidden_grad = refs[count:]
-    collect(pieces, hidden_grad)
+    collect(lax.axis_size("z"), pieces, hidden_grad)
     hidden = hidden_grad.shape[1]
     for lo, size in tiles(hidden, 128):
         gate_grad, up_grad = swiglu_back(
@@ -201,32 +200,16 @@
 
 
 def hidden_kernel(mine, other, down, *outs):
-    *blocks, far_one, far_two, held = outs
+    *blocks, held = outs
     chips, own, feat = other.shape
     n, rows, _ = held.shape
     g = jnp.concatenate([mine[1, :, :, :feat], other[...]], axis=0).reshape(2 * chips * own, feat)
     held[...] = dot_nt(g, down[...]).astype(BF16).reshape(held.shape)
     for distance in range(n):
-        block = held[lax.rem(lax.axis_index("z") + distance, n)]
-        if distance == n // 2:
-            cut = far_one.shape[1]
-            far_one[...] = block[:, :cut]
-            far_two[...] = block[:, cut:]
-        else:
-            blocks[distance if distance < n // 2 else distance - 1][...] = block
-
-
-def pass_on_kernel(ahead, behind, three_up, three_back, far_up, far_back, up, back):
-    cut = far_up.shape[1]
-    total = ahead[...].astype(F32) + three_up[...].astype(F32)
-    up[:, :cut] = (total[:, :cut] + far_up[...].astype(F32)).astype(BF16)
-    up[:, cut:] = total[:, cut:].astype(BF16)
-    total = behind[...].astype(F32) + three_back[...].astype(F32)
-    back[:, :cut] = total[:, :cut].astype(BF16)
-    back[:, cut:] = (total[:, cut:] + far_back[...].astype(F32)).astype(BF16)
-
-
-def sum_z_kernel(*refs):
+        blocks[distance][...] = held[lax.rem(lax.axis_index("z") + distance, n)]
+
+
+def add_kernel(*refs):
     *terms, out = refs
     total = terms[0][...].astype(F32)
     for term in terms[1:]:
@@ -295,12 +278,15 @@
     width = 2 * hidden + 2 * rank
     factor = adapter_scale / math.sqrt(tokens)
 
-    def gather_z(piece):
+    def gather_z(piece, halves):
         cut = piece.shape[1] // 256 * 128
         ahead_two, behind_two = ring(piece, -2), ring(piece, 2)
         ahead, behind = ring(piece, -1), ring(piece, 1)
         ahead_three, behind_three = ring(ahead_two, -1), ring(behind_two, 1)
-        far = [ring(ahead_two[:, :cut], -2), ring(behind_two[:, cut:], 2)]
+        if halves:
+            far = [ring(ahead_two[:, :cut], -2), ring(behind_two[:, cut:], 2)]
+        else:
+            far = [ring(ahead_two, -2)]
         return [piece, ahead, ahead_two, ahead_three] + far + [behind_three, behind_two, behind]
 
     message = call(
@@ -329,9 +315,9 @@
             back = call(functools.partial(ring_add_kernel, -step), kept((block, full)), back, parts)
     sent = call(middle_kernel, kept((block, width)), up, back, parts)
     whole, half_mine, half_other = call(
-        functools.partial(backward_kernel, n + 1),
+        functools.partial(backward_kernel, n),
         (kept((tokens, width)), kept((half, feat + 2 * rank), F32), kept((half, feat + 2 * rank))),
-        *gather_z(sent), weight, first, second,
+        *gather_z(sent, False), weight, first, second,
         flops=2 * tokens * feat * width,
     )
     shape = (chips, own, feat + 2 * rank)
@@ -340,26 +326,21 @@
 
     handed = lax.all_to_all(message.reshape((2 * chips,) + shape[1:]), ("pipe",) + CHIPS, 0, 0)
     handed = handed.reshape((2,) + shape)
-    cut = hidden // 256 * 128
-    zero, one, two, three, minus_three, minus_two, minus_one, far_one, far_two = call(
-        hidden_kernel,
-        (kept((block, hidden)),) * (n - 1) + (kept((block, cut)), kept((block, hidden - cut))),
+    zero, one, two, three, far, minus_three, minus_two, minus_one = call(
+        hidden_kernel, (kept((block, hidden)),) * n,
         handed, core_swap(handed[1, :, :, :feat]), down_weight,
         scratch=[pltpu.VMEM((n, block, hidden), BF16)],
         flops=2 * tokens * feat * hidden,
     )
-    up, back = call(
-        pass_on_kernel, (kept((block, hidden)),) * 2,
-        two, minus_two, ring(three, 1), ring(minus_three, -1), ring(far_one, 2), ring(far_two, -2),
-    )
-    message = call(
-        sum_z_kernel, kept((block, hidden)),
-        zero, ring(one, 1), ring(minus_one, -1), ring(up, 2), ring(back, -2),
+    up = call(add_kernel, kept((block, hidden)), two, ring(three, 1), ring(far, 2))
+    back = call(add_kernel, kept((block, hidden)), minus_two, ring(minus_three, -1))
+    summed = call(
+        add_kernel, kept((block, hidden)), zero, ring(one, 1), ring(minus_one, -1), ring(up, 2), ring(back, -2)
     )
     act, half_mine, half_other = call(
-        functools.partial(lower_kernel, n + 1),
+        functools.partial(lower_kernel, n),
         (kept((tokens, 2 * hidden)), kept((half, feat + 2 * rank), F32), kept((half, feat + 2 * rank))),
-        *gather_z(message), whole, weight, first, second,
+        *gather_z(summed, False), whole, weight, first, second,
         scratch=[pltpu.VMEM((tokens, hidden), BF16)],
         flops=2 * tokens * feat * width,
     )

time: 163 us -> 158 us (0.969)
  starting transfers between devices: 69.7 us -> 63.7 us
    ppermute x32 -> x29, starting transfers between devices: 50.4 us -> 46.8 us  [ring(): return lax.ppermute(block, 'z', [(i, (i + step) % n) for i in range(n)])]
    ppermute x5, starting transfers between devices: 19.3 us -> 16.9 us  [core_swap(): return lax.ppermute(block, 'core', [(0, 1), (1, 0)])]
    ppermute x32 -> x29, waiting for transfers between devices: 21.6 us -> 23.1 us  [ring(): return lax.ppermute(block, 'z', [(i, (i + step) % n) for i in range(n)])]
    pallas_call x22 -> x23, Pallas kernels: 12 us -> 12 us  [call(): pl.pallas_call(kernel, out_shape=outs, in_specs=[pl.BlockSpec(memory_spac...]
  transfers between devices with their start and end apart: 37 -> 34, of which waited for: 14 -> 17; matrix products, arithmetic and copies ran while one was open for 2% -> 2% of each run, Pallas kernels for 2% -> 2%
where the time goes in v5:
time: 158 us
  starting transfers between devices  63.7 us (40%)
  blocking collectives  50.5 us (32%)
  waiting for transfers between devices  26.1 us (17%)
  Pallas kernels  12 us (8%)
  local copies, waits for them, and re-layouts  4.39 us (3%)
    ppermute x29, starting transfers between devices, ring(): return lax.ppermute(block, 'z', [(i, (i + step) % n) for i in range(n)])  46.8 us
    ppermute x29, waiting for transfers between devices, ring(): return lax.ppermute(block, 'z', [(i, (i + step) % n) for i in range(n)])  23.1 us
    ppermute x5, starting transfers between devices, core_swap(): return lax.ppermute(block, 'core', [(0, 1), (1, 0)])  16.9 us
    all_to_all x1, blocking collectives, local(): lax.all_to_all(message.reshape((2 * chips,) + shape[1:]), ('pipe',) + CHI...  14.8 us
    all_to_all x1, blocking collectives, local(): mine = lax.all_to_all(message, CHIPS, 0, 0).reshape(half, 2 * feat)  14.3 us
    pallas_call x23, Pallas kernels, call(): pl.pallas_call(kernel, out_shape=outs, in_specs=[pl.BlockSpec(memory_spac...  12 us
    all_to_all x1, blocking collectives, local(): got = lax.all_to_all(message, CHIPS, 0, 0)  11.8 us
    all_to_all x1, blocking collectives, local(): lax.all_to_all(message, CHIPS, 0, 0)  9.69 us
  transfers between devices with their start and end apart: 34, of which 17 were waited for; matrix products, arithmetic and copies ran while one was open for 2% of the time, Pallas kernels for 2%

profile of v5, /device:TPU:1, one launch (start us, length us, event | category | flops | bytes accessed | tf_op | source)
XLA Modules:
  0.0 157.7 jit_solution(2150210077752757625)
XLA Ops:
  0.6 0.7 copy-done.3
  1.4 0.8 copy-done.4
  2.2 14.3 %all_to_all.20 = bf16[8,16,2048]{2,1,0:T(8,128)(2,1)S(1)} all-to-all(bf16[8,16,2048]{2,1,0:T(8,128)(2,1)S(1)} %shard_map.85), channel_id=1, replica_groups=mesh['x'=4,'yl'=2,'core'=2,'pipe'=2,'z'=8] {'x','yl'}, dimensions={0} | all-to-all | bytes 1048576 | tf_op jit(solution)/shard_map/all_to_all | solution.py:297
  16.5 2.1 %collective-permute-start = (bf16[128,2048]{1,0:T(8,128)(2,1)S(1)}, bf16[128,2048]{1,0:T(8,128)(2,1)S(1)}, u32[]{:S(2)}, u32[]{:S(2)}) collective-permute-start(bf16[128,2048]{1,0:T(8,128)(2,1)S(1)} %bitcast.23), channel_id=1, source_target_pairs={{0,16},{16,0},{1,17},{17,1},{2,18},{18,2},{3,19},{19,3},{4,20},{20... | collective-permute-start | bytes 1572872 | tf_op jit(solution)/shard_map/ppermute | solution.py:48
  18.5 2.9 %copy.9 = bf16[128,8,2,896]{3,1,2,0:T(8,128)(2,1)S(1)} copy(bf16[128,8,2,896]{3,2,1,0:T(2,128)(2,1)} %bitcast.41) | data formatting | bytes 7340032
  21.4 1.4 shard_map.86
  22.8 1.7 %collective-permute-start.1 = (bf16[32,1408]{1,0:T(8,128)(2,1)S(1)}, bf16[32,1408]{1,0:T(8,128)(2,1)S(1)}, u32[]{:S(2)}, u32[]{:S(2)}) collective-permute-start(bf16[32,1408]{1,0:T(8,128)(2,1)S(1)} %get-tuple-element.23), channel_id=1, source_target_pairs={{0,1},{1,2},{2,3},{3,4},{4,5},{5,6},{6,7},{7,0},{8,9},{9,10},{10,1... | collective-permute-start | bytes 270344 | tf_op jit(solution)/shard_map/ppermute | solution.py:53
  24.5 4.0 %collective-permute-start.5 = (bf16[32,1408]{1,0:T(8,128)(2,1)S(1)}, bf16[32,1408]{1,0:T(8,128)(2,1)S(1)}, u32[]{:S(2)}, u32[]{:S(2)}) collective-permute-start(bf16[32,1408]{1,0:T(8,128)(2,1)S(1)} %get-tuple-element.24), channel_id=1, source_target_pairs={{0,7},{1,0},{2,1},{3,2},{4,3},{5,4},{6,5},{7,6},{8,15},{9,8},{10,9... | collective-permute-start | bytes 270344 | tf_op jit(solution)/shard_map/ppermute | solution.py:53
  28.5 2.3 %shard_map.87.parts = bf16[8,32,2816]{2,1,0:T(8,128)(2,1)S(1)} custom-call(bf16[128,2048]{1,0:T(8,128)(2,1)S(1)} %bitcast.25, bf16[128,2048]{1,0:T(8,128)(2,1)S(1)} %collective-permute-done.other.inputs, bf16[1024,1792]{1,0:T(8,128)(2,1)S(1)} %bitcast.17, bf16[896,1024]{1,0:T(8,128)(2,1)S(1)} %bitcast.21, bf16[1024,128]{1,0:T(8,128)(2,1)S(1)} %bitcast.31, ...), custom_call_target="tpu_custom_call" | custom-call | flops 1476395008 | bytes 7045120 | tf_op jit(solution)/shard_map/pallas_call | solution.py:36
  30.8 0.6 collective-permute-done.1.moving
  31.5 0.1 collective-permute-start.2
  31.6 2.7 %collective-permute-start.6 = (bf16[32,2816]{1,0:T(8,128)(2,1)S(1)}, bf16[32,2816]{1,0:T(8,128)(2,1)S(1)}, u32[]{:S(2)}, u32[]{:S(2)}) collective-permute-start(bf16[32,2816]{1,0:T(8,128)(2,1)S(1)} %shard_map.91), channel_id=1, source_target_pairs={{0,7},{1,0},{2,1},{3,2},{4,3},{5,4},{6,5},{7,6},{8,15},{9,8},{10,9... | collective-permute-start | bytes 540680 | tf_op jit(solution)/shard_map/ppermute | solution.py:53
  34.3 3.9 %collective-permute-done.2.moving = bf16[32,2816]{1,0:T(8,128)(2,1)S(1)} collective-permute-done((bf16[32,2816]{1,0:T(8,128)(2,1)S(1)}, bf16[32,2816]{1,0:T(8,128)(2,1)S(1)}, u32[]{:S(2)}, u32[]{:S(2)}) %collective-permute-start.2) | collective-permute-done | bytes 180256 | tf_op jit(solution)/shard_map/ppermute | solution.py:53
  38.3 0.1 collective-permute-start.3
  38.5 2.7 %collective-permute-start.7 = (bf16[32,2816]{1,0:T(8,128)(2,1)S(1)}, bf16[32,2816]{1,0:T(8,128)(2,1)S(1)}, u32[]{:S(2)}, u32[]{:S(2)}) collective-permute-start(bf16[32,2816]{1,0:T(8,128)(2,1)S(1)} %shard_map.92), channel_id=1, source_target_pairs={{0,7},{1,0},{2,1},{3,2},{4,3},{5,4},{6,5},{7,6},{8,15},{9,8},{10,9... | collective-permute-start | bytes 540680 | tf_op jit(solution)/shard_map/ppermute | solution.py:53
  41.2 2.7 %collective-permute-done.3.moving = bf16[32,2816]{1,0:T(8,128)(2,1)S(1)} collective-permute-done((bf16[32,2816]{1,0:T(8,128)(2,1)S(1)}, bf16[32,2816]{1,0:T(8,128)(2,1)S(1)}, u32[]{:S(2)}, u32[]{:S(2)}) %collective-permute-start.3) | collective-permute-done | bytes 180256 | tf_op jit(solution)/shard_map/ppermute | solution.py:53
  44.0 0.1 collective-permute-start.4
  44.2 2.7 %collective-permute-start.8 = (bf16[32,2816]{1,0:T(8,128)(2,1)S(1)}, bf16[32,2816]{1,0:T(8,128)(2,1)S(1)}, u32[]{:S(2)}, u32[]{:S(2)}) collective-permute-start(bf16[32,2816]{1,0:T(8,128)(2,1)S(1)} %shard_map.93), channel_id=1, source_target_pairs={{0,7},{1,0},{2,1},{3,2},{4,3},{5,4},{6,5},{7,6},{8,15},{9,8},{10,9... | collective-permute-start | bytes 540680 | tf_op jit(solution)/shard_map/ppermute | solution.py:53
  46.9 2.7 %collective-permute-done.4.up_in = bf16[32,2816]{1,0:T(8,128)(2,1)S(1)} collective-permute-done((bf16[32,2816]{1,0:T(8,128)(2,1)S(1)}, bf16[32,2816]{1,0:T(8,128)(2,1)S(1)}, u32[]{:S(2)}, u32[]{:S(2)}) %collective-permute-start.4) | collective-permute-done | bytes 180256 | tf_op jit(solution)/shard_map/ppermute | solution.py:53
  49.7 0.1 shard_map.94.refs_0_
  49.8 1.7 %collective-permute-start.13 = (bf16[32,1920]{1,0:T(8,128)(2,1)S(1)}, bf16[32,1920]{1,0:T(8,128)(2,1)S(1)}, u32[]{:S(2)}, u32[]{:S(2)}) collective-permute-start(bf16[32,1920]{1,0:T(8,128)(2,1)S(1)} %shard_map.94.refs_0_), channel_id=1, source_target_pairs={{0,2},{1,3},{2,4},{3,5},{4,6},{5,7},{6,0},{7,1},{8,10},{9,11},{10,... | collective-permute-start | bytes 368648 | tf_op jit(solution)/shard_map/ppermute | solution.py:53
  51.5 2.0 %collective-permute-start.10 = (bf16[32,1920]{1,0:T(8,128)(2,1)S(1)}, bf16[32,1920]{1,0:T(8,128)(2,1)S(1)}, u32[]{:S(2)}, u32[]{:S(2)}) collective-permute-start(bf16[32,1920]{1,0:T(8,128)(2,1)S(1)} %shard_map.94.refs_0_), channel_id=1, source_target_pairs={{0,6},{1,7},{2,0},{3,1},{4,2},{5,3},{6,4},{7,5},{8,14},{9,15},{10,... | collective-permute-start | bytes 368648 | tf_op jit(solution)/shard_map/ppermute | solution.py:53
  53.4 0.7 collective-permute-start.15
  54.1 2.0 %collective-permute-start.9 = (bf16[32,1920]{1,0:T(8,128)(2,1)S(1)}, bf16[32,1920]{1,0:T(8,128)(2,1)S(1)}, u32[]{:S(2)}, u32[]{:S(2)}) collective-permute-start(bf16[32,1920]{1,0:T(8,128)(2,1)S(1)} %shard_map.94.refs_0_), channel_id=1, source_target_pairs={{0,7},{1,0},{2,1},{3,2},{4,3},{5,4},{6,5},{7,6},{8,15},{9,8},{10,9... | collective-permute-start | bytes 368648 | tf_op jit(solution)/shard_map/ppermute | solution.py:53
  56.1 1.4 collective-permute-start.14
  57.6 1.8 %collective-permute-start.12 = (bf16[32,1920]{1,0:T(8,128)(2,1)S(1)}, bf16[32,1920]{1,0:T(8,128)(2,1)S(1)}, u32[]{:S(2)}, u32[]{:S(2)}) collective-permute-start(bf16[32,1920]{1,0:T(8,128)(2,1)S(1)} %collective-permute-done.10.refs_2_), channel_id=1, source_target_pairs={{0,6},{1,7},{2,0},{3,1},{4,2},{5,3},{6,4},{7,5},{8,14},{9,15},{10,... | collective-permute-start | bytes 368648 | tf_op jit(solution)/shard_map/ppermute | solution.py:53
  59.4 1.6 %collective-permute-start.11 = (bf16[32,1920]{1,0:T(8,128)(2,1)S(1)}, bf16[32,1920]{1,0:T(8,128)(2,1)S(1)}, u32[]{:S(2)}, u32[]{:S(2)}) collective-permute-start(bf16[32,1920]{1,0:T(8,128)(2,1)S(1)} %collective-permute-done.10.refs_2_), channel_id=1, source_target_pairs={{0,7},{1,0},{2,1},{3,2},{4,3},{5,4},{6,5},{7,6},{8,15},{9,8},{10,9... | collective-permute-start | bytes 368648 | tf_op jit(solution)/shard_map/ppermute | solution.py:53
  61.0 2.0 %collective-permute-done.14.refs_5_ = bf16[32,1920]{1,0:T(8,128)(2,1)S(1)} collective-permute-done((bf16[32,1920]{1,0:T(8,128)(2,1)S(1)}, bf16[32,1920]{1,0:T(8,128)(2,1)S(1)}, u32[]{:S(2)}, u32[]{:S(2)}) %collective-permute-start.14) | collective-permute-done | bytes 122912 | tf_op jit(solution)/shard_map/ppermute | solution.py:53
  63.0 3.8 %collective-permute-done.12.refs_4_ = bf16[32,1920]{1,0:T(8,128)(2,1)S(1)} collective-permute-done((bf16[32,1920]{1,0:T(8,128)(2,1)S(1)}, bf16[32,1920]{1,0:T(8,128)(2,1)S(1)}, u32[]{:S(2)}, u32[]{:S(2)}) %collective-permute-start.12) | collective-permute-done | bytes 122912 | tf_op jit(solution)/shard_map/ppermute | solution.py:53
  66.9 0.7 collective-permute-done.11.refs_3_
  67.6 1.7 %shard_map.95 = (bf16[256,1920]{1,0:T(8,128)(2,1)S(1)}, f32[128,1152]{1,0:T(8,128)S(1)}, bf16[128,1152]{1,0:T(8,128)(2,1)S(1)}) custom-call(bf16[32,1920]{1,0:T(8,128)(2,1)S(1)} %shard_map.94.refs_0_, bf16[32,1920]{1,0:T(8,128)(2,1)S(1)} %collective-permute-done.9.refs_1_, bf16[32,1920]{1,0:T(8,128)(2,1)S(1)} %collective-permute-done.10.refs_2_, ...), custom_call_target="tpu_custom_call" | custom-call | flops 1006632960 | bytes 5144576 | tf_op jit(solution)/shard_map/pallas_call | solution.py:36
  69.3 5.5 %collective-permute-start.16 = (bf16[128,1152]{1,0:T(8,128)(2,1)S(1)}, bf16[128,1152]{1,0:T(8,128)(2,1)S(1)}, u32[]{:S(2)}, u32[]{:S(2)}) collective-permute-start(bf16[128,1152]{1,0:T(8,128)(2,1)S(1)} %get-tuple-element.26), channel_id=1, source_target_pairs={{0,16},{16,0},{1,17},{17,1},{2,18},{18,2},{3,19},{19,3},{4,20},{20... | collective-permute-start | bytes 884744 | tf_op jit(solution)/shard_map/ppermute | solution.py:48
  74.8 1.2 collective-permute-done.16.other
  76.0 9.7 %all_to_all.21.got = bf16[8,16,1152]{2,1,0:T(8,128)(2,1)S(1)} all-to-all(bf16[8,16,1152]{2,1,0:T(8,128)(2,1)S(1)} %shard_map.96), channel_id=1, replica_groups=mesh['x'=4,'yl'=2,'core'=2,'pipe'=2,'z'=8] {'x','yl'}, dimensions={0} | all-to-all | bytes 589824 | tf_op jit(solution)/shard_map/all_to_all | solution.py:325
  85.8 14.8 %all_to_all.22 = bf16[16,16,1152]{2,1,0:T(8,128)(2,1)S(1)} all-to-all(bf16[16,16,1152]{2,1,0:T(8,128)(2,1)S(1)} %bitcast.38), channel_id=1, replica_groups=mesh['x'=4,'yl'=2,'core'=2,'pipe'=2,'z'=8] {'pipe','x','yl'}, dimensions={0} | all-to-all | bytes 1179648 | tf_op jit(solution)/shard_map/all_to_all | solution.py:327
  100.7 3.0 %collective-permute-start.17 = (bf16[8,16,1024]{2,1,0:T(8,128)(2,1)S(1)}, bf16[8,16,1024]{2,1,0:T(8,128)(2,1)S(1)}, u32[]{:S(2)}, u32[]{:S(2)}) collective-permute-start(bf16[8,16,1024]{2,1,0:T(8,128)(2,1)S(1)} %slice_bitcast_fusion), channel_id=1, source_target_pairs={{0,16},{16,0},{1,17},{17,1},{2,18},{18,2},{3,19},{19,3},{4,20},{20... | collective-permute-start | bytes 786440 | tf_op jit(solution)/shard_map/ppermute | solution.py:48
  103.6 1.2 collective-permute-done.17.other
  104.8 0.8 shard_map.98
  105.6 0.9 collective-permute-start.20
  106.5 2.8 %collective-permute-start.21 = (bf16[32,896]{1,0:T(8,128)(2,1)S(1)}, bf16[32,896]{1,0:T(8,128)(2,1)S(1)}, u32[]{:S(2)}, u32[]{:S(2)}) collective-permute-start(bf16[32,896]{1,0:T(8,128)(2,1)S(1)} %get-tuple-element.32), channel_id=1, source_target_pairs={{0,2},{1,3},{2,4},{3,5},{4,6},{5,7},{6,0},{7,1},{8,10},{9,11},{10,... | collective-permute-start | bytes 172040 | tf_op jit(solution)/shard_map/ppermute | solution.py:53
  109.2 1.6 %collective-permute-start.23 = (bf16[32,896]{1,0:T(8,128)(2,1)S(1)}, bf16[32,896]{1,0:T(8,128)(2,1)S(1)}, u32[]{:S(2)}, u32[]{:S(2)}) collective-permute-start(bf16[32,896]{1,0:T(8,128)(2,1)S(1)} %get-tuple-element.34), channel_id=1, source_target_pairs={{0,7},{1,0},{2,1},{3,2},{4,3},{5,4},{6,5},{7,6},{8,15},{9,8},{10,9... | collective-permute-start | bytes 172040 | tf_op jit(solution)/shard_map/ppermute | solution.py:53
  110.9 2.7 %collective-permute-start.19 = (bf16[32,896]{1,0:T(8,128)(2,1)S(1)}, bf16[32,896]{1,0:T(8,128)(2,1)S(1)}, u32[]{:S(2)}, u32[]{:S(2)}) collective-permute-start(bf16[32,896]{1,0:T(8,128)(2,1)S(1)} %get-tuple-element.29), channel_id=1, source_target_pairs={{0,7},{1,0},{2,1},{3,2},{4,3},{5,4},{6,5},{7,6},{8,15},{9,8},{10,9... | collective-permute-start | bytes 172040 | tf_op jit(solution)/shard_map/ppermute | solution.py:53
  113.6 0.1 collective-permute-start.22
  113.7 3.8 %collective-permute-start.24 = (bf16[32,896]{1,0:T(8,128)(2,1)S(1)}, bf16[32,896]{1,0:T(8,128)(2,1)S(1)}, u32[]{:S(2)}, u32[]{:S(2)}) collective-permute-start(bf16[32,896]{1,0:T(8,128)(2,1)S(1)} %shard_map.100), channel_id=1, source_target_pairs={{0,6},{1,7},{2,0},{3,1},{4,2},{5,3},{6,4},{7,5},{8,14},{9,15},{10,... | collective-permute-start | bytes 172040 | tf_op jit(solution)/shard_map/ppermute | solution.py:53
  117.5 1.2 collective-permute-done.22.refs_3_
  118.8 0.5 collective-permute-done.24.refs_4_
  119.3 2.9 %collective-permute-start.29 = (bf16[32,896]{1,0:T(8,128)(2,1)S(1)}, bf16[32,896]{1,0:T(8,128)(2,1)S(1)}, u32[]{:S(2)}, u32[]{:S(2)}) collective-permute-start(bf16[32,896]{1,0:T(8,128)(2,1)S(1)} %shard_map.101.refs_0_), channel_id=1, source_target_pairs={{0,2},{1,3},{2,4},{3,5},{4,6},{5,7},{6,0},{7,1},{8,10},{9,11},{10,... | collective-permute-start | bytes 172040 | tf_op jit(solution)/shard_map/ppermute | solution.py:53
  122.2 1.3 collective-permute-start.26
  123.5 2.7 %collective-permute-start.25 = (bf16[32,896]{1,0:T(8,128)(2,1)S(1)}, bf16[32,896]{1,0:T(8,128)(2,1)S(1)}, u32[]{:S(2)}, u32[]{:S(2)}) collective-permute-start(bf16[32,896]{1,0:T(8,128)(2,1)S(1)} %shard_map.101.refs_0_), channel_id=1, source_target_pairs={{0,7},{1,0},{2,1},{3,2},{4,3},{5,4},{6,5},{7,6},{8,15},{9,8},{10,9... | collective-permute-start | bytes 172040 | tf_op jit(solution)/shard_map/ppermute | solution.py:53
  126.2 2.6 %collective-permute-start.28 = (bf16[32,896]{1,0:T(8,128)(2,1)S(1)}, bf16[32,896]{1,0:T(8,128)(2,1)S(1)}, u32[]{:S(2)}, u32[]{:S(2)}) collective-permute-start(bf16[32,896]{1,0:T(8,128)(2,1)S(1)} %collective-permute-done.26.refs_2_), channel_id=1, source_target_pairs={{0,6},{1,7},{2,0},{3,1},{4,2},{5,3},{6,4},{7,5},{8,14},{9,15},{10,... | collective-permute-start | bytes 172040 | tf_op jit(solution)/shard_map/ppermute | solution.py:53
  128.9 1.6 %collective-permute-done.30.refs_5_ = bf16[32,896]{1,0:T(8,128)(2,1)S(1)} collective-permute-done((bf16[32,896]{1,0:T(8,128)(2,1)S(1)}, bf16[32,896]{1,0:T(8,128)(2,1)S(1)}, u32[]{:S(2)}, u32[]{:S(2)}) %collective-permute-start.30) | collective-permute-done | bytes 57376 | tf_op jit(solution)/shard_map/ppermute | solution.py:53
  130.6 1.4 collective-permute-done.28.refs_4_
  132.0 1.6 collective-permute-done.27.refs_3_
  133.5 2.2 %shard_map.102 = (bf16[256,1792]{1,0:T(8,128)(2,1)S(1)}, f32[128,1152]{1,0:T(8,128)S(1)}, bf16[128,1152]{1,0:T(8,128)(2,1)S(1)}) custom-call(bf16[32,896]{1,0:T(8,128)(2,1)S(1)} %shard_map.101.refs_0_, bf16[32,896]{1,0:T(8,128)(2,1)S(1)} %collective-permute-done.25.refs_1_, bf16[32,896]{1,0:T(8,128)(2,1)S(1)} %collective-permute-done.26.refs_2_, ...), custom_call_target="tpu_custom_call" | custom-call | flops 1006632960 | bytes 5603328 | tf_op jit(solution)/shard_map/pallas_call | solution.py:36
  135.7 5.0 %collective-permute-start.32 = (bf16[128,1152]{1,0:T(8,128)(2,1)S(1)}, bf16[128,1152]{1,0:T(8,128)(2,1)S(1)}, u32[]{:S(2)}, u32[]{:S(2)}) collective-permute-start(bf16[128,1152]{1,0:T(8,128)(2,1)S(1)} %get-tuple-element.39), channel_id=1, source_target_pairs={{0,16},{16,0},{1,17},{17,1},{2,18},{18,2},{3,19},{19,3},{4,20},{20... | collective-permute-start | bytes 884744 | tf_op jit(solution)/shard_map/ppermute | solution.py:48
  140.7 1.1 shard_map.103
  141.8 0.1 collective-permute-done.32.other
  142.0 0.1 shard_map.104
  142.1 11.8 %all_to_all.23.got = bf16[8,16,2048]{2,1,0:T(8,128)(2,1)S(1)} all-to-all(bf16[8,16,2048]{2,1,0:T(8,128)(2,1)S(1)} %shard_map.104), channel_id=1, replica_groups=mesh['x'=4,'yl'=2,'core'=2,'pipe'=2,'z'=8] {'x','yl'}, dimensions={0} | all-to-all | bytes 1048576 | tf_op jit(solution)/shard_map/all_to_all | solution.py:356
  153.8 0.7 shard_map.105
  154.5 1.3 collective-permute-start.33
  155.8 0.3 shard_map.106.half
  156.1 0.6 collective-permute-done.33.back
  156.7 1.1 shard_map.107
  (43 shorter events, 0.7 us)
Async XLA Ops:
  0.6 0.8 copy-start.3
  1.4 0.8 copy-start.4
  16.5 4.9 %collective-permute-start = (bf16[128,2048]{1,0:T(8,128)(2,1)S(1)}, bf16[128,2048]{1,0:T(8,128)(2,1)S(1)}, u32[]{:S(2)}, u32[]{:S(2)}) collective-permute-start(bf16[128,2048]{1,0:T(8,128)(2,1)S(1)} %bitcast.23), channel_id=1, source_target_pairs={{0,16},{16,0},{1,17},{17,1},{2,18},{18,2},{3,19},{19,3},{4,20},{20... | collective-permute-start | bytes 1572872 | tf_op jit(solution)/shard_map/ppermute | solution.py:48
  18.5 2.9 %copy-start = (bf16[1,896,1024]{2,1,0:T(8,128)(2,1)S(1)}, bf16[1,896,1024]{2,1,0:T(8,128)(2,1)}, u32[]{:S(2)}) copy-start(bf16[1,896,1024]{2,1,0:T(8,128)(2,1)} %param.9) | copy-start | bytes 5505028
  18.5 2.9 %copy-start.1 = (bf16[1,1024,128]{2,1,0:T(8,128)(2,1)S(1)}, bf16[1,1024,128]{2,1,0:T(8,128)(2,1)}, u32[]{:S(2)}) copy-start(bf16[1,1024,128]{2,1,0:T(8,128)(2,1)} %param.10) | copy-start | bytes 786436
  18.5 2.9 %copy-start.2 = (bf16[1,2,64,896]{3,2,1,0:T(8,128)(2,1)S(1)}, bf16[1,2,64,896]{3,2,1,0:T(8,128)(2,1)}, u32[]{:S(2)}) copy-start(bf16[1,2,64,896]{3,2,1,0:T(8,128)(2,1)} %param.11) | copy-start | bytes 688132
  22.8 8.6 %collective-permute-start.1 = (bf16[32,1408]{1,0:T(8,128)(2,1)S(1)}, bf16[32,1408]{1,0:T(8,128)(2,1)S(1)}, u32[]{:S(2)}, u32[]{:S(2)}) collective-permute-start(bf16[32,1408]{1,0:T(8,128)(2,1)S(1)} %get-tuple-element.23), channel_id=1, source_target_pairs={{0,1},{1,2},{2,3},{3,4},{4,5},{5,6},{6,7},{7,0},{8,9},{9,10},{10,1... | collective-permute-start | bytes 270344 | tf_op jit(solution)/shard_map/ppermute | solution.py:53
  24.5 7.0 %collective-permute-start.5 = (bf16[32,1408]{1,0:T(8,128)(2,1)S(1)}, bf16[32,1408]{1,0:T(8,128)(2,1)S(1)}, u32[]{:S(2)}, u32[]{:S(2)}) collective-permute-start(bf16[32,1408]{1,0:T(8,128)(2,1)S(1)} %get-tuple-element.24), channel_id=1, source_target_pairs={{0,7},{1,0},{2,1},{3,2},{4,3},{5,4},{6,5},{7,6},{8,15},{9,8},{10,9... | collective-permute-start | bytes 270344 | tf_op jit(solution)/shard_map/ppermute | solution.py:53
  31.5 6.8 %collective-permute-start.2 = (bf16[32,2816]{1,0:T(8,128)(2,1)S(1)}, bf16[32,2816]{1,0:T(8,128)(2,1)S(1)}, u32[]{:S(2)}, u32[]{:S(2)}) collective-permute-start(bf16[32,2816]{1,0:T(8,128)(2,1)S(1)} %shard_map.88), channel_id=1, source_target_pairs={{0,1},{1,2},{2,3},{3,4},{4,5},{5,6},{6,7},{7,0},{8,9},{9,10},{10,1... | collective-permute-start | bytes 540680 | tf_op jit(solution)/shard_map/ppermute | solution.py:53
  31.6 6.8 %collective-permute-start.6 = (bf16[32,2816]{1,0:T(8,128)(2,1)S(1)}, bf16[32,2816]{1,0:T(8,128)(2,1)S(1)}, u32[]{:S(2)}, u32[]{:S(2)}) collective-permute-start(bf16[32,2816]{1,0:T(8,128)(2,1)S(1)} %shard_map.91), channel_id=1, source_target_pairs={{0,7},{1,0},{2,1},{3,2},{4,3},{5,4},{6,5},{7,6},{8,15},{9,8},{10,9... | collective-permute-start | bytes 540680 | tf_op jit(solution)/shard_map/ppermute | solution.py:53
  38.3 5.6 %collective-permute-start.3 = (bf16[32,2816]{1,0:T(8,128)(2,1)S(1)}, bf16[32,2816]{1,0:T(8,128)(2,1)S(1)}, u32[]{:S(2)}, u32[]{:S(2)}) collective-permute-start(bf16[32,2816]{1,0:T(8,128)(2,1)S(1)} %shard_map.89), channel_id=1, source_target_pairs={{0,1},{1,2},{2,3},{3,4},{4,5},{5,6},{6,7},{7,0},{8,9},{9,10},{10,1... | collective-permute-start | bytes 540680 | tf_op jit(solution)/shard_map/ppermute | solution.py:53
  38.5 5.6 %collective-permute-start.7 = (bf16[32,2816]{1,0:T(8,128)(2,1)S(1)}, bf16[32,2816]{1,0:T(8,128)(2,1)S(1)}, u32[]{:S(2)}, u32[]{:S(2)}) collective-permute-start(bf16[32,2816]{1,0:T(8,128)(2,1)S(1)} %shard_map.92), channel_id=1, source_target_pairs={{0,7},{1,0},{2,1},{3,2},{4,3},{5,4},{6,5},{7,6},{8,15},{9,8},{10,9... | collective-permute-start | bytes 540680 | tf_op jit(solution)/shard_map/ppermute | solution.py:53
  44.0 5.6 %collective-permute-start.4 = (bf16[32,2816]{1,0:T(8,128)(2,1)S(1)}, bf16[32,2816]{1,0:T(8,128)(2,1)S(1)}, u32[]{:S(2)}, u32[]{:S(2)}) collective-permute-start(bf16[32,2816]{1,0:T(8,128)(2,1)S(1)} %shard_map.90), channel_id=1, source_target_pairs={{0,1},{1,2},{2,3},{3,4},{4,5},{5,6},{6,7},{7,0},{8,9},{9,10},{10,1... | collective-permute-start | bytes 540680 | tf_op jit(solution)/shard_map/ppermute | solution.py:53
  44.2 5.5 %collective-permute-start.8 = (bf16[32,2816]{1,0:T(8,128)(2,1)S(1)}, bf16[32,2816]{1,0:T(8,128)(2,1)S(1)}, u32[]{:S(2)}, u32[]{:S(2)}) collective-permute-start(bf16[32,2816]{1,0:T(8,128)(2,1)S(1)} %shard_map.93), channel_id=1, source_target_pairs={{0,7},{1,0},{2,1},{3,2},{4,3},{5,4},{6,5},{7,6},{8,15},{9,8},{10,9... | collective-permute-start | bytes 540680 | tf_op jit(solution)/shard_map/ppermute | solution.py:53
  49.8 6.3 %collective-permute-start.13 = (bf16[32,1920]{1,0:T(8,128)(2,1)S(1)}, bf16[32,1920]{1,0:T(8,128)(2,1)S(1)}, u32[]{:S(2)}, u32[]{:S(2)}) collective-permute-start(bf16[32,1920]{1,0:T(8,128)(2,1)S(1)} %shard_map.94.refs_0_), channel_id=1, source_target_pairs={{0,2},{1,3},{2,4},{3,5},{4,6},{5,7},{6,0},{7,1},{8,10},{9,11},{10,... | collective-permute-start | bytes 368648 | tf_op jit(solution)/shard_map/ppermute | solution.py:53
  51.5 6.1 %collective-permute-start.10 = (bf16[32,1920]{1,0:T(8,128)(2,1)S(1)}, bf16[32,1920]{1,0:T(8,128)(2,1)S(1)}, u32[]{:S(2)}, u32[]{:S(2)}) collective-permute-start(bf16[32,1920]{1,0:T(8,128)(2,1)S(1)} %shard_map.94.refs_0_), channel_id=1, source_target_pairs={{0,6},{1,7},{2,0},{3,1},{4,2},{5,3},{6,4},{7,5},{8,14},{9,15},{10,... | collective-permute-start | bytes 368648 | tf_op jit(solution)/shard_map/ppermute | solution.py:53
  53.4 7.6 %collective-permute-start.15 = (bf16[32,1920]{1,0:T(8,128)(2,1)S(1)}, bf16[32,1920]{1,0:T(8,128)(2,1)S(1)}, u32[]{:S(2)}, u32[]{:S(2)}) collective-permute-start(bf16[32,1920]{1,0:T(8,128)(2,1)S(1)} %shard_map.94.refs_0_), channel_id=1, source_target_pairs={{0,1},{1,2},{2,3},{3,4},{4,5},{5,6},{6,7},{7,0},{8,9},{9,10},{10,1... | collective-permute-start | bytes 368648 | tf_op jit(solution)/shard_map/ppermute | solution.py:53
  54.1 6.9 %collective-permute-start.9 = (bf16[32,1920]{1,0:T(8,128)(2,1)S(1)}, bf16[32,1920]{1,0:T(8,128)(2,1)S(1)}, u32[]{:S(2)}, u32[]{:S(2)}) collective-permute-start(bf16[32,1920]{1,0:T(8,128)(2,1)S(1)} %shard_map.94.refs_0_), channel_id=1, source_target_pairs={{0,7},{1,0},{2,1},{3,2},{4,3},{5,4},{6,5},{7,6},{8,15},{9,8},{10,9... | collective-permute-start | bytes 368648 | tf_op jit(solution)/shard_map/ppermute | solution.py:53
  56.1 6.9 %collective-permute-start.14 = (bf16[32,1920]{1,0:T(8,128)(2,1)S(1)}, bf16[32,1920]{1,0:T(8,128)(2,1)S(1)}, u32[]{:S(2)}, u32[]{:S(2)}) collective-permute-start(bf16[32,1920]{1,0:T(8,128)(2,1)S(1)} %collective-permute-done.13.refs_6_), channel_id=1, source_target_pairs={{0,1},{1,2},{2,3},{3,4},{4,5},{5,6},{6,7},{7,0},{8,9},{9,10},{10,1... | collective-permute-start | bytes 368648 | tf_op jit(solution)/shard_map/ppermute | solution.py:53
  57.6 9.3 %collective-permute-start.12 = (bf16[32,1920]{1,0:T(8,128)(2,1)S(1)}, bf16[32,1920]{1,0:T(8,128)(2,1)S(1)}, u32[]{:S(2)}, u32[]{:S(2)}) collective-permute-start(bf16[32,1920]{1,0:T(8,128)(2,1)S(1)} %collective-permute-done.10.refs_2_), channel_id=1, source_target_pairs={{0,6},{1,7},{2,0},{3,1},{4,2},{5,3},{6,4},{7,5},{8,14},{9,15},{10,... | collective-permute-start | bytes 368648 | tf_op jit(solution)/shard_map/ppermute | solution.py:53
  59.4 8.2 %collective-permute-start.11 = (bf16[32,1920]{1,0:T(8,128)(2,1)S(1)}, bf16[32,1920]{1,0:T(8,128)(2,1)S(1)}, u32[]{:S(2)}, u32[]{:S(2)}) collective-permute-start(bf16[32,1920]{1,0:T(8,128)(2,1)S(1)} %collective-permute-done.10.refs_2_), channel_id=1, source_target_pairs={{0,7},{1,0},{2,1},{3,2},{4,3},{5,4},{6,5},{7,6},{8,15},{9,8},{10,9... | collective-permute-start | bytes 368648 | tf_op jit(solution)/shard_map/ppermute | solution.py:53
  69.3 6.7 %collective-permute-start.16 = (bf16[128,1152]{1,0:T(8,128)(2,1)S(1)}, bf16[128,1152]{1,0:T(8,128)(2,1)S(1)}, u32[]{:S(2)}, u32[]{:S(2)}) collective-permute-start(bf16[128,1152]{1,0:T(8,128)(2,1)S(1)} %get-tuple-element.26), channel_id=1, source_target_pairs={{0,16},{16,0},{1,17},{17,1},{2,18},{18,2},{3,19},{19,3},{4,20},{20... | collective-permute-start | bytes 884744 | tf_op jit(solution)/shard_map/ppermute | solution.py:48
  100.7 4.1 %collective-permute-start.17 = (bf16[8,16,1024]{2,1,0:T(8,128)(2,1)S(1)}, bf16[8,16,1024]{2,1,0:T(8,128)(2,1)S(1)}, u32[]{:S(2)}, u32[]{:S(2)}) collective-permute-start(bf16[8,16,1024]{2,1,0:T(8,128)(2,1)S(1)} %slice_bitcast_fusion), channel_id=1, source_target_pairs={{0,16},{16,0},{1,17},{17,1},{2,18},{18,2},{3,19},{19,3},{4,20},{20... | collective-permute-start | bytes 786440 | tf_op jit(solution)/shard_map/ppermute | solution.py:48
  105.6 8.0 %collective-permute-start.20 = (bf16[32,896]{1,0:T(8,128)(2,1)S(1)}, bf16[32,896]{1,0:T(8,128)(2,1)S(1)}, u32[]{:S(2)}, u32[]{:S(2)}) collective-permute-start(bf16[32,896]{1,0:T(8,128)(2,1)S(1)} %get-tuple-element.31), channel_id=1, source_target_pairs={{0,1},{1,2},{2,3},{3,4},{4,5},{5,6},{6,7},{7,0},{8,9},{9,10},{10,1... | collective-permute-start | bytes 172040 | tf_op jit(solution)/shard_map/ppermute | solution.py:53
  106.5 7.1 %collective-permute-start.21 = (bf16[32,896]{1,0:T(8,128)(2,1)S(1)}, bf16[32,896]{1,0:T(8,128)(2,1)S(1)}, u32[]{:S(2)}, u32[]{:S(2)}) collective-permute-start(bf16[32,896]{1,0:T(8,128)(2,1)S(1)} %get-tuple-element.32), channel_id=1, source_target_pairs={{0,2},{1,3},{2,4},{3,5},{4,6},{5,7},{6,0},{7,1},{8,10},{9,11},{10,... | collective-permute-start | bytes 172040 | tf_op jit(solution)/shard_map/ppermute | solution.py:53
  109.2 4.4 %collective-permute-start.23 = (bf16[32,896]{1,0:T(8,128)(2,1)S(1)}, bf16[32,896]{1,0:T(8,128)(2,1)S(1)}, u32[]{:S(2)}, u32[]{:S(2)}) collective-permute-start(bf16[32,896]{1,0:T(8,128)(2,1)S(1)} %get-tuple-element.34), channel_id=1, source_target_pairs={{0,7},{1,0},{2,1},{3,2},{4,3},{5,4},{6,5},{7,6},{8,15},{9,8},{10,9... | collective-permute-start | bytes 172040 | tf_op jit(solution)/shard_map/ppermute | solution.py:53
  110.8 6.7 %collective-permute-start.18 = (bf16[32,896]{1,0:T(8,128)(2,1)S(1)}, bf16[32,896]{1,0:T(8,128)(2,1)S(1)}, u32[]{:S(2)}, u32[]{:S(2)}) collective-permute-start(bf16[32,896]{1,0:T(8,128)(2,1)S(1)} %get-tuple-element.28), channel_id=1, source_target_pairs={{0,1},{1,2},{2,3},{3,4},{4,5},{5,6},{6,7},{7,0},{8,9},{9,10},{10,1... | collective-permute-start | bytes 172040 | tf_op jit(solution)/shard_map/ppermute | solution.py:53
  110.9 6.7 %collective-permute-start.19 = (bf16[32,896]{1,0:T(8,128)(2,1)S(1)}, bf16[32,896]{1,0:T(8,128)(2,1)S(1)}, u32[]{:S(2)}, u32[]{:S(2)}) collective-permute-start(bf16[32,896]{1,0:T(8,128)(2,1)S(1)} %get-tuple-element.29), channel_id=1, source_target_pairs={{0,7},{1,0},{2,1},{3,2},{4,3},{5,4},{6,5},{7,6},{8,15},{9,8},{10,9... | collective-permute-start | bytes 172040 | tf_op jit(solution)/shard_map/ppermute | solution.py:53
  113.6 5.2 %collective-permute-start.22 = (bf16[32,896]{1,0:T(8,128)(2,1)S(1)}, bf16[32,896]{1,0:T(8,128)(2,1)S(1)}, u32[]{:S(2)}, u32[]{:S(2)}) collective-permute-start(bf16[32,896]{1,0:T(8,128)(2,1)S(1)} %shard_map.99), channel_id=1, source_target_pairs={{0,2},{1,3},{2,4},{3,5},{4,6},{5,7},{6,0},{7,1},{8,10},{9,11},{10,... | collective-permute-start | bytes 172040 | tf_op jit(solution)/shard_map/ppermute | solution.py:53
  113.7 5.6 %collective-permute-start.24 = (bf16[32,896]{1,0:T(8,128)(2,1)S(1)}, bf16[32,896]{1,0:T(8,128)(2,1)S(1)}, u32[]{:S(2)}, u32[]{:S(2)}) collective-permute-start(bf16[32,896]{1,0:T(8,128)(2,1)S(1)} %shard_map.100), channel_id=1, source_target_pairs={{0,6},{1,7},{2,0},{3,1},{4,2},{5,3},{6,4},{7,5},{8,14},{9,15},{10,... | collective-permute-start | bytes 172040 | tf_op jit(solution)/shard_map/ppermute | solution.py:53
  119.3 6.9 %collective-permute-start.29 = (bf16[32,896]{1,0:T(8,128)(2,1)S(1)}, bf16[32,896]{1,0:T(8,128)(2,1)S(1)}, u32[]{:S(2)}, u32[]{:S(2)}) collective-permute-start(bf16[32,896]{1,0:T(8,128)(2,1)S(1)} %shard_map.101.refs_0_), channel_id=1, source_target_pairs={{0,2},{1,3},{2,4},{3,5},{4,6},{5,7},{6,0},{7,1},{8,10},{9,11},{10,... | collective-permute-start | bytes 172040 | tf_op jit(solution)/shard_map/ppermute | solution.py:53
  122.2 4.0 %collective-permute-start.26 = (bf16[32,896]{1,0:T(8,128)(2,1)S(1)}, bf16[32,896]{1,0:T(8,128)(2,1)S(1)}, u32[]{:S(2)}, u32[]{:S(2)}) collective-permute-start(bf16[32,896]{1,0:T(8,128)(2,1)S(1)} %shard_map.101.refs_0_), channel_id=1, source_target_pairs={{0,6},{1,7},{2,0},{3,1},{4,2},{5,3},{6,4},{7,5},{8,14},{9,15},{10,... | collective-permute-start | bytes 172040 | tf_op jit(solution)/shard_map/ppermute | solution.py:53
  123.5 5.4 %collective-permute-start.31 = (bf16[32,896]{1,0:T(8,128)(2,1)S(1)}, bf16[32,896]{1,0:T(8,128)(2,1)S(1)}, u32[]{:S(2)}, u32[]{:S(2)}) collective-permute-start(bf16[32,896]{1,0:T(8,128)(2,1)S(1)} %shard_map.101.refs_0_), channel_id=1, source_target_pairs={{0,1},{1,2},{2,3},{3,4},{4,5},{5,6},{6,7},{7,0},{8,9},{9,10},{10,1... | collective-permute-start | bytes 172040 | tf_op jit(solution)/shard_map/ppermute | solution.py:53
  123.5 5.4 %collective-permute-start.25 = (bf16[32,896]{1,0:T(8,128)(2,1)S(1)}, bf16[32,896]{1,0:T(8,128)(2,1)S(1)}, u32[]{:S(2)}, u32[]{:S(2)}) collective-permute-start(bf16[32,896]{1,0:T(8,128)(2,1)S(1)} %shard_map.101.refs_0_), channel_id=1, source_target_pairs={{0,7},{1,0},{2,1},{3,2},{4,3},{5,4},{6,5},{7,6},{8,15},{9,8},{10,9... | collective-permute-start | bytes 172040 | tf_op jit(solution)/shard_map/ppermute | solution.py:53
  126.2 4.4 %collective-permute-start.30 = (bf16[32,896]{1,0:T(8,128)(2,1)S(1)}, bf16[32,896]{1,0:T(8,128)(2,1)S(1)}, u32[]{:S(2)}, u32[]{:S(2)}) collective-permute-start(bf16[32,896]{1,0:T(8,128)(2,1)S(1)} %collective-permute-done.29.refs_6_), channel_id=1, source_target_pairs={{0,1},{1,2},{2,3},{3,4},{4,5},{5,6},{6,7},{7,0},{8,9},{9,10},{10,1... | collective-permute-start | bytes 172040 | tf_op jit(solution)/shard_map/ppermute | solution.py:53
  126.2 5.8 %collective-permute-start.28 = (bf16[32,896]{1,0:T(8,128)(2,1)S(1)}, bf16[32,896]{1,0:T(8,128)(2,1)S(1)}, u32[]{:S(2)}, u32[]{:S(2)}) collective-permute-start(bf16[32,896]{1,0:T(8,128)(2,1)S(1)} %collective-permute-done.26.refs_2_), channel_id=1, source_target_pairs={{0,6},{1,7},{2,0},{3,1},{4,2},{5,3},{6,4},{7,5},{8,14},{9,15},{10,... | collective-permute-start | bytes 172040 | tf_op jit(solution)/shard_map/ppermute | solution.py:53
  128.8 4.7 %collective-permute-start.27 = (bf16[32,896]{1,0:T(8,128)(2,1)S(1)}, bf16[32,896]{1,0:T(8,128)(2,1)S(1)}, u32[]{:S(2)}, u32[]{:S(2)}) collective-permute-start(bf16[32,896]{1,0:T(8,128)(2,1)S(1)} %collective-permute-done.26.refs_2_), channel_id=1, source_target_pairs={{0,7},{1,0},{2,1},{3,2},{4,3},{5,4},{6,5},{7,6},{8,15},{9,8},{10,9... | collective-permute-start | bytes 172040 | tf_op jit(solution)/shard_map/ppermute | solution.py:53
  135.7 6.3 %collective-permute-start.32 = (bf16[128,1152]{1,0:T(8,128)(2,1)S(1)}, bf16[128,1152]{1,0:T(8,128)(2,1)S(1)}, u32[]{:S(2)}, u32[]{:S(2)}) collective-permute-start(bf16[128,1152]{1,0:T(8,128)(2,1)S(1)} %get-tuple-element.39), channel_id=1, source_target_pairs={{0,16},{16,0},{1,17},{17,1},{2,18},{18,2},{3,19},{19,3},{4,20},{20... | collective-permute-start | bytes 884744 | tf_op jit(solution)/shard_map/ppermute | solution.py:48
  154.5 2.2 %collective-permute-start.33 = (bf16[128,128]{1,0:T(8,128)(2,1)S(1)}, bf16[128,128]{1,0:T(8,128)(2,1)S(1)}, u32[]{:S(2)}, u32[]{:S(2)}) collective-permute-start(bf16[128,128]{1,0:T(8,128)(2,1)S(1)} %get-tuple-element.41.back), channel_id=1, source_target_pairs={{0,16},{16,0},{1,17},{17,1},{2,18},{18,2},{3,19},{19,3},{4,20},{20... | collective-permute-start | bytes 98312 | tf_op jit(solution)/shard_map/ppermute | solution.py:48

commit v6 on v5

--- a/solution.py
+++ b/solution.py
@@ -181,29 +181,29 @@
     input_partials(act, weight, first, second, mine, other)
 
 
-def spread_kernel(acts, grads, out):
-    feat = acts.shape[1]
+def spread_kernel(rows, out):
     for chip in range(out.shape[0]):
-        out[chip, :, :feat] = acts[...]
-        out[chip, :, feat:] = grads[...]
+        out[chip] = rows[...]
 
 
 def add_cores_kernel(mine, other, out):
     out[...] = (mine[...] + other[...].astype(F32)).astype(BF16).reshape(out.shape)
 
 
-def hand_kernel(got, out):
+def hand_kernel(got, back, out):
     total = jnp.sum(got[...].astype(F32), axis=0).astype(BF16)
+    feat = out.shape[3]
+    back[...] = total[:, feat:]
     for section in range(out.shape[0]):
         for chip in range(out.shape[1]):
-            out[section, chip] = total
+            out[section, chip] = total[:, :feat]
 
 
 def hidden_kernel(mine, other, down, *outs):
     *blocks, held = outs
     chips, own, feat = other.shape
     n, rows, _ = held.shape
-    g = jnp.concatenate([mine[1, :, :, :feat], other[...]], axis=0).reshape(2 * chips * own, feat)
+    g = jnp.concatenate([mine[1], other[...]], axis=0).reshape(2 * chips * own, feat)
     held[...] = dot_nt(g, down[...]).astype(BF16).reshape(held.shape)
     for distance in range(n):
         blocks[distance][...] = held[lax.rem(lax.axis_index("z") + distance, n)]
@@ -217,26 +217,31 @@
     out[...] = total.astype(BF16)
 
 
-def last_message_kernel(mine, other, out):
+def last_message_kernel(mine, other, back_one, out):
     total = (mine[...] + other[...].astype(F32)).astype(BF16)
     chips, rows, _ = out.shape
-    wide = total.shape[1] - (out.shape[2] - total.shape[1]) // (chips - 1)
-    rank = total.shape[1] - wide
+    rank = back_one.shape[1]
+    wide = total.shape[1] - rank
     out[:, :, :wide] = total[:, :wide].reshape(chips, rows, wide)
     for chip in range(chips):
         block = total[chip * rows:(chip + 1) * rows, wide:]
         for target in range(chips):
             out[target, :, wide + chip * rank:wide + (chip + 1) * rank] = block
 
+    @pl.when(lax.axis_index("pipe") == 1)
+    def _():
+        for target in range(chips):
+            out[target, :, :rank] = back_one[...]
+
 
 def last_sum_kernel(got, handed, grad, back):
     chips, rows, _ = got.shape
     feat, rank = grad.shape[1], back.shape[1]
     total = jnp.sum(got[...].astype(F32), axis=0).astype(BF16)
     upper = lax.axis_index("pipe") == 1
-    grad[...] = jnp.where(upper, handed[1, lax.axis_index(CHIPS), :, :feat], total[:, :feat])
+    grad[...] = jnp.where(upper, handed[1, lax.axis_index(CHIPS)], total[:, :feat])
     for chip in range(chips):
-        held = jnp.where(upper, handed[1, chip, :, feat:], total[:, feat + chip * rank:feat + (chip + 1) * rank])
+        held = jnp.where(upper, got[chip, :, :rank], total[:, feat + chip * rank:feat + (chip + 1) * rank])
         back[chip * rows:(chip + 1) * rows, :] = held
 
 
@@ -289,11 +294,8 @@
             far = [ring(ahead_two, -2)]
         return [piece, ahead, ahead_two, ahead_three] + far + [behind_three, behind_two, behind]
 
-    message = call(
-        spread_kernel, kept((chips, own, 2 * feat)),
-        acts[0].reshape(own, feat), output_gradient.reshape(own, feat),
-        pin=False,
-    )
+    message = jnp.concatenate([acts[0].reshape(own, feat), output_gradient.reshape(own, feat)], axis=1)
+    message = call(spread_kernel, kept((chips, own, 2 * feat)), message)
     mine = lax.all_to_all(message, CHIPS, 0, 0).reshape(half, 2 * feat)
     other = core_swap(mine)
 
@@ -320,15 +322,17 @@
         *gather_z(sent, False), weight, first, second,
         flops=2 * tokens * feat * width,
     )
-    shape = (chips, own, feat + 2 * rank)
-    message = call(add_cores_kernel, kept(shape), half_mine, core_swap(half_other))
-    message = call(hand_kernel, kept((2,) + shape), lax.all_to_all(message, CHIPS, 0, 0))
+    shape = (chips, own, feat)
+    message = call(add_cores_kernel, kept((chips, own, feat + 2 * rank)), half_mine, core_swap(half_other))
+    back_one, message = call(
+        hand_kernel, (kept((own, 2 * rank)), kept((2,) + shape)), lax.all_to_all(message, CHIPS, 0, 0)
+    )
 
     handed = lax.all_to_all(message.reshape((2 * chips,) + shape[1:]), ("pipe",) + CHIPS, 0, 0)
     handed = handed.reshape((2,) + shape)
     zero, one, two, three, far, minus_three, minus_two, minus_one = call(
         hidden_kernel, (kept((block, hidden)),) * n,
-        handed, core_swap(handed[1, :, :, :feat]), down_weight,
+        handed, core_swap(handed[1]), down_weight,
         scratch=[pltpu.VMEM((n, block, hidden), BF16)],
         flops=2 * tokens * feat * hidden,
     )
@@ -351,7 +355,8 @@
     )
     half_mine, grad_up = lax.optimization_barrier((half_mine, grad_up))
     message = call(
-        last_message_kernel, kept((chips, own, feat + chips * 2 * rank)), half_mine, core_swap(half_other)
+        last_message_kernel, kept((chips, own, feat + chips * 2 * rank)), half_mine, core_swap(half_other),
+        back_one,
     )
     got = lax.all_to_all(message, CHIPS, 0, 0)
     grad_inputs, back_mine = call(

time: 158 us -> 157 us (level)
    unnamed x11 -> x7, local copies, waits for them, and re-layouts: 4.37 us -> 2.86 us
  transfers between devices with their start and end apart: 34 -> 34, of which waited for: 17 -> 17; matrix products, arithmetic and copies ran while one was open for 2% -> 2% of each run, Pallas kernels for 2% -> 3%
where the time goes in v6:
time: 157 us; the launch traced here: 156 us
  starting transfers between devices  63.7 us (41%)
  blocking collectives  49.9 us (32%)
  waiting for transfers between devices  26.1 us (17%)
  Pallas kernels  12.1 us (8%)
  local copies, waits for them, and re-layouts  2.88 us (2%)
    ppermute x29, starting transfers between devices, ring(): return lax.ppermute(block, 'z', [(i, (i + step) % n) for i in range(n)])  46.8 us
    ppermute x29, waiting for transfers between devices, ring(): return lax.ppermute(block, 'z', [(i, (i + step) % n) for i in range(n)])  23 us
    ppermute x5, starting transfers between devices, core_swap(): return lax.ppermute(block, 'core', [(0, 1), (1, 0)])  16.9 us
    all_to_all x1, blocking collectives, local(): mine = lax.all_to_all(message, CHIPS, 0, 0).reshape(half, 2 * feat)  14.3 us
    all_to_all x1, blocking collectives, local(): lax.all_to_all(message.reshape((2 * chips,) + shape[1:]), ('pipe',) + CHI...  14.2 us
    pallas_call x23, Pallas kernels, call(): pl.pallas_call(kernel, out_shape=outs, in_specs=[pl.BlockSpec(memory_spac...  12.1 us
    all_to_all x1, blocking collectives, local(): got = lax.all_to_all(message, CHIPS, 0, 0)  11.8 us
    all_to_all x1, blocking collectives, local(): lax.all_to_all(message, CHIPS, 0, 0)  9.69 us
  transfers between devices with their start and end apart: 34, of which 17 were waited for; matrix products, arithmetic and copies ran while one was open for 2% of the time, Pallas kernels for 3%

profile of v6, /device:TPU:1, one launch (start us, length us, event | category | flops | bytes accessed | tf_op | source)
XLA Modules:
  0.0 156.3 jit_solution(2356445906129510116)
XLA Ops:
  0.6 0.8 pad_maximum_fusion.rows
  1.5 14.3 %all_to_all.20 = bf16[8,16,2048]{2,1,0:T(8,128)(2,1)S(1)} all-to-all(bf16[8,16,2048]{2,1,0:T(8,128)(2,1)S(1)} %shard_map.85), channel_id=1, replica_groups=mesh['x'=4,'yl'=2,'core'=2,'pipe'=2,'z'=8] {'x','yl'}, dimensions={0} | all-to-all | bytes 1048576 | tf_op jit(solution)/shard_map/all_to_all | solution.py:299
  15.7 2.1 %collective-permute-start = (bf16[128,2048]{1,0:T(8,128)(2,1)S(1)}, bf16[128,2048]{1,0:T(8,128)(2,1)S(1)}, u32[]{:S(2)}, u32[]{:S(2)}) collective-permute-start(bf16[128,2048]{1,0:T(8,128)(2,1)S(1)} %bitcast.21), channel_id=1, source_target_pairs={{0,16},{16,0},{1,17},{17,1},{2,18},{18,2},{3,19},{19,3},{4,20},{20... | collective-permute-start | bytes 1572872 | tf_op jit(solution)/shard_map/ppermute | solution.py:48
  17.8 2.9 %copy.9 = bf16[128,8,2,896]{3,1,2,0:T(8,128)(2,1)S(1)} copy(bf16[128,8,2,896]{3,2,1,0:T(2,128)(2,1)} %bitcast.36) | data formatting | bytes 7340032
  20.7 1.4 shard_map.86
  22.1 1.7 %collective-permute-start.1 = (bf16[32,1408]{1,0:T(8,128)(2,1)S(1)}, bf16[32,1408]{1,0:T(8,128)(2,1)S(1)}, u32[]{:S(2)}, u32[]{:S(2)}) collective-permute-start(bf16[32,1408]{1,0:T(8,128)(2,1)S(1)} %get-tuple-element.25), channel_id=1, source_target_pairs={{0,1},{1,2},{2,3},{3,4},{4,5},{5,6},{6,7},{7,0},{8,9},{9,10},{10,1... | collective-permute-start | bytes 270344 | tf_op jit(solution)/shard_map/ppermute | solution.py:53
  23.8 4.0 %collective-permute-start.5 = (bf16[32,1408]{1,0:T(8,128)(2,1)S(1)}, bf16[32,1408]{1,0:T(8,128)(2,1)S(1)}, u32[]{:S(2)}, u32[]{:S(2)}) collective-permute-start(bf16[32,1408]{1,0:T(8,128)(2,1)S(1)} %get-tuple-element.26), channel_id=1, source_target_pairs={{0,7},{1,0},{2,1},{3,2},{4,3},{5,4},{6,5},{7,6},{8,15},{9,8},{10,9... | collective-permute-start | bytes 270344 | tf_op jit(solution)/shard_map/ppermute | solution.py:53
  27.8 2.3 %shard_map.87.parts = bf16[8,32,2816]{2,1,0:T(8,128)(2,1)S(1)} custom-call(bf16[128,2048]{1,0:T(8,128)(2,1)S(1)} %bitcast.23, bf16[128,2048]{1,0:T(8,128)(2,1)S(1)} %collective-permute-done.other.inputs, bf16[1024,1792]{1,0:T(8,128)(2,1)S(1)} %bitcast.15, bf16[896,1024]{1,0:T(8,128)(2,1)S(1)} %bitcast.19, bf16[1024,128]{1,0:T(8,128)(2,1)S(1)} %bitcast.28, ...), custom_call_target="tpu_custom_call" | custom-call | flops 1476395008 | bytes 7045120 | tf_op jit(solution)/shard_map/pallas_call | solution.py:36
  30.1 0.6 collective-permute-done.1.moving
  30.7 0.1 collective-permute-start.2
  30.9 2.7 %collective-permute-start.6 = (bf16[32,2816]{1,0:T(8,128)(2,1)S(1)}, bf16[32,2816]{1,0:T(8,128)(2,1)S(1)}, u32[]{:S(2)}, u32[]{:S(2)}) collective-permute-start(bf16[32,2816]{1,0:T(8,128)(2,1)S(1)} %shard_map.91), channel_id=1, source_target_pairs={{0,7},{1,0},{2,1},{3,2},{4,3},{5,4},{6,5},{7,6},{8,15},{9,8},{10,9... | collective-permute-start | bytes 540680 | tf_op jit(solution)/shard_map/ppermute | solution.py:53
  33.6 3.9 %collective-permute-done.2.moving = bf16[32,2816]{1,0:T(8,128)(2,1)S(1)} collective-permute-done((bf16[32,2816]{1,0:T(8,128)(2,1)S(1)}, bf16[32,2816]{1,0:T(8,128)(2,1)S(1)}, u32[]{:S(2)}, u32[]{:S(2)}) %collective-permute-start.2) | collective-permute-done | bytes 180256 | tf_op jit(solution)/shard_map/ppermute | solution.py:53
  37.6 0.1 collective-permute-start.3
  37.8 2.7 %collective-permute-start.7 = (bf16[32,2816]{1,0:T(8,128)(2,1)S(1)}, bf16[32,2816]{1,0:T(8,128)(2,1)S(1)}, u32[]{:S(2)}, u32[]{:S(2)}) collective-permute-start(bf16[32,2816]{1,0:T(8,128)(2,1)S(1)} %shard_map.92), channel_id=1, source_target_pairs={{0,7},{1,0},{2,1},{3,2},{4,3},{5,4},{6,5},{7,6},{8,15},{9,8},{10,9... | collective-permute-start | bytes 540680 | tf_op jit(solution)/shard_map/ppermute | solution.py:53
  40.5 2.7 %collective-permute-done.3.moving = bf16[32,2816]{1,0:T(8,128)(2,1)S(1)} collective-permute-done((bf16[32,2816]{1,0:T(8,128)(2,1)S(1)}, bf16[32,2816]{1,0:T(8,128)(2,1)S(1)}, u32[]{:S(2)}, u32[]{:S(2)}) %collective-permute-start.3) | collective-permute-done | bytes 180256 | tf_op jit(solution)/shard_map/ppermute | solution.py:53
  43.3 0.1 collective-permute-start.4
  43.5 2.7 %collective-permute-start.8 = (bf16[32,2816]{1,0:T(8,128)(2,1)S(1)}, bf16[32,2816]{1,0:T(8,128)(2,1)S(1)}, u32[]{:S(2)}, u32[]{:S(2)}) collective-permute-start(bf16[32,2816]{1,0:T(8,128)(2,1)S(1)} %shard_map.93), channel_id=1, source_target_pairs={{0,7},{1,0},{2,1},{3,2},{4,3},{5,4},{6,5},{7,6},{8,15},{9,8},{10,9... | collective-permute-start | bytes 540680 | tf_op jit(solution)/shard_map/ppermute | solution.py:53
  46.2 2.7 %collective-permute-done.4.up_in = bf16[32,2816]{1,0:T(8,128)(2,1)S(1)} collective-permute-done((bf16[32,2816]{1,0:T(8,128)(2,1)S(1)}, bf16[32,2816]{1,0:T(8,128)(2,1)S(1)}, u32[]{:S(2)}, u32[]{:S(2)}) %collective-permute-start.4) | collective-permute-done | bytes 180256 | tf_op jit(solution)/shard_map/ppermute | solution.py:53
  48.9 0.1 shard_map.94.refs_0_
  49.1 1.7 %collective-permute-start.13 = (bf16[32,1920]{1,0:T(8,128)(2,1)S(1)}, bf16[32,1920]{1,0:T(8,128)(2,1)S(1)}, u32[]{:S(2)}, u32[]{:S(2)}) collective-permute-start(bf16[32,1920]{1,0:T(8,128)(2,1)S(1)} %shard_map.94.refs_0_), channel_id=1, source_target_pairs={{0,2},{1,3},{2,4},{3,5},{4,6},{5,7},{6,0},{7,1},{8,10},{9,11},{10,... | collective-permute-start | bytes 368648 | tf_op jit(solution)/shard_map/ppermute | solution.py:53
  50.7 2.0 %collective-permute-start.10 = (bf16[32,1920]{1,0:T(8,128)(2,1)S(1)}, bf16[32,1920]{1,0:T(8,128)(2,1)S(1)}, u32[]{:S(2)}, u32[]{:S(2)}) collective-permute-start(bf16[32,1920]{1,0:T(8,128)(2,1)S(1)} %shard_map.94.refs_0_), channel_id=1, source_target_pairs={{0,6},{1,7},{2,0},{3,1},{4,2},{5,3},{6,4},{7,5},{8,14},{9,15},{10,... | collective-permute-start | bytes 368648 | tf_op jit(solution)/shard_map/ppermute | solution.py:53
  52.7 0.7 collective-permute-start.15
  53.4 2.0 %collective-permute-start.9 = (bf16[32,1920]{1,0:T(8,128)(2,1)S(1)}, bf16[32,1920]{1,0:T(8,128)(2,1)S(1)}, u32[]{:S(2)}, u32[]{:S(2)}) collective-permute-start(bf16[32,1920]{1,0:T(8,128)(2,1)S(1)} %shard_map.94.refs_0_), channel_id=1, source_target_pairs={{0,7},{1,0},{2,1},{3,2},{4,3},{5,4},{6,5},{7,6},{8,15},{9,8},{10,9... | collective-permute-start | bytes 368648 | tf_op jit(solution)/shard_map/ppermute | solution.py:53
  55.4 1.4 collective-permute-start.14
  56.8 1.8 %collective-permute-start.12 = (bf16[32,1920]{1,0:T(8,128)(2,1)S(1)}, bf16[32,1920]{1,0:T(8,128)(2,1)S(1)}, u32[]{:S(2)}, u32[]{:S(2)}) collective-permute-start(bf16[32,1920]{1,0:T(8,128)(2,1)S(1)} %collective-permute-done.10.refs_2_), channel_id=1, source_target_pairs={{0,6},{1,7},{2,0},{3,1},{4,2},{5,3},{6,4},{7,5},{8,14},{9,15},{10,... | collective-permute-start | bytes 368648 | tf_op jit(solution)/shard_map/ppermute | solution.py:53
  58.6 1.6 %collective-permute-start.11 = (bf16[32,1920]{1,0:T(8,128)(2,1)S(1)}, bf16[32,1920]{1,0:T(8,128)(2,1)S(1)}, u32[]{:S(2)}, u32[]{:S(2)}) collective-permute-start(bf16[32,1920]{1,0:T(8,128)(2,1)S(1)} %collective-permute-done.10.refs_2_), channel_id=1, source_target_pairs={{0,7},{1,0},{2,1},{3,2},{4,3},{5,4},{6,5},{7,6},{8,15},{9,8},{10,9... | collective-permute-start | bytes 368648 | tf_op jit(solution)/shard_map/ppermute | solution.py:53
  60.3 2.0 %collective-permute-done.14.refs_5_ = bf16[32,1920]{1,0:T(8,128)(2,1)S(1)} collective-permute-done((bf16[32,1920]{1,0:T(8,128)(2,1)S(1)}, bf16[32,1920]{1,0:T(8,128)(2,1)S(1)}, u32[]{:S(2)}, u32[]{:S(2)}) %collective-permute-start.14) | collective-permute-done | bytes 122912 | tf_op jit(solution)/shard_map/ppermute | solution.py:53
  62.3 3.8 %collective-permute-done.12.refs_4_ = bf16[32,1920]{1,0:T(8,128)(2,1)S(1)} collective-permute-done((bf16[32,1920]{1,0:T(8,128)(2,1)S(1)}, bf16[32,1920]{1,0:T(8,128)(2,1)S(1)}, u32[]{:S(2)}, u32[]{:S(2)}) %collective-permute-start.12) | collective-permute-done | bytes 122912 | tf_op jit(solution)/shard_map/ppermute | solution.py:53
  66.2 0.7 collective-permute-done.11.refs_3_
  66.9 1.7 %shard_map.95 = (bf16[256,1920]{1,0:T(8,128)(2,1)S(1)}, f32[128,1152]{1,0:T(8,128)S(1)}, bf16[128,1152]{1,0:T(8,128)(2,1)S(1)}) custom-call(bf16[32,1920]{1,0:T(8,128)(2,1)S(1)} %shard_map.94.refs_0_, bf16[32,1920]{1,0:T(8,128)(2,1)S(1)} %collective-permute-done.9.refs_1_, bf16[32,1920]{1,0:T(8,128)(2,1)S(1)} %collective-permute-done.10.refs_2_, ...), custom_call_target="tpu_custom_call" | custom-call | flops 1006632960 | bytes 5144576 | tf_op jit(solution)/shard_map/pallas_call | solution.py:36
  68.6 5.5 %collective-permute-start.16 = (bf16[128,1152]{1,0:T(8,128)(2,1)S(1)}, bf16[128,1152]{1,0:T(8,128)(2,1)S(1)}, u32[]{:S(2)}, u32[]{:S(2)}) collective-permute-start(bf16[128,1152]{1,0:T(8,128)(2,1)S(1)} %get-tuple-element.28), channel_id=1, source_target_pairs={{0,16},{16,0},{1,17},{17,1},{2,18},{18,2},{3,19},{19,3},{4,20},{20... | collective-permute-start | bytes 884744 | tf_op jit(solution)/shard_map/ppermute | solution.py:48
  74.0 1.2 collective-permute-done.16.other
  75.3 9.7 %all_to_all.21.got = bf16[8,16,1152]{2,1,0:T(8,128)(2,1)S(1)} all-to-all(bf16[8,16,1152]{2,1,0:T(8,128)(2,1)S(1)} %shard_map.96), channel_id=1, replica_groups=mesh['x'=4,'yl'=2,'core'=2,'pipe'=2,'z'=8] {'x','yl'}, dimensions={0} | all-to-all | bytes 589824 | tf_op jit(solution)/shard_map/all_to_all | solution.py:328
  85.1 14.2 %all_to_all.22 = bf16[16,16,1024]{2,1,0:T(8,128)(2,1)S(1)} all-to-all(bf16[16,16,1024]{2,1,0:T(8,128)(2,1)S(1)} %bitcast.35), channel_id=1, replica_groups=mesh['x'=4,'yl'=2,'core'=2,'pipe'=2,'z'=8] {'pipe','x','yl'}, dimensions={0} | all-to-all | bytes 1048576 | tf_op jit(solution)/shard_map/all_to_all | solution.py:331
  99.3 2.9 %collective-permute-start.17 = (bf16[8,16,1024]{2,1,0:T(8,128)(2,1)S(1)}, bf16[8,16,1024]{2,1,0:T(8,128)(2,1)S(1)}, u32[]{:S(2)}, u32[]{:S(2)}) collective-permute-start(bf16[8,16,1024]{2,1,0:T(8,128)(2,1)S(1)} %slice.5), channel_id=1, source_target_pairs={{0,16},{16,0},{1,17},{17,1},{2,18},{18,2},{3,19},{19,3},{4,20},{20... | collective-permute-start | bytes 786440 | tf_op jit(solution)/shard_map/ppermute | solution.py:48
  102.2 1.2 collective-permute-done.17.other
  103.4 0.8 shard_map.98
  104.2 0.9 collective-permute-start.20
  105.1 2.8 %collective-permute-start.21 = (bf16[32,896]{1,0:T(8,128)(2,1)S(1)}, bf16[32,896]{1,0:T(8,128)(2,1)S(1)}, u32[]{:S(2)}, u32[]{:S(2)}) collective-permute-start(bf16[32,896]{1,0:T(8,128)(2,1)S(1)} %get-tuple-element.35), channel_id=1, source_target_pairs={{0,2},{1,3},{2,4},{3,5},{4,6},{5,7},{6,0},{7,1},{8,10},{9,11},{10,... | collective-permute-start | bytes 172040 | tf_op jit(solution)/shard_map/ppermute | solution.py:53
  107.8 1.6 %collective-permute-start.23 = (bf16[32,896]{1,0:T(8,128)(2,1)S(1)}, bf16[32,896]{1,0:T(8,128)(2,1)S(1)}, u32[]{:S(2)}, u32[]{:S(2)}) collective-permute-start(bf16[32,896]{1,0:T(8,128)(2,1)S(1)} %get-tuple-element.37), channel_id=1, source_target_pairs={{0,7},{1,0},{2,1},{3,2},{4,3},{5,4},{6,5},{7,6},{8,15},{9,8},{10,9... | collective-permute-start | bytes 172040 | tf_op jit(solution)/shard_map/ppermute | solution.py:53
  109.5 2.7 %collective-permute-start.19 = (bf16[32,896]{1,0:T(8,128)(2,1)S(1)}, bf16[32,896]{1,0:T(8,128)(2,1)S(1)}, u32[]{:S(2)}, u32[]{:S(2)}) collective-permute-start(bf16[32,896]{1,0:T(8,128)(2,1)S(1)} %get-tuple-element.32), channel_id=1, source_target_pairs={{0,7},{1,0},{2,1},{3,2},{4,3},{5,4},{6,5},{7,6},{8,15},{9,8},{10,9... | collective-permute-start | bytes 172040 | tf_op jit(solution)/shard_map/ppermute | solution.py:53
  112.2 0.1 collective-permute-start.22
  112.3 3.8 %collective-permute-start.24 = (bf16[32,896]{1,0:T(8,128)(2,1)S(1)}, bf16[32,896]{1,0:T(8,128)(2,1)S(1)}, u32[]{:S(2)}, u32[]{:S(2)}) collective-permute-start(bf16[32,896]{1,0:T(8,128)(2,1)S(1)} %shard_map.100), channel_id=1, source_target_pairs={{0,6},{1,7},{2,0},{3,1},{4,2},{5,3},{6,4},{7,5},{8,14},{9,15},{10,... | collective-permute-start | bytes 172040 | tf_op jit(solution)/shard_map/ppermute | solution.py:53
  116.1 1.2 collective-permute-done.22.refs_3_
  117.4 0.5 collective-permute-done.24.refs_4_
  117.9 2.9 %collective-permute-start.29 = (bf16[32,896]{1,0:T(8,128)(2,1)S(1)}, bf16[32,896]{1,0:T(8,128)(2,1)S(1)}, u32[]{:S(2)}, u32[]{:S(2)}) collective-permute-start(bf16[32,896]{1,0:T(8,128)(2,1)S(1)} %shard_map.101.refs_0_), channel_id=1, source_target_pairs={{0,2},{1,3},{2,4},{3,5},{4,6},{5,7},{6,0},{7,1},{8,10},{9,11},{10,... | collective-permute-start | bytes 172040 | tf_op jit(solution)/shard_map/ppermute | solution.py:53
  120.8 1.3 collective-permute-start.26
  122.1 2.7 %collective-permute-start.25 = (bf16[32,896]{1,0:T(8,128)(2,1)S(1)}, bf16[32,896]{1,0:T(8,128)(2,1)S(1)}, u32[]{:S(2)}, u32[]{:S(2)}) collective-permute-start(bf16[32,896]{1,0:T(8,128)(2,1)S(1)} %shard_map.101.refs_0_), channel_id=1, source_target_pairs={{0,7},{1,0},{2,1},{3,2},{4,3},{5,4},{6,5},{7,6},{8,15},{9,8},{10,9... | collective-permute-start | bytes 172040 | tf_op jit(solution)/shard_map/ppermute | solution.py:53
  124.8 2.6 %collective-permute-start.28 = (bf16[32,896]{1,0:T(8,128)(2,1)S(1)}, bf16[32,896]{1,0:T(8,128)(2,1)S(1)}, u32[]{:S(2)}, u32[]{:S(2)}) collective-permute-start(bf16[32,896]{1,0:T(8,128)(2,1)S(1)} %collective-permute-done.26.refs_2_), channel_id=1, source_target_pairs={{0,6},{1,7},{2,0},{3,1},{4,2},{5,3},{6,4},{7,5},{8,14},{9,15},{10,... | collective-permute-start | bytes 172040 | tf_op jit(solution)/shard_map/ppermute | solution.py:53
  127.5 0.1 collective-permute-done.31.refs_7_
  127.5 1.6 %collective-permute-done.30.refs_5_ = bf16[32,896]{1,0:T(8,128)(2,1)S(1)} collective-permute-done((bf16[32,896]{1,0:T(8,128)(2,1)S(1)}, bf16[32,896]{1,0:T(8,128)(2,1)S(1)}, u32[]{:S(2)}, u32[]{:S(2)}) %collective-permute-start.30) | collective-permute-done | bytes 57376 | tf_op jit(solution)/shard_map/ppermute | solution.py:53
  129.2 1.4 collective-permute-done.28.refs_4_
  130.6 1.6 %collective-permute-done.27.refs_3_ = bf16[32,896]{1,0:T(8,128)(2,1)S(1)} collective-permute-done((bf16[32,896]{1,0:T(8,128)(2,1)S(1)}, bf16[32,896]{1,0:T(8,128)(2,1)S(1)}, u32[]{:S(2)}, u32[]{:S(2)}) %collective-permute-start.27) | collective-permute-done | bytes 57376 | tf_op jit(solution)/shard_map/ppermute | solution.py:53
  132.1 2.2 %shard_map.102 = (bf16[256,1792]{1,0:T(8,128)(2,1)S(1)}, f32[128,1152]{1,0:T(8,128)S(1)}, bf16[128,1152]{1,0:T(8,128)(2,1)S(1)}) custom-call(bf16[32,896]{1,0:T(8,128)(2,1)S(1)} %shard_map.101.refs_0_, bf16[32,896]{1,0:T(8,128)(2,1)S(1)} %collective-permute-done.25.refs_1_, bf16[32,896]{1,0:T(8,128)(2,1)S(1)} %collective-permute-done.26.refs_2_, ...), custom_call_target="tpu_custom_call" | custom-call | flops 1006632960 | bytes 5603328 | tf_op jit(solution)/shard_map/pallas_call | solution.py:36
  134.3 5.0 %collective-permute-start.32 = (bf16[128,1152]{1,0:T(8,128)(2,1)S(1)}, bf16[128,1152]{1,0:T(8,128)(2,1)S(1)}, u32[]{:S(2)}, u32[]{:S(2)}) collective-permute-start(bf16[128,1152]{1,0:T(8,128)(2,1)S(1)} %get-tuple-element.42), channel_id=1, source_target_pairs={{0,16},{16,0},{1,17},{17,1},{2,18},{18,2},{3,19},{19,3},{4,20},{20... | collective-permute-start | bytes 884744 | tf_op jit(solution)/shard_map/ppermute | solution.py:48
  139.3 1.1 shard_map.103
  140.4 0.1 collective-permute-done.32.other
  140.6 0.1 shard_map.104
  140.7 11.8 %all_to_all.23.got = bf16[8,16,2048]{2,1,0:T(8,128)(2,1)S(1)} all-to-all(bf16[8,16,2048]{2,1,0:T(8,128)(2,1)S(1)} %shard_map.104), channel_id=1, replica_groups=mesh['x'=4,'yl'=2,'core'=2,'pipe'=2,'z'=8] {'x','yl'}, dimensions={0} | all-to-all | bytes 1048576 | tf_op jit(solution)/shard_map/all_to_all | solution.py:361
  152.4 0.7 shard_map.105
  153.1 1.3 collective-permute-start.33
  154.4 0.3 shard_map.106.half
  154.7 0.6 collective-permute-done.33.back
  155.3 1.1 shard_map.107
  (40 shorter events, 0.6 us)
Async XLA Ops:
  15.7 4.9 %collective-permute-start = (bf16[128,2048]{1,0:T(8,128)(2,1)S(1)}, bf16[128,2048]{1,0:T(8,128)(2,1)S(1)}, u32[]{:S(2)}, u32[]{:S(2)}) collective-permute-start(bf16[128,2048]{1,0:T(8,128)(2,1)S(1)} %bitcast.21), channel_id=1, source_target_pairs={{0,16},{16,0},{1,17},{17,1},{2,18},{18,2},{3,19},{19,3},{4,20},{20... | collective-permute-start | bytes 1572872 | tf_op jit(solution)/shard_map/ppermute | solution.py:48
  17.8 2.9 %copy-start = (bf16[1,896,1024]{2,1,0:T(8,128)(2,1)S(1)}, bf16[1,896,1024]{2,1,0:T(8,128)(2,1)}, u32[]{:S(2)}) copy-start(bf16[1,896,1024]{2,1,0:T(8,128)(2,1)} %param.9) | copy-start | bytes 5505028
  17.8 2.9 %copy-start.1 = (bf16[1,1024,128]{2,1,0:T(8,128)(2,1)S(1)}, bf16[1,1024,128]{2,1,0:T(8,128)(2,1)}, u32[]{:S(2)}) copy-start(bf16[1,1024,128]{2,1,0:T(8,128)(2,1)} %param.10) | copy-start | bytes 786436
  17.8 2.9 %copy-start.2 = (bf16[1,2,64,896]{3,2,1,0:T(8,128)(2,1)S(1)}, bf16[1,2,64,896]{3,2,1,0:T(8,128)(2,1)}, u32[]{:S(2)}) copy-start(bf16[1,2,64,896]{3,2,1,0:T(8,128)(2,1)} %param.11) | copy-start | bytes 688132
  22.1 8.6 %collective-permute-start.1 = (bf16[32,1408]{1,0:T(8,128)(2,1)S(1)}, bf16[32,1408]{1,0:T(8,128)(2,1)S(1)}, u32[]{:S(2)}, u32[]{:S(2)}) collective-permute-start(bf16[32,1408]{1,0:T(8,128)(2,1)S(1)} %get-tuple-element.25), channel_id=1, source_target_pairs={{0,1},{1,2},{2,3},{3,4},{4,5},{5,6},{6,7},{7,0},{8,9},{9,10},{10,1... | collective-permute-start | bytes 270344 | tf_op jit(solution)/shard_map/ppermute | solution.py:53
  23.8 7.0 %collective-permute-start.5 = (bf16[32,1408]{1,0:T(8,128)(2,1)S(1)}, bf16[32,1408]{1,0:T(8,128)(2,1)S(1)}, u32[]{:S(2)}, u32[]{:S(2)}) collective-permute-start(bf16[32,1408]{1,0:T(8,128)(2,1)S(1)} %get-tuple-element.26), channel_id=1, source_target_pairs={{0,7},{1,0},{2,1},{3,2},{4,3},{5,4},{6,5},{7,6},{8,15},{9,8},{10,9... | collective-permute-start | bytes 270344 | tf_op jit(solution)/shard_map/ppermute | solution.py:53
  30.7 6.8 %collective-permute-start.2 = (bf16[32,2816]{1,0:T(8,128)(2,1)S(1)}, bf16[32,2816]{1,0:T(8,128)(2,1)S(1)}, u32[]{:S(2)}, u32[]{:S(2)}) collective-permute-start(bf16[32,2816]{1,0:T(8,128)(2,1)S(1)} %shard_map.88), channel_id=1, source_target_pairs={{0,1},{1,2},{2,3},{3,4},{4,5},{5,6},{6,7},{7,0},{8,9},{9,10},{10,1... | collective-permute-start | bytes 540680 | tf_op jit(solution)/shard_map/ppermute | solution.py:53
  30.9 6.8 %collective-permute-start.6 = (bf16[32,2816]{1,0:T(8,128)(2,1)S(1)}, bf16[32,2816]{1,0:T(8,128)(2,1)S(1)}, u32[]{:S(2)}, u32[]{:S(2)}) collective-permute-start(bf16[32,2816]{1,0:T(8,128)(2,1)S(1)} %shard_map.91), channel_id=1, source_target_pairs={{0,7},{1,0},{2,1},{3,2},{4,3},{5,4},{6,5},{7,6},{8,15},{9,8},{10,9... | collective-permute-start | bytes 540680 | tf_op jit(solution)/shard_map/ppermute | solution.py:53
  37.6 5.6 %collective-permute-start.3 = (bf16[32,2816]{1,0:T(8,128)(2,1)S(1)}, bf16[32,2816]{1,0:T(8,128)(2,1)S(1)}, u32[]{:S(2)}, u32[]{:S(2)}) collective-permute-start(bf16[32,2816]{1,0:T(8,128)(2,1)S(1)} %shard_map.89), channel_id=1, source_target_pairs={{0,1},{1,2},{2,3},{3,4},{4,5},{5,6},{6,7},{7,0},{8,9},{9,10},{10,1... | collective-permute-start | bytes 540680 | tf_op jit(solution)/shard_map/ppermute | solution.py:53
  37.8 5.6 %collective-permute-start.7 = (bf16[32,2816]{1,0:T(8,128)(2,1)S(1)}, bf16[32,2816]{1,0:T(8,128)(2,1)S(1)}, u32[]{:S(2)}, u32[]{:S(2)}) collective-permute-start(bf16[32,2816]{1,0:T(8,128)(2,1)S(1)} %shard_map.92), channel_id=1, source_target_pairs={{0,7},{1,0},{2,1},{3,2},{4,3},{5,4},{6,5},{7,6},{8,15},{9,8},{10,9... | collective-permute-start | bytes 540680 | tf_op jit(solution)/shard_map/ppermute | solution.py:53
  43.3 5.6 %collective-permute-start.4 = (bf16[32,2816]{1,0:T(8,128)(2,1)S(1)}, bf16[32,2816]{1,0:T(8,128)(2,1)S(1)}, u32[]{:S(2)}, u32[]{:S(2)}) collective-permute-start(bf16[32,2816]{1,0:T(8,128)(2,1)S(1)} %shard_map.90), channel_id=1, source_target_pairs={{0,1},{1,2},{2,3},{3,4},{4,5},{5,6},{6,7},{7,0},{8,9},{9,10},{10,1... | collective-permute-start | bytes 540680 | tf_op jit(solution)/shard_map/ppermute | solution.py:53
  43.5 5.5 %collective-permute-start.8 = (bf16[32,2816]{1,0:T(8,128)(2,1)S(1)}, bf16[32,2816]{1,0:T(8,128)(2,1)S(1)}, u32[]{:S(2)}, u32[]{:S(2)}) collective-permute-start(bf16[32,2816]{1,0:T(8,128)(2,1)S(1)} %shard_map.93), channel_id=1, source_target_pairs={{0,7},{1,0},{2,1},{3,2},{4,3},{5,4},{6,5},{7,6},{8,15},{9,8},{10,9... | collective-permute-start | bytes 540680 | tf_op jit(solution)/shard_map/ppermute | solution.py:53
  49.1 6.3 %collective-permute-start.13 = (bf16[32,1920]{1,0:T(8,128)(2,1)S(1)}, bf16[32,1920]{1,0:T(8,128)(2,1)S(1)}, u32[]{:S(2)}, u32[]{:S(2)}) collective-permute-start(bf16[32,1920]{1,0:T(8,128)(2,1)S(1)} %shard_map.94.refs_0_), channel_id=1, source_target_pairs={{0,2},{1,3},{2,4},{3,5},{4,6},{5,7},{6,0},{7,1},{8,10},{9,11},{10,... | collective-permute-start | bytes 368648 | tf_op jit(solution)/shard_map/ppermute | solution.py:53
  50.7 6.1 %collective-permute-start.10 = (bf16[32,1920]{1,0:T(8,128)(2,1)S(1)}, bf16[32,1920]{1,0:T(8,128)(2,1)S(1)}, u32[]{:S(2)}, u32[]{:S(2)}) collective-permute-start(bf16[32,1920]{1,0:T(8,128)(2,1)S(1)} %shard_map.94.refs_0_), channel_id=1, source_target_pairs={{0,6},{1,7},{2,0},{3,1},{4,2},{5,3},{6,4},{7,5},{8,14},{9,15},{10,... | collective-permute-start | bytes 368648 | tf_op jit(solution)/shard_map/ppermute | solution.py:53
  52.7 7.6 %collective-permute-start.15 = (bf16[32,1920]{1,0:T(8,128)(2,1)S(1)}, bf16[32,1920]{1,0:T(8,128)(2,1)S(1)}, u32[]{:S(2)}, u32[]{:S(2)}) collective-permute-start(bf16[32,1920]{1,0:T(8,128)(2,1)S(1)} %shard_map.94.refs_0_), channel_id=1, source_target_pairs={{0,1},{1,2},{2,3},{3,4},{4,5},{5,6},{6,7},{7,0},{8,9},{9,10},{10,1... | collective-permute-start | bytes 368648 | tf_op jit(solution)/shard_map/ppermute | solution.py:53
  53.4 6.9 %collective-permute-start.9 = (bf16[32,1920]{1,0:T(8,128)(2,1)S(1)}, bf16[32,1920]{1,0:T(8,128)(2,1)S(1)}, u32[]{:S(2)}, u32[]{:S(2)}) collective-permute-start(bf16[32,1920]{1,0:T(8,128)(2,1)S(1)} %shard_map.94.refs_0_), channel_id=1, source_target_pairs={{0,7},{1,0},{2,1},{3,2},{4,3},{5,4},{6,5},{7,6},{8,15},{9,8},{10,9... | collective-permute-start | bytes 368648 | tf_op jit(solution)/shard_map/ppermute | solution.py:53
  55.4 6.9 %collective-permute-start.14 = (bf16[32,1920]{1,0:T(8,128)(2,1)S(1)}, bf16[32,1920]{1,0:T(8,128)(2,1)S(1)}, u32[]{:S(2)}, u32[]{:S(2)}) collective-permute-start(bf16[32,1920]{1,0:T(8,128)(2,1)S(1)} %collective-permute-done.13.refs_6_), channel_id=1, source_target_pairs={{0,1},{1,2},{2,3},{3,4},{4,5},{5,6},{6,7},{7,0},{8,9},{9,10},{10,1... | collective-permute-start | bytes 368648 | tf_op jit(solution)/shard_map/ppermute | solution.py:53
  56.8 9.3 %collective-permute-start.12 = (bf16[32,1920]{1,0:T(8,128)(2,1)S(1)}, bf16[32,1920]{1,0:T(8,128)(2,1)S(1)}, u32[]{:S(2)}, u32[]{:S(2)}) collective-permute-start(bf16[32,1920]{1,0:T(8,128)(2,1)S(1)} %collective-permute-done.10.refs_2_), channel_id=1, source_target_pairs={{0,6},{1,7},{2,0},{3,1},{4,2},{5,3},{6,4},{7,5},{8,14},{9,15},{10,... | collective-permute-start | bytes 368648 | tf_op jit(solution)/shard_map/ppermute | solution.py:53
  58.6 8.2 %collective-permute-start.11 = (bf16[32,1920]{1,0:T(8,128)(2,1)S(1)}, bf16[32,1920]{1,0:T(8,128)(2,1)S(1)}, u32[]{:S(2)}, u32[]{:S(2)}) collective-permute-start(bf16[32,1920]{1,0:T(8,128)(2,1)S(1)} %collective-permute-done.10.refs_2_), channel_id=1, source_target_pairs={{0,7},{1,0},{2,1},{3,2},{4,3},{5,4},{6,5},{7,6},{8,15},{9,8},{10,9... | collective-permute-start | bytes 368648 | tf_op jit(solution)/shard_map/ppermute | solution.py:53
  68.6 6.7 %collective-permute-start.16 = (bf16[128,1152]{1,0:T(8,128)(2,1)S(1)}, bf16[128,1152]{1,0:T(8,128)(2,1)S(1)}, u32[]{:S(2)}, u32[]{:S(2)}) collective-permute-start(bf16[128,1152]{1,0:T(8,128)(2,1)S(1)} %get-tuple-element.28), channel_id=1, source_target_pairs={{0,16},{16,0},{1,17},{17,1},{2,18},{18,2},{3,19},{19,3},{4,20},{20... | collective-permute-start | bytes 884744 | tf_op jit(solution)/shard_map/ppermute | solution.py:48
  99.3 4.1 %collective-permute-start.17 = (bf16[8,16,1024]{2,1,0:T(8,128)(2,1)S(1)}, bf16[8,16,1024]{2,1,0:T(8,128)(2,1)S(1)}, u32[]{:S(2)}, u32[]{:S(2)}) collective-permute-start(bf16[8,16,1024]{2,1,0:T(8,128)(2,1)S(1)} %slice.5), channel_id=1, source_target_pairs={{0,16},{16,0},{1,17},{17,1},{2,18},{18,2},{3,19},{19,3},{4,20},{20... | collective-permute-start | bytes 786440 | tf_op jit(solution)/shard_map/ppermute | solution.py:48
  104.2 8.0 %collective-permute-start.20 = (bf16[32,896]{1,0:T(8,128)(2,1)S(1)}, bf16[32,896]{1,0:T(8,128)(2,1)S(1)}, u32[]{:S(2)}, u32[]{:S(2)}) collective-permute-start(bf16[32,896]{1,0:T(8,128)(2,1)S(1)} %get-tuple-element.34), channel_id=1, source_target_pairs={{0,1},{1,2},{2,3},{3,4},{4,5},{5,6},{6,7},{7,0},{8,9},{9,10},{10,1... | collective-permute-start | bytes 172040 | tf_op jit(solution)/shard_map/ppermute | solution.py:53
  105.1 7.1 %collective-permute-start.21 = (bf16[32,896]{1,0:T(8,128)(2,1)S(1)}, bf16[32,896]{1,0:T(8,128)(2,1)S(1)}, u32[]{:S(2)}, u32[]{:S(2)}) collective-permute-start(bf16[32,896]{1,0:T(8,128)(2,1)S(1)} %get-tuple-element.35), channel_id=1, source_target_pairs={{0,2},{1,3},{2,4},{3,5},{4,6},{5,7},{6,0},{7,1},{8,10},{9,11},{10,... | collective-permute-start | bytes 172040 | tf_op jit(solution)/shard_map/ppermute | solution.py:53
  107.8 4.4 %collective-permute-start.23 = (bf16[32,896]{1,0:T(8,128)(2,1)S(1)}, bf16[32,896]{1,0:T(8,128)(2,1)S(1)}, u32[]{:S(2)}, u32[]{:S(2)}) collective-permute-start(bf16[32,896]{1,0:T(8,128)(2,1)S(1)} %get-tuple-element.37), channel_id=1, source_target_pairs={{0,7},{1,0},{2,1},{3,2},{4,3},{5,4},{6,5},{7,6},{8,15},{9,8},{10,9... | collective-permute-start | bytes 172040 | tf_op jit(solution)/shard_map/ppermute | solution.py:53
  109.4 6.7 %collective-permute-start.18 = (bf16[32,896]{1,0:T(8,128)(2,1)S(1)}, bf16[32,896]{1,0:T(8,128)(2,1)S(1)}, u32[]{:S(2)}, u32[]{:S(2)}) collective-permute-start(bf16[32,896]{1,0:T(8,128)(2,1)S(1)} %get-tuple-element.31), channel_id=1, source_target_pairs={{0,1},{1,2},{2,3},{3,4},{4,5},{5,6},{6,7},{7,0},{8,9},{9,10},{10,1... | collective-permute-start | bytes 172040 | tf_op jit(solution)/shard_map/ppermute | solution.py:53
  109.5 6.7 %collective-permute-start.19 = (bf16[32,896]{1,0:T(8,128)(2,1)S(1)}, bf16[32,896]{1,0:T(8,128)(2,1)S(1)}, u32[]{:S(2)}, u32[]{:S(2)}) collective-permute-start(bf16[32,896]{1,0:T(8,128)(2,1)S(1)} %get-tuple-element.32), channel_id=1, source_target_pairs={{0,7},{1,0},{2,1},{3,2},{4,3},{5,4},{6,5},{7,6},{8,15},{9,8},{10,9... | collective-permute-start | bytes 172040 | tf_op jit(solution)/shard_map/ppermute | solution.py:53
  112.2 5.2 %collective-permute-start.22 = (bf16[32,896]{1,0:T(8,128)(2,1)S(1)}, bf16[32,896]{1,0:T(8,128)(2,1)S(1)}, u32[]{:S(2)}, u32[]{:S(2)}) collective-permute-start(bf16[32,896]{1,0:T(8,128)(2,1)S(1)} %shard_map.99), channel_id=1, source_target_pairs={{0,2},{1,3},{2,4},{3,5},{4,6},{5,7},{6,0},{7,1},{8,10},{9,11},{10,... | collective-permute-start | bytes 172040 | tf_op jit(solution)/shard_map/ppermute | solution.py:53
  112.3 5.6 %collective-permute-start.24 = (bf16[32,896]{1,0:T(8,128)(2,1)S(1)}, bf16[32,896]{1,0:T(8,128)(2,1)S(1)}, u32[]{:S(2)}, u32[]{:S(2)}) collective-permute-start(bf16[32,896]{1,0:T(8,128)(2,1)S(1)} %shard_map.100), channel_id=1, source_target_pairs={{0,6},{1,7},{2,0},{3,1},{4,2},{5,3},{6,4},{7,5},{8,14},{9,15},{10,... | collective-permute-start | bytes 172040 | tf_op jit(solution)/shard_map/ppermute | solution.py:53
  117.9 6.9 %collective-permute-start.29 = (bf16[32,896]{1,0:T(8,128)(2,1)S(1)}, bf16[32,896]{1,0:T(8,128)(2,1)S(1)}, u32[]{:S(2)}, u32[]{:S(2)}) collective-permute-start(bf16[32,896]{1,0:T(8,128)(2,1)S(1)} %shard_map.101.refs_0_), channel_id=1, source_target_pairs={{0,2},{1,3},{2,4},{3,5},{4,6},{5,7},{6,0},{7,1},{8,10},{9,11},{10,... | collective-permute-start | bytes 172040 | tf_op jit(solution)/shard_map/ppermute | solution.py:53
  120.8 4.0 %collective-permute-start.26 = (bf16[32,896]{1,0:T(8,128)(2,1)S(1)}, bf16[32,896]{1,0:T(8,128)(2,1)S(1)}, u32[]{:S(2)}, u32[]{:S(2)}) collective-permute-start(bf16[32,896]{1,0:T(8,128)(2,1)S(1)} %shard_map.101.refs_0_), channel_id=1, source_target_pairs={{0,6},{1,7},{2,0},{3,1},{4,2},{5,3},{6,4},{7,5},{8,14},{9,15},{10,... | collective-permute-start | bytes 172040 | tf_op jit(solution)/shard_map/ppermute | solution.py:53
  122.1 5.4 %collective-permute-start.31 = (bf16[32,896]{1,0:T(8,128)(2,1)S(1)}, bf16[32,896]{1,0:T(8,128)(2,1)S(1)}, u32[]{:S(2)}, u32[]{:S(2)}) collective-permute-start(bf16[32,896]{1,0:T(8,128)(2,1)S(1)} %shard_map.101.refs_0_), channel_id=1, source_target_pairs={{0,1},{1,2},{2,3},{3,4},{4,5},{5,6},{6,7},{7,0},{8,9},{9,10},{10,1... | collective-permute-start | bytes 172040 | tf_op jit(solution)/shard_map/ppermute | solution.py:53
  122.1 5.4 %collective-permute-start.25 = (bf16[32,896]{1,0:T(8,128)(2,1)S(1)}, bf16[32,896]{1,0:T(8,128)(2,1)S(1)}, u32[]{:S(2)}, u32[]{:S(2)}) collective-permute-start(bf16[32,896]{1,0:T(8,128)(2,1)S(1)} %shard_map.101.refs_0_), channel_id=1, source_target_pairs={{0,7},{1,0},{2,1},{3,2},{4,3},{5,4},{6,5},{7,6},{8,15},{9,8},{10,9... | collective-permute-start | bytes 172040 | tf_op jit(solution)/shard_map/ppermute | solution.py:53
  124.8 4.4 %collective-permute-start.30 = (bf16[32,896]{1,0:T(8,128)(2,1)S(1)}, bf16[32,896]{1,0:T(8,128)(2,1)S(1)}, u32[]{:S(2)}, u32[]{:S(2)}) collective-permute-start(bf16[32,896]{1,0:T(8,128)(2,1)S(1)} %collective-permute-done.29.refs_6_), channel_id=1, source_target_pairs={{0,1},{1,2},{2,3},{3,4},{4,5},{5,6},{6,7},{7,0},{8,9},{9,10},{10,1... | collective-permute-start | bytes 172040 | tf_op jit(solution)/shard_map/ppermute | solution.py:53
  124.8 5.8 %collective-permute-start.28 = (bf16[32,896]{1,0:T(8,128)(2,1)S(1)}, bf16[32,896]{1,0:T(8,128)(2,1)S(1)}, u32[]{:S(2)}, u32[]{:S(2)}) collective-permute-start(bf16[32,896]{1,0:T(8,128)(2,1)S(1)} %collective-permute-done.26.refs_2_), channel_id=1, source_target_pairs={{0,6},{1,7},{2,0},{3,1},{4,2},{5,3},{6,4},{7,5},{8,14},{9,15},{10,... | collective-permute-start | bytes 172040 | tf_op jit(solution)/shard_map/ppermute | solution.py:53
  127.4 4.7 %collective-permute-start.27 = (bf16[32,896]{1,0:T(8,128)(2,1)S(1)}, bf16[32,896]{1,0:T(8,128)(2,1)S(1)}, u32[]{:S(2)}, u32[]{:S(2)}) collective-permute-start(bf16[32,896]{1,0:T(8,128)(2,1)S(1)} %collective-permute-done.26.refs_2_), channel_id=1, source_target_pairs={{0,7},{1,0},{2,1},{3,2},{4,3},{5,4},{6,5},{7,6},{8,15},{9,8},{10,9... | collective-permute-start | bytes 172040 | tf_op jit(solution)/shard_map/ppermute | solution.py:53
  134.3 6.3 %collective-permute-start.32 = (bf16[128,1152]{1,0:T(8,128)(2,1)S(1)}, bf16[128,1152]{1,0:T(8,128)(2,1)S(1)}, u32[]{:S(2)}, u32[]{:S(2)}) collective-permute-start(bf16[128,1152]{1,0:T(8,128)(2,1)S(1)} %get-tuple-element.42), channel_id=1, source_target_pairs={{0,16},{16,0},{1,17},{17,1},{2,18},{18,2},{3,19},{19,3},{4,20},{20... | collective-permute-start | bytes 884744 | tf_op jit(solution)/shard_map/ppermute | solution.py:48
  153.1 2.2 %collective-permute-start.33 = (bf16[128,128]{1,0:T(8,128)(2,1)S(1)}, bf16[128,128]{1,0:T(8,128)(2,1)S(1)}, u32[]{:S(2)}, u32[]{:S(2)}) collective-permute-start(bf16[128,128]{1,0:T(8,128)(2,1)S(1)} %get-tuple-element.45.back), channel_id=1, source_target_pairs={{0,16},{16,0},{1,17},{17,1},{2,18},{18,2},{3,19},{19,3},{4,20},{20... | collective-permute-start | bytes 98312 | tf_op jit(solution)/shard_map/ppermute | solution.py:48
